TPU v7x, 32 devices: a whole 2x2x4 slice. The times are simulated.
32 devices in a mesh: region: 4 (over y, x), shard: 8 (over z, core).
Axes of the slice: x: 2, y: 2, z: 4, core: 2. Of those that a mesh axis runs over, the one named last changes fastest.
Arguments:
- tiles: bfloat16 [32768, 512], P(('region', 'shard')), may hold values from -6 to 6
- tile_block: int32 [32768], P(('region', 'shard')), may hold values from 0 to 15
- neighbors: int32 [512, 64], P(('region', 'shard')), may hold values from 0 to 511, as said below
- counts: int32 [512], P(('region', 'shard')), may hold values from 1 to 64, as said below
- flows: int32 [512, 64], P(('region', 'shard')), may hold values from 0 to 22, as said below
- w_anchor: bfloat16 [512, 1024], P('shard'), may hold values from -0.25 to 0.25
- w_dest: bfloat16 [512, 1024], P('shard'), may hold values from -0.25 to 0.25
- w_hidden: bfloat16 [1024, 1024], P('shard'), may hold values from -0.1875 to 0.1875
- w_out: bfloat16 [1024], replicated, may hold values from -0.1875 to 0.1875
Outputs:
- hidden_grad: float32 [1024, 1024], P('shard')
- out_grad: float32 [1024], replicated
- loss: float32 [], replicated
Inputs may be any that keep to these rules, and one draw needn't show every extreme that they name: `neighbors`: every destination lies in the anchor's region, at most 32 blocks from the anchor in the region's order; the first counts slots hold distinct blocks, the others hold the anchor itself. `counts`: some anchor of every region has all 64 slots valid. `flows`: zero in slots at or beyond the anchor's count; the first slot holds at least one trip.
All inputs are finite; a program needn't handle non-finite values.
Results may differ from a plain program's by a relative error of at most 0.017.
Values may be sent and summed in bfloat16 or wider, within the bound.
No kernel may reach another device: no remote copies, remote signals or barrier semaphores. Data moves between devices by JAX's collectives and lax.ppermute only.
A program may use at most 64 MiB of HBM per device.

v0:
```python
import jax
import jax.numpy as jnp
from jax import lax
from jax.sharding import PartitionSpec as P


def shifted(array, axis, by):
    devices = lax.axis_size(axis)
    pairs = [(i, i + by) for i in range(devices) if 0 <= i + by < devices]
    return lax.ppermute(array, axis, pairs)


def shards(tiles, tile_block, neighbors, counts, flows, w_anchor, w_dest, w_hidden, w_out):
    blk = counts.shape[0]
    slots = neighbors.shape[1]
    pairs = blk * slots
    onehot = (tile_block[None, :] == jnp.arange(blk, dtype=jnp.int32)[:, None]).astype(jnp.bfloat16)
    sums = jnp.dot(onehot, tiles, preferred_element_type=jnp.float32)
    scale = lax.rsqrt(jnp.mean(sums * sums, axis=-1, keepdims=True) + 1e-05)
    features = (sums * scale).astype(jnp.bfloat16)
    w_orig_all, w_dest_all, w_hid_all = (
        lax.all_gather(w_anchor, "shard", axis=0, tiled=True),
        lax.all_gather(w_dest, "shard", axis=0, tiled=True),
        lax.all_gather(w_hidden, "shard", axis=0, tiled=True),
    )
    hidden = w_hid_all.shape[1]
    shard_pos = lax.axis_index("shard")
    region_size = blk * lax.axis_size("shard")
    local_ids = neighbors % region_size
    pieces = []
    for step in (2, 1):
        pieces.append(shifted(features, "shard", step))
    pieces.append(features)
    for step in (-1, -2):
        pieces.append(shifted(features, "shard", step))
    window = jnp.concatenate(pieces, axis=0)
    dest_slot = local_ids - (shard_pos - 2) * blk
    anchor_proj = jnp.dot(features, w_orig_all, preferred_element_type=jnp.float32)
    dest_proj = jnp.dot(window, w_dest_all, preferred_element_type=jnp.float32)
    valid = jnp.arange(slots, dtype=jnp.int32)[None, :] < counts[:, None]
    weight_out = w_out.astype(jnp.float32)
    flow_f = flows.astype(jnp.float32)
    total = lax.psum(jnp.sum(flow_f), ("region", "shard"))
    first = jnp.maximum(anchor_proj[:, None, :] + dest_proj[dest_slot], 0.0).astype(jnp.bfloat16)
    first = first.reshape(pairs, hidden)
    active = jnp.maximum(jnp.dot(first, w_hid_all, preferred_element_type=jnp.float32), 0.0)
    scores = jnp.sum(active * weight_out, axis=-1).reshape(blk, slots)
    masked = jnp.where(valid, scores, -jnp.inf)
    top = jnp.max(masked, axis=-1, keepdims=True)
    expo = jnp.where(valid, jnp.exp(scores - top), 0.0)
    mass = jnp.sum(expo, axis=-1, keepdims=True)
    probs = expo / mass
    logp = scores - top - jnp.log(mass)
    anchor_total = jnp.sum(flow_f, axis=-1, keepdims=True)
    sgrad = (jnp.where(valid, probs * anchor_total - flow_f, 0.0) / total).reshape(pairs)
    numer = -jnp.sum(jnp.where(valid, flow_f * logp, 0.0))
    sgrad, numer = (sgrad, numer)
    pre = (sgrad[:, None] * weight_out * (active > 0)).astype(jnp.bfloat16)
    grad = lax.dot_general(first, pre, (((0,), (0,)), ((), ())), preferred_element_type=jnp.float32)
    gout = jnp.sum(sgrad[:, None] * active, axis=0)
    numer_all, out_grad = lax.psum((numer, gout), ("region", "shard"))
    partial_rows = lax.psum_scatter(grad, "shard", scatter_dimension=0, tiled=True)
    hidden_grad = lax.psum(partial_rows, "region")
    return (hidden_grad, out_grad, numer_all / total)


def solution(mesh):
    return jax.shard_map(
        shards,
        mesh=mesh,
        in_specs=(
            P(("region", "shard"), None),
            P(("region", "shard")),
            P(("region", "shard"), None),
            P(("region", "shard")),
            P(("region", "shard"), None),
            P("shard", None),
            P("shard", None),
            P("shard", None),
            P(),
        ),
        out_specs=(P("shard", None), P(), P()),
        check_vma=False,
    )
```

profile of v0, /device:TPU:0, one launch (start us, length us, event | category | flops | bytes accessed | tf_op | source)
XLA Modules:
  0.0 249.1 jit_solution(15187647124152556390)
XLA Ops:
  7.2 0.0 copy-start
  7.2 0.0 all-gather.6.cloned.1.call-start
  7.2 0.7 all-gather.6.cloned.1.call-update
  7.9 0.0 all-gather.4.cloned.1.call-start
  8.0 0.7 all-gather.4.cloned.1.call-update
  8.7 0.0 all-gather.8.cloned.1.call-start
  8.7 0.7 all-gather.8.cloned.1.call-update
  9.4 0.0 reduce-scatter.2.cloned.1.call-start
  9.4 0.0 copy-done
  9.5 1.0 multiply_reduce_fusion.2
  10.5 0.1 multiply_convert_fusion
  10.6 4.9 %collective-permute-start = (bf16[16,512]{1,0:T(8,128)(2,1)S(1)}, bf16[16,512]{1,0:T(8,128)(2,1)S(1)}, u32[]{:S(2)}, u32[]{:S(2)}) collective-permute-start(bf16[16,512]{1,0:T(8,128)(2,1)S(1)} %multiply_convert_fusion), channel_id=1, source_target_pairs={{0,2},{1,3},{2,4},{3,5},{4,6},{5,7},{8,10},{9,11},{10,12},{11,13},... | collective-permute-start | bytes 49160 | tf_op jit(solution)/shard_map/ppermute | solution.py:10
  15.5 1.5 collective-permute-start.1
  17.0 1.3 collective-permute-start.2
  18.3 1.3 collective-permute-start.3
  19.6 0.7 compare_select_fusion
  20.3 0.1 reshape.39
  20.4 0.7 convert_element_type.24
  21.1 0.0 collective-permute-done
  21.1 0.0 collective-permute-done.1
  21.1 0.1 constant_dynamic-update-slice_fusion.2
  21.2 0.5 collective-permute-done.2
  21.7 4.7 %collective-permute-done.3 = bf16[16,512]{1,0:T(8,128)(2,1)S(1)} collective-permute-done((bf16[16,512]{1,0:T(8,128)(2,1)S(1)}, bf16[16,512]{1,0:T(8,128)(2,1)S(1)}, u32[]{:S(2)}, u32[]{:S(2)}) %collective-permute-start.3) | collective-permute-done | bytes 16416 | tf_op jit(solution)/shard_map/ppermute | solution.py:10
  26.5 8.1 %all-gather.6.cloned.1.call-done = bf16[512,1024]{1,0:T(8,128)(2,1)} async-done(((bf16[64,1024]{1,0:T(8,128)(2,1)}), bf16[512,1024]{1,0:T(8,128)(2,1)}) %all-gather.6.cloned.1.call-update) | async-done | bytes 1048592 | tf_op jit(solution)/shard_map/all_gather | solution.py:23
  34.6 1.5 fusion.11
  36.1 5.4 %gather_fusion = f32[1024,1024]{1,0:T(8,128)} fusion(f32[80,1024]{1,0:T(8,128)S(1)} %fusion.11, s32[1024]{0:T(1024)S(1)} %broadcast_clamp_fusion), kind=kCustom, calls=%fused_computation | custom fusion | bytes 8392704 | tf_op jit(solution)/shard_map/gather | solution.py:44
  41.5 16.4 %all-gather.4.cloned.1.call-done = bf16[512,1024]{1,0:T(8,128)(2,1)} async-done(((bf16[64,1024]{1,0:T(8,128)(2,1)}), bf16[512,1024]{1,0:T(8,128)(2,1)}) %all-gather.4.cloned.1.call-update) | async-done | bytes 1048592 | tf_op jit(solution)/shard_map/all_gather | solution.py:22
  58.0 1.5 fusion.10
  59.5 2.8 %maximum_convert_fusion = bf16[16,64,1024]{2,1,0:T(8,128)(2,1)S(1)} fusion(f32[16,64,1024]{2,1,0:T(8,128)} %bitcast.10, f32[16,1024]{1,0:T(8,128)S(1)} %fusion.10), kind=kLoop, calls=%fused_computation.4 | loop fusion | flops 3145728 | bytes 6356992 | tf_op jit(solution)/shard_map/convert_element_type | solution.py:44
  62.3 26.1 %all-gather.8.cloned.1.call-done = bf16[1024,1024]{1,0:T(8,128)(2,1)} async-done(((bf16[128,1024]{1,0:T(8,128)(2,1)}), bf16[1024,1024]{1,0:T(8,128)(2,1)}) %all-gather.8.cloned.1.call-update) | async-done | bytes 2097168 | tf_op jit(solution)/shard_map/all_gather | solution.py:24
  88.4 5.9 %multiply_reduce_fusion.1 = (f32[1024]{0:T(1024)S(1)}, f32[1024,1024]{1,0:T(8,128)}) fusion(f32[1024]{0:T(1024)S(1)} %convert_element_type.24, bf16[1024,1024]{1,0:T(8,128)(2,1)S(1)} %bitcast.11, bf16[1024,1024]{1,0:T(8,128)(2,1)} %all-gather.8.cloned.1.call-done), kind=kOutput, calls=%fused_computation.3 | convolution fusion | flops 2150628352 | bytes 8396800 | tf_op jit(solution)/shard_map/dot_general | solution.py:46
  94.2 0.1 reshape.36
  94.3 0.0 copy-done.2
  94.3 0.2 select_reduce_fusion.1
  94.5 0.2 fusion.8
  94.7 0.7 select_reduce_fusion
  95.4 40.4 %psum.28 = f32[]{:T(128)} all-reduce(f32[]{:T(128)} %get-tuple-element.4), channel_id=1, replica_groups=mesh['region'=4,'shard'=8] {'region','shard'}, use_global_device_ids=true, to_apply=%region_6.7 | all-reduce | flops 1 | bytes 8 | tf_op jit(solution)/shard_map/psum | solution.py:43
  135.7 0.7 select_divide_fusion
  136.5 0.1 mul.63
  136.5 6.7 %fusion = f32[1024,1024]{1,0:T(8,128)} fusion(bf16[1024,1024]{1,0:T(8,128)(2,1)S(1)} %bitcast.12, f32[1024,1024]{1,0:T(8,128)} %get-tuple-element.11, f32[1024]{0:T(1024)S(1)} %mul.63, f32[1024]{0:T(1024)S(1)} %convert_element_type.24), kind=kOutput, calls=%fused_computation.5 | convolution fusion | flops 2151677952 | bytes 10493952 | tf_op jit(solution)/shard_map/dot_general | solution.py:59
  143.3 0.0 reduce-scatter.2.cloned.1.call-update
  143.3 0.0 all-reduce.3.cloned.1.call-start
  143.3 49.7 %reduce-scatter.2.cloned.1.call-done = f32[128,1024]{1,0:T(8,128)} async-done(((f32[1024,1024]{1,0:T(8,128)}), f32[128,1024]{1,0:T(8,128)}) %reduce-scatter.2.cloned.1.call-update) | async-done | bytes 524304 | tf_op jit(solution)/shard_map/reduce_scatter | solution.py:62
  193.0 0.0 all-reduce.3.cloned.1.call-update
  193.7 2.7 %multiply_reduce_fusion = f32[1024]{0:T(1024)S(1)} fusion(f32[1024,1024]{1,0:T(8,128)} %get-tuple-element.11, f32[1024]{0:T(1024)S(1)} %mul.63), kind=kLoop, calls=%fused_computation.1 | loop fusion | flops 3144704 | bytes 4202496 | tf_op jit(solution)/shard_map/reduce_sum | solution.py:60
  196.4 38.0 %all-reduce = (f32[1024]{0:T(1024)}, f32[]{:T(128)}) all-reduce(f32[1024]{0:T(1024)S(1)} %multiply_reduce_fusion, f32[]{:T(128)S(6)} %neg.3), channel_id=1, replica_groups=mesh['region'=4,'shard'=8] {'region','shard'}, use_global_device_ids=true, to_apply=%region_10.11 | all-reduce | flops 1025 | bytes 8200 | tf_op jit(solution)/shard_map/psum | solution.py:61
  235.7 3.9 %all-reduce.3.cloned.1.call-done = f32[128,1024]{1,0:T(8,128)} async-done(((f32[128,1024]{1,0:T(8,128)}), f32[128,1024]{1,0:T(8,128)}) %all-reduce.3.cloned.1.call-update) | async-done | bytes 524304 | tf_op jit(solution)/shard_map/psum | solution.py:63
  239.6 1.9 copy.17
  (10 shorter events, 0.0 us)
Async XLA Ops:
  7.2 2.3 copy-start
  7.2 27.4 %all-gather.6.cloned.1.call-start = ((), (), s32[]{:S(2)}) async-start(), calls=%async_computation.2 | async-start | bytes 1179648 | tf_op jit(solution)/shard_map/all_gather | solution.py:23
  7.9 50.1 %all-gather.4.cloned.1.call-start = ((), (), s32[]{:S(2)}) async-start(), calls=%async_computation.1 | async-start | bytes 1179648 | tf_op jit(solution)/shard_map/all_gather | solution.py:22
  8.7 79.7 %all-gather.8.cloned.1.call-start = ((), (), s32[]{:S(2)}) async-start(), calls=%async_computation.3 | async-start | bytes 2359296 | tf_op jit(solution)/shard_map/all_gather | solution.py:24
  9.4 183.6 %reduce-scatter.2.cloned.1.call-start = ((), (), s32[]{:S(2)}) async-start(), calls=%async_computation.4 | async-start | bytes 4718592 | tf_op jit(solution)/shard_map/reduce_scatter | solution.py:62
  10.6 10.5 %collective-permute-start = (bf16[16,512]{1,0:T(8,128)(2,1)S(1)}, bf16[16,512]{1,0:T(8,128)(2,1)S(1)}, u32[]{:S(2)}, u32[]{:S(2)}) collective-permute-start(bf16[16,512]{1,0:T(8,128)(2,1)S(1)} %multiply_convert_fusion), channel_id=1, source_target_pairs={{0,2},{1,3},{2,4},{3,5},{4,6},{5,7},{8,10},{9,11},{10,12},{11,13},... | collective-permute-start | bytes 49160 | tf_op jit(solution)/shard_map/ppermute | solution.py:10
  15.5 5.6 %collective-permute-start.1 = (bf16[16,512]{1,0:T(8,128)(2,1)S(1)}, bf16[16,512]{1,0:T(8,128)(2,1)S(1)}, u32[]{:S(2)}, u32[]{:S(2)}) collective-permute-start(bf16[16,512]{1,0:T(8,128)(2,1)S(1)} %multiply_convert_fusion), channel_id=1, source_target_pairs={{0,1},{1,2},{2,3},{3,4},{4,5},{5,6},{6,7},{8,9},{9,10},{10,11},{11... | collective-permute-start | bytes 49160 | tf_op jit(solution)/shard_map/ppermute | solution.py:10
  17.0 4.7 %collective-permute-start.2 = (bf16[16,512]{1,0:T(8,128)(2,1)S(1)}, bf16[16,512]{1,0:T(8,128)(2,1)S(1)}, u32[]{:S(2)}, u32[]{:S(2)}) collective-permute-start(bf16[16,512]{1,0:T(8,128)(2,1)S(1)} %multiply_convert_fusion), channel_id=1, source_target_pairs={{1,0},{2,1},{3,2},{4,3},{5,4},{6,5},{7,6},{9,8},{10,9},{11,10},{12... | collective-permute-start | bytes 49160 | tf_op jit(solution)/shard_map/ppermute | solution.py:10
  18.3 8.2 %collective-permute-start.3 = (bf16[16,512]{1,0:T(8,128)(2,1)S(1)}, bf16[16,512]{1,0:T(8,128)(2,1)S(1)}, u32[]{:S(2)}, u32[]{:S(2)}) collective-permute-start(bf16[16,512]{1,0:T(8,128)(2,1)S(1)} %multiply_convert_fusion), channel_id=1, source_target_pairs={{2,0},{3,1},{4,2},{5,3},{6,4},{7,5},{10,8},{11,9},{12,10},{13,11},... | collective-permute-start | bytes 49160 | tf_op jit(solution)/shard_map/ppermute | solution.py:10
  88.3 5.9 %copy-start.2 = (s32[16]{0:T(128)S(1)}, s32[16]{0:T(128)}, u32[]{:S(2)}) copy-start(s32[16]{0:T(128)} %param.12) | copy-start | bytes 196
  88.4 6.3 %copy-start.1 = (s32[16,64]{1,0:T(8,128)S(1)}, s32[16,64]{1,0:T(8,128)}, u32[]{:S(2)}) copy-start(s32[16,64]{1,0:T(8,128)} %param.13) | copy-start | bytes 12292
  143.3 96.3 %all-reduce.3.cloned.1.call-start = ((), (), s32[]{:S(2)}) async-start(), calls=%async_computation.5 | async-start | bytes 1048576 | tf_op jit(solution)/shard_map/psum | solution.py:63
Sparse Core Ops, SparseCore 0:
  9.6 24.9 all-gather.5
  36.2 21.7 all-gather.3
  59.6 28.7 all-gather.7
  143.4 49.5 reduce-scatter.1
  195.9 43.6 all-reduce.2
where the time goes:
time: 250 us; the launch traced here: 249 us
  waiting for transfers between devices  112 us (45%)
  blocking collectives  78.3 us (31%)
  between operations  17 us (7%)
  matrix products  16.7 us (7%)
  starting transfers between devices  9.17 us (4%)
  other arithmetic  8.83 us (4%)
  local copies, waits for them, and re-layouts  7.56 us (3%)
    reduce_scatter x1, waiting for transfers between devices, shards(): lax.psum_scatter(grad, 'shard', scatter_dimension=0, tiled=True)  49.7 us
    psum x1, blocking collectives, shards(): total = lax.psum(jnp.sum(flow_f), ('region', 'shard'))  40.4 us
    psum x1, blocking collectives, shards(): numer_all, out_grad = lax.psum((numer, gout), ('region', 'shard'))  38 us
    all_gather x1, waiting for transfers between devices, shards(): lax.all_gather(w_hidden, 'shard', axis=0, tiled=True)  26.1 us
    all_gather x1, waiting for transfers between devices, shards(): lax.all_gather(w_anchor, 'shard', axis=0, tiled=True)  16.4 us
    ppermute x4, starting transfers between devices, shifted(): return lax.ppermute(array, axis, pairs)  8.97 us
    all_gather x1, waiting for transfers between devices, shards(): lax.all_gather(w_dest, 'shard', axis=0, tiled=True)  8.12 us
    dot_general x1, matrix products, shards(): lax.dot_general(first, pre, (((0,), (0,)), ((), ())), preferred_element_t...  6.74 us
  transfers between devices with their start and end apart: 9, of which 7 were waited for; matrix products, arithmetic and copies ran while one was open for 7% of the time, Pallas kernels for 0%

commit v1 on v0

v1 whole, which is shorter than its diff:
```python
import functools

import jax
import jax.numpy as jnp
from jax import lax
from jax.experimental import pallas as pl
from jax.experimental.pallas import tpu as pltpu
from jax.sharding import PartitionSpec as P

BF = jnp.bfloat16
F32 = jnp.float32
REACH = 2
TAIL = 16
MIB = 1024 * 1024
VMEM = pl.BlockSpec(memory_space=pltpu.VMEM)


def along_z(array, by):
    devices = lax.axis_size("shard")
    return lax.ppermute(array, "shard", [(i, (i + 2 * by) % devices) for i in range(devices)])


def swap_core(array):
    devices = lax.axis_size("shard")
    return lax.ppermute(array, "shard", [(i, i ^ 1) for i in range(devices)])


def swap_region(array, by):
    devices = lax.axis_size("region")
    return lax.ppermute(array, "region", [(i, i ^ by) for i in range(devices)])


def room(mib):
    return pltpu.CompilerParams(vmem_limit_bytes=int(mib * MIB))


def identity(n):
    same = lax.broadcasted_iota(jnp.int32, (n, n), 0) == lax.broadcasted_iota(jnp.int32, (n, n), 1)
    return jnp.where(same, 1.0, 0.0).astype(BF)


def turned(one, array):
    return lax.dot_general(one, array, (((1,), (1,)), ((), ())), preferred_element_type=F32).astype(BF)


def split(value):
    high = value.astype(BF)
    return high, (value - high.astype(F32)).astype(BF)


def pack_tail(sums):
    high, low = split(sums)
    return jnp.concatenate([high.astype(F32), low.astype(F32)], axis=0).astype(BF)


def unpack_tail(rows):
    wide = rows.astype(F32)
    return wide[:8] + wide[8:]


def unit_rows(shard_at, rows, cols, region):
    first = shard_at * rows
    return pl.ds(pl.multiple_of(((first // cols) ^ region) * cols + first % cols, rows), rows)


def score_kernel(n_region, n_z, blk, slots, *refs):
    half = 2 + n_region
    mine, other, rest = refs[:half], refs[half : 2 * half], refs[2 * half :]
    w_out, first_out, act_out, score_out, ids, flows, feat, own, w_in, w_mid, w_mid_t, table, tables, plain = rest
    step = pl.program_id(0)
    region = lax.axis_index("region")
    shard = lax.axis_index("shard")
    z, core = shard // 2, shard % 2
    window = (2 * REACH + 1) * blk
    lines = blk * slots // 128
    hidden, cols = w_mid.shape
    parts = feat.shape[1] // cols

    @pl.when(step == 0)
    def assemble():
        raw_cut = mine[0].shape[1] // 2
        dest_rows = (n_z - 1) * raw_cut
        feat_rows = 3 * parts * blk
        slot_row = dest_rows + feat_rows
        slot_rows = blk if cols >= 2 * slots else 2 * blk
        anchor_base = slot_row + slot_rows
        for source, core_at in ((mine, core), (other, 1 - core)):
            raw, mids, planes = source[0], source[1], source[2:]
            rows_mid = hidden // (2 * n_z)
            for j in range(n_z):
                shard_at = 2 * lax.rem(z - j + n_z, n_z) + core_at
                at = pl.ds(pl.multiple_of(shard_at * raw_cut, raw_cut), raw_cut)
                mid = rows_mid + (j - 1) * (rows_mid + raw_cut) if j > 0 else 0
                w_mid[unit_rows(shard_at, rows_mid, cols, region), :] = mids[mid : mid + rows_mid, :]
                for i in range(n_region):
                    base = (j - 1) * raw_cut
                    if j == 0:
                        w_in[i, at, :cols] = raw[i, :raw_cut, :]
                        w_in[i, at, cols:] = raw[i, raw_cut:, :]
                    else:
                        if i == n_region - 1:
                            w_in[i, at, :cols] = mids[mid + rows_mid : mid + rows_mid + raw_cut, :]
                        else:
                            w_in[i, at, :cols] = planes[i][anchor_base + base : anchor_base + base + raw_cut, :]
                        w_in[i, at, cols:] = planes[i][base : base + raw_cut, :]
        one = identity(cols)
        w_mid_t[...] = turned(one, w_mid[...])
        left = lax.broadcasted_iota(jnp.int32, (lines, 128), 1) < slots
        for i in range(n_region):
            near, far = mine[2 + i], other[2 + i]
            for t in range(parts):
                below, here, above = (
                    slice(dest_rows + (k * parts + t) * blk, dest_rows + (k * parts + t + 1) * blk) for k in range(3)
                )
                lanes = slice(t * cols, (t + 1) * cols)
                before = jnp.where(core == 0, far[below, :], far[here, :])
                after = jnp.where(core == 0, far[here, :], far[above, :])
                for k, part in enumerate((near[below, :], before, near[here, :], after, near[above, :])):
                    feat[i * window + k * blk : i * window + (k + 1) * blk, lanes] = part
                own[i * blk : (i + 1) * blk, lanes] = near[here, :]
            if slot_rows == blk:
                plain[...] = near[slot_row : slot_row + blk, : 2 * slots].astype(F32)
            else:
                plain[:, :slots] = near[slot_row : slot_row + blk, :slots].astype(F32)
                plain[:, slots:] = near[slot_row + blk : slot_row + 2 * blk, :slots].astype(F32)
            even = plain[pl.ds(0, lines, stride=2), :]
            odd = plain[pl.ds(1, lines, stride=2), :]
            ids[i] = jnp.where(left, even, pltpu.roll(odd, slots, 1))
            flows[i] = jnp.where(left, pltpu.roll(even, slots, 1), odd)
        for k in range(n_region):
            lanes = slice(k * cols, (k + 1) * cols)
            high, low = split(jnp.dot(feat[...], w_in[k, :, cols:], preferred_element_type=F32))
            high_a, low_a = split(jnp.dot(own[...], w_in[k, :, :cols], preferred_element_type=F32))
            for i in range(n_region):
                table[i, :window, lanes] = high[i * window : (i + 1) * window]
                table[i, window : 2 * window, lanes] = low[i * window : (i + 1) * window]
                table[i, 2 * window : 2 * window + blk, lanes] = high_a[i * blk : (i + 1) * blk]
                table[i, 2 * window + blk :, lanes] = low_a[i * blk : (i + 1) * blk]
        wide = one if cols == 256 else identity(256)
        for i in range(n_region):
            for k in range(0, hidden, 256):
                tables[i, k : k + 256, :] = turned(wide, table[i, :, k : k + 256])

    group = 8
    pairs = group * slots
    spread = pairs // 128
    chosen = ids[step]
    lookup = tables[step]
    dest_row = lax.broadcasted_iota(jnp.int32, (2 * window, pairs), 0)
    dest_row = jnp.where(dest_row >= window, dest_row - window, dest_row).astype(F32)
    anchor_row = lax.broadcasted_iota(jnp.int32, (2 * blk, pairs), 0)
    anchor_row = jnp.where(anchor_row >= blk, anchor_row - blk, anchor_row)
    anchor_lane = lax.broadcasted_iota(jnp.int32, (2 * blk, pairs), 1) // slots
    weight = w_out[...]
    for c in range(blk // group):
        at = slice(c * pairs, (c + 1) * pairs)
        spot = jnp.concatenate([chosen[c * spread + k : c * spread + k + 1, :] for k in range(spread)], axis=1)
        dest_hot = jnp.where(dest_row == spot, 1.0, 0.0)
        anchor_hot = jnp.where(anchor_row == anchor_lane + c * group, 1.0, 0.0)
        onehot = jnp.concatenate([dest_hot, anchor_hot], axis=0).astype(BF)
        first = jnp.maximum(jnp.dot(lookup, onehot, preferred_element_type=F32).astype(BF), 0)
        first_out[:, at] = first
        active = jnp.maximum(jnp.dot(w_mid_t[...], first, preferred_element_type=F32), 0.0)
        act_out[:, at] = active.astype(BF)
        score = jnp.sum(active * weight, axis=0, keepdims=True)
        for k in range(spread):
            score_out[c * spread + k : c * spread + k + 1, :] = score[:, k * 128 : (k + 1) * 128]


def grad_kernel(n_region, n_z, slots, *refs):
    scores, rest = refs[:n_region], refs[n_region:]
    ids, flows, first, act, w_out, keep, send, grad, gout, sums = rest
    step = pl.program_id(0)
    cols = act.shape[0]

    @pl.when(step == 0)
    def clear():
        grad[...] = jnp.zeros_like(grad)
        gout[...] = jnp.zeros_like(gout)
        sums[...] = jnp.zeros_like(sums)

    score = scores[0][...]
    for other in scores[1:]:
        score = score + other[...]
    valid = ids[step] >= 0
    left = lax.broadcasted_iota(jnp.int32, score.shape, 1) < slots

    def halves(reduce, value, rest):
        low = reduce(jnp.where(left, value, rest), axis=1, keepdims=True)
        high = reduce(jnp.where(left, rest, value), axis=1, keepdims=True)
        return jnp.where(left, low, high)

    top = halves(jnp.max, jnp.where(valid, score, -jnp.inf), -jnp.inf)
    expo = jnp.where(valid, jnp.exp(score - top), 0.0)
    mass = halves(jnp.sum, expo, 0.0)
    probs = expo / mass
    logp = score - top - jnp.log(mass)
    flow = flows[step]
    anchor_total = halves(jnp.sum, flow, 0.0)
    sgrad = jnp.where(valid, probs * anchor_total - flow, 0.0)
    sums[0] += flow
    sums[1] -= jnp.where(valid, flow * logp, 0.0)

    lanes = score.shape[1]
    weight = jnp.broadcast_to(w_out[...], (cols, lanes))
    pre = []
    for q in range(score.shape[0]):
        line = sgrad[q : q + 1, :]
        active = act[:, q * lanes : (q + 1) * lanes].astype(F32)
        gained = active * line if q == 0 else gained + active * line
        pre.append(jnp.where(active > 0, weight * line, 0.0).astype(BF))
    gout[...] += gained
    pre = jnp.concatenate(pre, axis=1)
    grad[...] += lax.dot_general(first[...], pre, (((1,), (1,)), ((), ())), preferred_element_type=F32)

    @pl.when(step == n_region - 1)
    def finish():
        out = jnp.sum(gout[...].T, axis=0, keepdims=True)
        total = jnp.sum(sums[0])
        numer = jnp.sum(sums[1])
        row = lax.broadcasted_iota(jnp.int32, (8, cols), 0)
        lane = lax.broadcasted_iota(jnp.int32, (8, cols), 1)
        stats = jnp.where(lane == 0, total, jnp.where(lane == 1, numer, 0.0))
        tail = pack_tail(jnp.where(row == 0, out, jnp.where(row == 1, stats, 0.0)))
        rows = keep.shape[1] - TAIL
        region = lax.axis_index("region")
        shard = lax.axis_index("shard")
        z, core = shard // 2, shard % 2
        for j in range(n_z):
            z_at = lax.rem(z + j, n_z)
            for target, core_at in ((keep, core), (send, 1 - core)):
                target[j, :rows, :] = grad[unit_rows(2 * z_at + core_at, rows, cols, region), :].astype(BF)
                target[j, rows:, :] = tail


def core_sum_kernel(keep, received, *outs):
    for j, out in enumerate(outs):
        rows = out.shape[0] - TAIL
        out[:rows, :] = (keep[j, :rows, :].astype(F32) + received[j, :rows, :].astype(F32)).astype(BF)
        out[rows:, :] = pack_tail(unpack_tail(keep[j, rows:, :]) + unpack_tail(received[j, rows:, :]))


def z_sum_kernel(*refs):
    blocks, (out, tails) = refs[:-2], refs[-2:]
    n_z = len(blocks)
    rows = out.shape[0] - TAIL
    total = blocks[0][:rows, :].astype(F32)
    for block in blocks[1:]:
        total = total + block[:rows, :].astype(F32)
    out[:rows, :] = total.astype(BF)
    for j, block in enumerate(blocks):
        tails[j] = unpack_tail(block[rows:, :])
    z = lax.axis_index("shard") // 2
    tail = tails[z]
    for z_at in range(1, n_z):
        tail = tail + tails[lax.rem(z - z_at + n_z, n_z)]
    out[rows:, :] = pack_tail(tail)


def finish_kernel(*refs):
    blocks, (grad, out_grad, loss, held) = refs[:-4], refs[-4:]
    n_region = len(blocks)
    cols = blocks[0].shape[1]
    rows = grad.shape[0]
    for i, block in enumerate(blocks):
        held[i] = block[...]
    region = lax.axis_index("region")
    stats = unpack_tail(held[region][rows:, :])
    total = stats[1:2, 0:1]
    numer = stats[1:2, 1:2]
    loss[...] = numer / total
    inverse = 1.0 / total
    for q in range(n_region):
        block = held[region ^ q]
        grad[:, q * cols : (q + 1) * cols] = block[:rows, :].astype(F32) * inverse
        out_grad[:, q * cols : (q + 1) * cols] = unpack_tail(block[rows:, :])[0:1, :] * inverse


def shards(tiles, tile_block, neighbors, counts, flows, w_anchor, w_dest, w_hidden, w_out):
    blk = counts.shape[0]
    slots = neighbors.shape[1]
    n_region = lax.axis_size("region")
    n_shard = lax.axis_size("shard")
    n_z = n_shard // 2
    hidden = w_hidden.shape[1]
    rows_in = w_anchor.shape[0]
    depth = rows_in * n_shard
    cols = hidden // n_region
    pairs = blk * slots
    lines = pairs // 128
    window = (2 * REACH + 1) * blk
    region = lax.axis_index("region")

    def cut(array, i):
        return lax.dynamic_slice_in_dim(array, (region ^ i) * cols, cols, array.ndim - 1)

    def along_rows(features):
        return [features[:, t * cols : (t + 1) * cols] for t in range(depth // cols)]

    raw = jnp.stack([jnp.concatenate([cut(w_anchor, i), cut(w_dest, i)], axis=0) for i in range(n_region)])
    piece = jnp.concatenate([cut(w_anchor, 0), cut(w_dest, 0)], axis=0)

    piece, tile_block = lax.optimization_barrier((piece, tile_block))
    onehot = (tile_block[None, :] == jnp.arange(blk, dtype=jnp.int32)[:, None]).astype(BF)
    sums = jnp.dot(onehot, tiles, preferred_element_type=F32)
    scale = lax.rsqrt(jnp.mean(sums * sums, axis=-1, keepdims=True) + 1e-05)
    features = jnp.concatenate(along_rows((sums * scale).astype(BF)), axis=0)

    payload = jnp.concatenate([piece, features], axis=0)
    from_z = [along_z(payload if j in (1, n_z - 1) else piece, j) for j in range(1, n_z)]

    spot = neighbors % (blk * n_shard) - (lax.axis_index("shard") - REACH) * blk
    valid = jnp.arange(slots, dtype=jnp.int32)[None, :] < counts[:, None]
    slot_table = jnp.concatenate([jnp.where(valid, spot, -1), flows], axis=1 if cols >= 2 * slots else 0).astype(BF)
    slot_table = jnp.pad(slot_table, ((0, 0), (0, cols - slot_table.shape[1])))

    held = 2 * rows_in
    ends = [p[held:] for p in (from_z[0], from_z[-1])]
    shared = jnp.concatenate([p[rows_in:held] for p in from_z] + [ends[0], features, ends[1], slot_table], axis=0)
    plane = jnp.concatenate([shared] + [p[:rows_in] for p in from_z], axis=0)
    planes = [plane] + [swap_region(plane, i) for i in range(1, n_region - 1)] + [swap_region(shared, n_region - 1)]

    mid_raw = cut(w_hidden, 0)
    far_plane = swap_core(plane)
    mid_send, far_plane = lax.optimization_barrier(
        (jnp.concatenate([mid_raw, cut(w_anchor, n_region - 1)], axis=0), far_plane)
    )
    mids = jnp.concatenate([mid_raw] + [along_z(mid_send, j) for j in range(1, n_z)], axis=0)
    mine = [raw, mids, *planes]
    other = [swap_core(raw), swap_core(mids), far_plane] + [swap_core(x) for x in planes[1:]]
    weight_out = cut(w_out, 0).astype(F32).reshape(cols, 1)

    first, act, score, ids, flow = pl.pallas_call(
        functools.partial(score_kernel, n_region, n_z, blk, slots),
        grid=(n_region,),
        in_specs=[VMEM] * (2 * len(mine) + 1),
        out_specs=[
            pl.BlockSpec((hidden, pairs), lambda i: (0, i)),
            pl.BlockSpec((cols, pairs), lambda i: (0, i)),
            pl.BlockSpec((lines, 128), lambda i: (i, 0)),
            VMEM,
            VMEM,
        ],
        scratch_shapes=[
            pltpu.VMEM((n_region * window, depth), BF),
            pltpu.VMEM((n_region * blk, depth), BF),
            pltpu.VMEM((n_region, depth, 2 * cols), BF),
            pltpu.VMEM((hidden, cols), BF),
            pltpu.VMEM((cols, hidden), BF),
            pltpu.VMEM((n_region, 2 * (window + blk), hidden), BF),
            pltpu.VMEM((n_region, hidden, 2 * (window + blk)), BF),
            pltpu.VMEM((blk, 2 * slots), F32),
        ],
        out_shape=[
            jax.ShapeDtypeStruct((hidden, n_region * pairs), BF),
            jax.ShapeDtypeStruct((cols, n_region * pairs), BF),
            jax.ShapeDtypeStruct((n_region * lines, 128), F32),
            jax.ShapeDtypeStruct((n_region, lines, 128), F32),
            jax.ShapeDtypeStruct((n_region, lines, 128), F32),
        ],
        compiler_params=room(14 + 1.25 * n_region),
        name="scores",
    )(*mine, *other, weight_out)

    parts = [score] + [swap_region(score, i) for i in range(1, n_region)]
    rows = hidden // n_shard
    block = jax.ShapeDtypeStruct((rows + TAIL, cols), BF)
    blocks = jax.ShapeDtypeStruct((n_z, rows + TAIL, cols), BF)
    keep, send = pl.pallas_call(
        functools.partial(grad_kernel, n_region, n_z, slots),
        grid=(n_region,),
        in_specs=[pl.BlockSpec((lines, 128), functools.partial(lambda k, i: (i ^ k, 0), k)) for k in range(n_region)]
        + [
            VMEM,
            VMEM,
            pl.BlockSpec((hidden, pairs), lambda i: (0, i)),
            pl.BlockSpec((cols, pairs), lambda i: (0, i)),
            VMEM,
        ],
        out_specs=[VMEM, VMEM],
        scratch_shapes=[
            pltpu.VMEM((hidden, cols), F32),
            pltpu.VMEM((cols, 128), F32),
            pltpu.VMEM((2, lines, 128), F32),
        ],
        out_shape=[blocks, blocks],
        compiler_params=room(14),
        name="gradient",
    )(*parts, ids, flow, first, act, weight_out)

    own_rows = pl.pallas_call(
        core_sum_kernel,
        in_specs=[VMEM] * 2,
        out_specs=[VMEM] * n_z,
        out_shape=[block] * n_z,
        compiler_params=room(4),
        name="core_sum",
    )(keep, swap_core(send))
    own_rows = [own_rows[0]] + [along_z(own_rows[j], j) for j in range(1, n_z)]
    reduced = pl.pallas_call(
        z_sum_kernel,
        in_specs=[VMEM] * n_z,
        out_specs=VMEM,
        out_shape=block,
        scratch_shapes=[pltpu.VMEM((n_z, 8, cols), F32)],
        compiler_params=room(4),
        name="z_sum",
    )(*own_rows)
    final = [reduced] + [swap_region(reduced, i) for i in range(1, n_region)]
    hidden_grad, out_grad, loss = pl.pallas_call(
        finish_kernel,
        in_specs=[VMEM] * n_region,
        out_specs=[VMEM] * 3,
        out_shape=[
            jax.ShapeDtypeStruct((rows, hidden), F32),
            jax.ShapeDtypeStruct((1, hidden), F32),
            jax.ShapeDtypeStruct((1, 1), F32),
        ],
        scratch_shapes=[pltpu.VMEM((n_region, rows + TAIL, cols), BF)],
        compiler_params=room(4),
        name="finish",
    )(*final)
    return (hidden_grad, out_grad.reshape(hidden), loss.reshape(()))


def solution(mesh):
    return jax.shard_map(
        shards,
        mesh=mesh,
        in_specs=(
            P(("region", "shard"), None),
            P(("region", "shard")),
            P(("region", "shard"), None),
            P(("region", "shard")),
            P(("region", "shard"), None),
            P("shard", None),
            P("shard", None),
            P("shard", None),
            P(),
        ),
        out_specs=(P("shard", None), P(), P()),
        check_vma=False,
    )
```

time: 250 us -> 71.7 us (0.29)
  waiting for transfers between devices: 112 us -> 23.3 us
  blocking collectives: 78.3 us -> 0 us
  starting transfers between devices: 9.17 us -> 26.7 us
  between operations: 17 us -> 0.89 us
  matrix products: 16.7 us -> 1.04 us
  Pallas kernels: 0 us -> 14.8 us
  other arithmetic: 8.83 us -> 2.5 us
  local copies, waits for them, and re-layouts: 7.56 us -> 2.03 us
    psum x2 -> x0, blocking collectives: 78.3 us -> none  [the longest x1 40.4 us: shards(): total = lax.psum(jnp.sum(flow_f), ('region', 'shard'))]
    all_gather x3 -> x0, waiting for transfers between devices: 50.6 us -> none  [the longest x1 26.1 us: shards(): lax.all_gather(w_hidden, 'shard', axis=0, tiled=True)]
    reduce_scatter x1 -> x0, waiting for transfers between devices: 49.7 us -> none  [shards(): lax.psum_scatter(grad, 'shard', scatter_dimension=0, tiled=True)]
    ppermute x4 -> x25, waiting for transfers between devices: 5.28 us -> 23.3 us  [the longest x9 14.6 us: along_z(): lax.ppermute(array, 'shard', [(i, (i + 2 * by) % devices) for i in range(...]
    ppermute x4 -> x25, starting transfers between devices: 8.97 us -> 26.7 us  [the longest x9 14.2 us: along_z(): lax.ppermute(array, 'shard', [(i, (i + 2 * by) % devices) for i in range(...]
    dot_general x5 -> x1, matrix products: 16.7 us -> 1.04 us  [shards(): sums = jnp.dot(onehot, tiles, preferred_element_type=F32)]
    pallas_call x0 -> x5, Pallas kernels: none -> 14.8 us  [the longest x1 8.68 us: shards(): pl.pallas_call(functools.partial(score_kernel, n_region, n_z, blk, slots)...]
    gather x1 -> x0, local copies, waits for them, and re-layouts: 5.43 us -> none  [shards(): dest_proj[dest_slot]]
  transfers between devices with their start and end apart: 9 -> 25, of which waited for: 7 -> 13; matrix products, arithmetic and copies ran while one was open for 7% -> 6% of each run, Pallas kernels for 0% -> 0%
where the time goes in v1:
time: 71.7 us; the launch traced here: 71.3 us
  starting transfers between devices  26.7 us (37%)
  waiting for transfers between devices  23.3 us (32%)
  Pallas kernels  14.8 us (21%)
  other arithmetic  2.5 us (3%)
  local copies, waits for them, and re-layouts  2.03 us (3%)
  matrix products  1.04 us (1%)
  between operations  0.89 us (1%)
    ppermute x9, waiting for transfers between devices, along_z(): lax.ppermute(array, 'shard', [(i, (i + 2 * by) % devices) for i in range(...  14.6 us
    ppermute x9, starting transfers between devices, along_z(): lax.ppermute(array, 'shard', [(i, (i + 2 * by) % devices) for i in range(...  14.2 us
    ppermute x9, starting transfers between devices, swap_region(): return lax.ppermute(array, 'region', [(i, i ^ by) for i in range(devices)])  11.1 us
    pallas_call x1, Pallas kernels, shards(): pl.pallas_call(functools.partial(score_kernel, n_region, n_z, blk, slots)...  8.68 us
    ppermute x9, waiting for transfers between devices, swap_region(): return lax.ppermute(array, 'region', [(i, i ^ by) for i in range(devices)])  6.07 us
    pallas_call x1, Pallas kernels, shards(): pl.pallas_call(functools.partial(grad_kernel, n_region, n_z, slots), grid...  5.13 us
    ppermute x7, waiting for transfers between devices, swap_core(): return lax.ppermute(array, 'shard', [(i, i ^ 1) for i in range(devices)])  2.65 us
    dynamic_slice x2, local copies, waits for them, and re-layouts, cut(): lax.dynamic_slice_in_dim(array, (region ^ i) * cols, cols, array.ndim - 1)  1.83 us
  transfers between devices with their start and end apart: 25, of which 13 were waited for; matrix products, arithmetic and copies ran while one was open for 6% of the time, Pallas kernels for 0%

profile of v1, /device:TPU:0, one launch (start us, length us, event | category | flops | bytes accessed | tf_op | source)
XLA Modules:
  0.0 71.3 jit_solution(2314468702654440959)
XLA Ops:
  0.7 1.0 %constant_dynamic-slice_fusion.7 = (bf16[64,256]{1,0:T(8,128)(2,1)S(1)}, bf16[64,256]{1,0:T(8,128)(2,1)S(1)}, bf16[64,256]{1,0:T(8,128)(2,1)S(1)}, bf16[64,256]{...) fusion(bf16[64,1024]{1,0:T(8,128)(2,1)} %param.15, ...), kind=kLoop, calls=%fused_computation.51 | loop fusion | bytes 524304 | tf_op jit(solution)/shard_map/dynamic_slice | solution.py:295
  1.7 4.1 %collective-permute-start.1 = (bf16[128,256]{1,0:T(8,128)(2,1)S(1)}, bf16[128,256]{1,0:T(8,128)(2,1)S(1)}, u32[]{:S(2)}, u32[]{:S(2)}) collective-permute-start(bf16[128,256]{1,0:T(8,128)(2,1)S(1)} %get-tuple-element.21), channel_id=1, source_target_pairs={{0,4},{1,5},{2,6},{3,7},{4,0},{5,1},{6,2},{7,3},{8,12},{9,13},{10,... | collective-permute-start | bytes 196616 | tf_op jit(solution)/shard_map/ppermute | solution.py:20
  5.8 1.0 %multiply_reduce_fusion = (f32[16]{0:T(128)S(1)}, f32[16,512]{1,0:T(8,128)S(1)}) fusion(bf16[1024,512]{1,0:T(8,128)(2,1)S(1)} %copy-done, s32[1024]{0:T(1024)} %param.10), kind=kOutput, calls=%fused_computation.30 | convolution fusion | flops 16809968 | bytes 1085504 | tf_op jit(solution)/shard_map/dot_general | solution.py:305
  6.8 0.1 multiply_convert_fusion
  6.9 1.4 %collective-permute-start.2 = (bf16[160,256]{1,0:T(8,128)(2,1)S(1)}, bf16[160,256]{1,0:T(8,128)(2,1)S(1)}, u32[]{:S(2)}, u32[]{:S(2)}) collective-permute-start(bf16[160,256]{1,0:T(8,128)(2,1)S(1)} %pad_maximum_fusion.3), channel_id=1, source_target_pairs={{0,6},{1,7},{2,0},{3,1},{4,2},{5,3},{6,4},{7,5},{8,14},{9,15},{10,... | collective-permute-start | bytes 245768 | tf_op jit(solution)/shard_map/ppermute | solution.py:20
  8.3 0.7 collective-permute-start
  9.0 0.7 convert.8
  9.7 0.8 %fusion.7 = bf16[16,64]{1,0:T(8,128)(2,1)S(1)} fusion(s32[16,64]{1,0:T(8,128)} %param.11, s32[]{:T(128)S(6)} %mul.42, s32[16]{0:T(128)} %param.12), kind=kLoop, calls=%fused_computation.41 | loop fusion | flops 15360 | bytes 6212 | tf_op jit(solution)/shard_map/convert.1
  10.5 0.8 %constant_dynamic-slice_fusion = bf16[128,256]{1,0:T(8,128)(2,1)S(1)} fusion(bf16[128,1024]{1,0:T(8,128)(2,1)} %param.16, s32[]{:T(128)S(6)} %select_n.32), kind=kLoop, calls=%fused_computation.44 | loop fusion | bytes 131076 | tf_op jit(solution)/shard_map/dynamic_slice | solution.py:295
  11.3 3.2 %collective-permute-done = bf16[160,256]{1,0:T(8,128)(2,1)S(1)} collective-permute-done((bf16[160,256]{1,0:T(8,128)(2,1)S(1)}, bf16[160,256]{1,0:T(8,128)(2,1)S(1)}, u32[]{:S(2)}, u32[]{:S(2)}) %collective-permute-start) | collective-permute-done | bytes 81952 | tf_op jit(solution)/shard_map/ppermute | solution.py:20
  14.7 0.1 constant_dynamic-update-slice_fusion.11
  14.9 1.6 %collective-permute-start.8 = (bf16[496,256]{1,0:T(8,128)(2,1)S(1)}, bf16[496,256]{1,0:T(8,128)(2,1)S(1)}, u32[]{:S(2)}, u32[]{:S(2)}) collective-permute-start(bf16[496,256]{1,0:T(8,128)(2,1)S(1)} %constant_dynamic-update-slice_fusion.refs_2_), channel_id=1, source_target_pairs={{0,16},{8,24},{16,0},{24,8},{1,17},{9,25},{17,1},{25,9},{2,18},{10... | collective-permute-start | bytes 761864 | tf_op jit(solution)/shard_map/ppermute | solution.py:30
  16.5 1.5 %collective-permute-start.7 = (bf16[496,256]{1,0:T(8,128)(2,1)S(1)}, bf16[496,256]{1,0:T(8,128)(2,1)S(1)}, u32[]{:S(2)}, u32[]{:S(2)}) collective-permute-start(bf16[496,256]{1,0:T(8,128)(2,1)S(1)} %constant_dynamic-update-slice_fusion.refs_2_), channel_id=1, source_target_pairs={{0,8},{8,0},{16,24},{24,16},{1,9},{9,1},{17,25},{25,17},{2,10},{10... | collective-permute-start | bytes 761864 | tf_op jit(solution)/shard_map/ppermute | solution.py:30
  18.0 1.5 %collective-permute-start.6 = (bf16[192,256]{1,0:T(8,128)(2,1)S(1)}, bf16[192,256]{1,0:T(8,128)(2,1)S(1)}, u32[]{:S(2)}, u32[]{:S(2)}) collective-permute-start(bf16[192,256]{1,0:T(8,128)(2,1)S(1)} %pad_maximum_fusion.2), channel_id=1, source_target_pairs={{0,6},{1,7},{2,0},{3,1},{4,2},{5,3},{6,4},{7,5},{8,14},{9,15},{10,... | collective-permute-start | bytes 294920 | tf_op jit(solution)/shard_map/ppermute | solution.py:20
  19.5 1.4 %collective-permute-start.4 = (bf16[192,256]{1,0:T(8,128)(2,1)S(1)}, bf16[192,256]{1,0:T(8,128)(2,1)S(1)}, u32[]{:S(2)}, u32[]{:S(2)}) collective-permute-start(bf16[192,256]{1,0:T(8,128)(2,1)S(1)} %pad_maximum_fusion.2), channel_id=1, source_target_pairs={{0,2},{1,3},{2,4},{3,5},{4,6},{5,7},{6,0},{7,1},{8,10},{9,11},{10,... | collective-permute-start | bytes 294920 | tf_op jit(solution)/shard_map/ppermute | solution.py:20
  20.9 1.8 %collective-permute-done.6 = bf16[192,256]{1,0:T(8,128)(2,1)S(1)} collective-permute-done((bf16[192,256]{1,0:T(8,128)(2,1)S(1)}, bf16[192,256]{1,0:T(8,128)(2,1)S(1)}, u32[]{:S(2)}, u32[]{:S(2)}) %collective-permute-start.6) | collective-permute-done | bytes 98336 | tf_op jit(solution)/shard_map/ppermute | solution.py:20
  22.7 1.0 %collective-permute-start.9 = (bf16[304,256]{1,0:T(8,128)(2,1)S(1)}, bf16[304,256]{1,0:T(8,128)(2,1)}, u32[]{:S(2)}, u32[]{:S(2)}) collective-permute-start(bf16[304,256]{1,0:T(8,128)(2,1)S(1)} %get-tuple-element.63), channel_id=1, source_target_pairs={{0,24},{8,16},{16,8},{24,0},{1,25},{9,17},{17,9},{25,1},{2,26},{10... | collective-permute-start | bytes 466952 | tf_op jit(solution)/shard_map/ppermute | solution.py:30
  23.7 5.3 %collective-permute-done.5 = bf16[192,256]{1,0:T(8,128)(2,1)S(1)} collective-permute-done((bf16[192,256]{1,0:T(8,128)(2,1)S(1)}, bf16[192,256]{1,0:T(8,128)(2,1)S(1)}, u32[]{:S(2)}, u32[]{:S(2)}) %collective-permute-start.5) | collective-permute-done | bytes 98336 | tf_op jit(solution)/shard_map/ppermute | solution.py:20
  29.0 0.1 collective-permute-start.11
  29.1 0.6 collective-permute-start.10
  29.6 0.1 collective-permute-start.13
  29.7 0.4 collective-permute-start.12
  30.2 0.1 collective-permute-start.14
  30.2 0.8 %dynamic-slice_convert_fusion = f32[256]{0:T(256)S(1)} fusion(bf16[1024]{0:T(1024)(128)(2,1)} %param.17, s32[]{:T(128)S(6)} %select_n.32), kind=kLoop, calls=%fused_computation.53 | loop fusion | flops 256 | bytes 1540 | tf_op jit(solution)/shard_map/reshape | solution.py:331
  31.0 0.1 copy.12.refs_12_.refs_8_
  31.1 1.1 %collective-permute-done.14.refs_11_ = bf16[304,256]{1,0:T(8,128)(2,1)} collective-permute-done((bf16[304,256]{1,0:T(8,128)(2,1)}, bf16[304,256]{1,0:T(8,128)(2,1)}, u32[]{:S(2)}, u32[]{:S(2)}) %collective-permute-start.14) | collective-permute-done | bytes 155680 | tf_op jit(solution)/shard_map/ppermute | solution.py:25
  32.2 8.7 %scores.1 = (bf16[1024,4096]{1,0:T(8,128)(2,1)S(1)}, bf16[256,4096]{1,0:T(8,128)(2,1)S(1)}, f32[32,128]{1,0:T(8,128)S(1)}, f32[4,8,128]{2,1,0:T(8,128)S(1)}, f32[4,8,128]{2,1,0:T(8,128)S(1)}) custom-call(bf16[4,128,256]{2,1,0:T(8,128)(2,1)S(1)} %pad_maximum_fusion.1.refs_0_, bf16[704,256]{1,0:T(8,128)(2,1)S(1)} %pad_maximum_fusion.refs_1_, ...), custom_call_target="tpu_custom_call" | custom-call | tf_op jit(solution)/shard_map/scores/pallas_call | solution.py:333
  40.9 1.1 %collective-permute-start.17 = (f32[32,128]{1,0:T(8,128)S(1)}, f32[32,128]{1,0:T(8,128)S(1)}, u32[]{:S(2)}, u32[]{:S(2)}) collective-permute-start(f32[32,128]{1,0:T(8,128)S(1)} %get-tuple-element.25.refs_0_), channel_id=1, source_target_pairs={{0,24},{8,16},{16,8},{24,0},{1,25},{9,17},{17,9},{25,1},{2,26},{10... | collective-permute-start | bytes 49160 | tf_op jit(solution)/shard_map/ppermute | solution.py:30
  42.1 0.9 %collective-permute-start.16 = (f32[32,128]{1,0:T(8,128)S(1)}, f32[32,128]{1,0:T(8,128)S(1)}, u32[]{:S(2)}, u32[]{:S(2)}) collective-permute-start(f32[32,128]{1,0:T(8,128)S(1)} %get-tuple-element.25.refs_0_), channel_id=1, source_target_pairs={{0,16},{8,24},{16,0},{24,8},{1,17},{9,25},{17,1},{25,9},{2,18},{10... | collective-permute-start | bytes 49160 | tf_op jit(solution)/shard_map/ppermute | solution.py:30
  43.0 1.5 %collective-permute-start.15 = (f32[32,128]{1,0:T(8,128)S(1)}, f32[32,128]{1,0:T(8,128)S(1)}, u32[]{:S(2)}, u32[]{:S(2)}) collective-permute-start(f32[32,128]{1,0:T(8,128)S(1)} %get-tuple-element.25.refs_0_), channel_id=1, source_target_pairs={{0,8},{8,0},{16,24},{24,16},{1,9},{9,1},{17,25},{25,17},{2,10},{10... | collective-permute-start | bytes 49160 | tf_op jit(solution)/shard_map/ppermute | solution.py:30
  44.5 1.1 %collective-permute-done.17.refs_3_ = f32[32,128]{1,0:T(8,128)S(1)} collective-permute-done((f32[32,128]{1,0:T(8,128)S(1)}, f32[32,128]{1,0:T(8,128)S(1)}, u32[]{:S(2)}, u32[]{:S(2)}) %collective-permute-start.17) | collective-permute-done | bytes 16416 | tf_op jit(solution)/shard_map/ppermute | solution.py:30
  45.6 0.2 collective-permute-done.16.refs_2_
  45.8 0.9 %collective-permute-done.15.refs_1_ = f32[32,128]{1,0:T(8,128)S(1)} collective-permute-done((f32[32,128]{1,0:T(8,128)S(1)}, f32[32,128]{1,0:T(8,128)S(1)}, u32[]{:S(2)}, u32[]{:S(2)}) %collective-permute-start.15) | collective-permute-done | bytes 16416 | tf_op jit(solution)/shard_map/ppermute | solution.py:30
  46.7 5.1 %gradient.1 = (bf16[4,144,256]{2,1,0:T(8,128)(2,1)S(1)}, bf16[4,144,256]{2,1,0:T(8,128)(2,1)S(1)}) custom-call(f32[32,128]{1,0:T(8,128)S(1)} %get-tuple-element.25.refs_0_, f32[32,128]{1,0:T(8,128)S(1)} %collective-permute-done.15.refs_1_, f32[32,128]{1,0:T(8,128)S(1)} %collective-permute-done.16.refs_2_, f32[32,128]{1,0:T(8,128)S(1)} %collective-permute-done.17.refs_3_, ...), custom_call_target="tpu_custom_call" | custom-call | tf_op jit(solution)/shard_map/gradient/pallas_call | solution.py:369
  52.0 1.6 %collective-permute-done.18.received = bf16[4,144,256]{2,1,0:T(8,128)(2,1)S(1)} collective-permute-done((bf16[4,144,256]{2,1,0:T(8,128)(2,1)S(1)}, bf16[4,144,256]{2,1,0:T(8,128)(2,1)S(1)}, u32[]{:S(2)}, u32[]{:S(2)}) %collective-permute-start.18) | collective-permute-done | bytes 294944 | tf_op jit(solution)/shard_map/ppermute | solution.py:25
  53.5 0.1 core_sum.1
  53.6 0.2 collective-permute-start.19
  53.8 3.2 %collective-permute-start.20 = (bf16[144,256]{1,0:T(8,128)(2,1)S(1)}, bf16[144,256]{1,0:T(8,128)(2,1)S(1)}, u32[]{:S(2)}, u32[]{:S(2)}) collective-permute-start(bf16[144,256]{1,0:T(8,128)(2,1)S(1)} %get-tuple-element.34), channel_id=1, source_target_pairs={{0,4},{1,5},{2,6},{3,7},{4,0},{5,1},{6,2},{7,3},{8,12},{9,13},{10,... | collective-permute-start | bytes 221192 | tf_op jit(solution)/shard_map/ppermute | solution.py:20
  57.0 1.7 %collective-permute-start.21 = (bf16[144,256]{1,0:T(8,128)(2,1)S(1)}, bf16[144,256]{1,0:T(8,128)(2,1)S(1)}, u32[]{:S(2)}, u32[]{:S(2)}) collective-permute-start(bf16[144,256]{1,0:T(8,128)(2,1)S(1)} %get-tuple-element.35), channel_id=1, source_target_pairs={{0,6},{1,7},{2,0},{3,1},{4,2},{5,3},{6,4},{7,5},{8,14},{9,15},{10,... | collective-permute-start | bytes 221192 | tf_op jit(solution)/shard_map/ppermute | solution.py:20
  58.7 1.9 %collective-permute-done.19.refs_1_ = bf16[144,256]{1,0:T(8,128)(2,1)S(1)} collective-permute-done((bf16[144,256]{1,0:T(8,128)(2,1)S(1)}, bf16[144,256]{1,0:T(8,128)(2,1)S(1)}, u32[]{:S(2)}, u32[]{:S(2)}) %collective-permute-start.19) | collective-permute-done | bytes 73760 | tf_op jit(solution)/shard_map/ppermute | solution.py:20
  60.6 2.4 %collective-permute-done.20.refs_2_ = bf16[144,256]{1,0:T(8,128)(2,1)S(1)} collective-permute-done((bf16[144,256]{1,0:T(8,128)(2,1)S(1)}, bf16[144,256]{1,0:T(8,128)(2,1)S(1)}, u32[]{:S(2)}, u32[]{:S(2)}) %collective-permute-start.20) | collective-permute-done | bytes 73760 | tf_op jit(solution)/shard_map/ppermute | solution.py:20
  63.1 1.5 %collective-permute-start.24 = (bf16[144,256]{1,0:T(8,128)(2,1)S(1)}, bf16[144,256]{1,0:T(8,128)(2,1)S(1)}, u32[]{:S(2)}, u32[]{:S(2)}) collective-permute-start(bf16[144,256]{1,0:T(8,128)(2,1)S(1)} %z_sum.1.refs_0_), channel_id=1, source_target_pairs={{0,24},{8,16},{16,8},{24,0},{1,25},{9,17},{17,9},{25,1},{2,26},{10... | collective-permute-start | bytes 221192 | tf_op jit(solution)/shard_map/ppermute | solution.py:30
  64.5 1.5 %collective-permute-start.23 = (bf16[144,256]{1,0:T(8,128)(2,1)S(1)}, bf16[144,256]{1,0:T(8,128)(2,1)S(1)}, u32[]{:S(2)}, u32[]{:S(2)}) collective-permute-start(bf16[144,256]{1,0:T(8,128)(2,1)S(1)} %z_sum.1.refs_0_), channel_id=1, source_target_pairs={{0,16},{8,24},{16,0},{24,8},{1,17},{9,25},{17,1},{25,9},{2,18},{10... | collective-permute-start | bytes 221192 | tf_op jit(solution)/shard_map/ppermute | solution.py:30
  66.1 0.5 collective-permute-start.22
  66.6 1.8 %collective-permute-done.24.refs_3_ = bf16[144,256]{1,0:T(8,128)(2,1)S(1)} collective-permute-done((bf16[144,256]{1,0:T(8,128)(2,1)S(1)}, bf16[144,256]{1,0:T(8,128)(2,1)S(1)}, u32[]{:S(2)}, u32[]{:S(2)}) %collective-permute-start.24) | collective-permute-done | bytes 73760 | tf_op jit(solution)/shard_map/ppermute | solution.py:30
  68.4 0.8 %collective-permute-done.23.refs_2_ = bf16[144,256]{1,0:T(8,128)(2,1)S(1)} collective-permute-done((bf16[144,256]{1,0:T(8,128)(2,1)S(1)}, bf16[144,256]{1,0:T(8,128)(2,1)S(1)}, u32[]{:S(2)}, u32[]{:S(2)}) %collective-permute-start.23) | collective-permute-done | bytes 73760 | tf_op jit(solution)/shard_map/ppermute | solution.py:30
  69.2 1.2 %collective-permute-done.22.refs_1_ = bf16[144,256]{1,0:T(8,128)(2,1)S(1)} collective-permute-done((bf16[144,256]{1,0:T(8,128)(2,1)S(1)}, bf16[144,256]{1,0:T(8,128)(2,1)S(1)}, u32[]{:S(2)}, u32[]{:S(2)}) %collective-permute-start.22) | collective-permute-done | bytes 73760 | tf_op jit(solution)/shard_map/ppermute | solution.py:30
  70.4 0.9 %finish.1 = (f32[128,1024]{1,0:T(8,128)}, f32[1,1024]{1,0:T(1,128)}, f32[1,1]{1,0:T(1,128)}) custom-call(bf16[144,256]{1,0:T(8,128)(2,1)S(1)} %z_sum.1.refs_0_, bf16[144,256]{1,0:T(8,128)(2,1)S(1)} %collective-permute-done.22.refs_1_, bf16[144,256]{1,0:T(8,128)(2,1)S(1)} %collective-permute-done.23.refs_2_, bf16[144,256]{1,0:T(8,128)(2,1)S(1)} %collective-permute-done.24.refs_3_), custom_call_target="tpu_custom_call" | custom-call | tf_op jit(solution)/shard_map/finish/pallas_call | solution.py:410
  (39 shorter events, 0.4 us)
Async XLA Ops:
  0.6 5.1 %copy-start = (bf16[1024,512]{1,0:T(8,128)(2,1)S(1)}, bf16[1024,512]{1,0:T(8,128)(2,1)}, u32[]{:S(2)}) copy-start(bf16[1024,512]{1,0:T(8,128)(2,1)} %param.9) | copy-start | bytes 3145732
  1.7 12.9 %collective-permute-start.1 = (bf16[128,256]{1,0:T(8,128)(2,1)S(1)}, bf16[128,256]{1,0:T(8,128)(2,1)S(1)}, u32[]{:S(2)}, u32[]{:S(2)}) collective-permute-start(bf16[128,256]{1,0:T(8,128)(2,1)S(1)} %get-tuple-element.21), channel_id=1, source_target_pairs={{0,4},{1,5},{2,6},{3,7},{4,0},{5,1},{6,2},{7,3},{8,12},{9,13},{10,... | collective-permute-start | bytes 196616 | tf_op jit(solution)/shard_map/ppermute | solution.py:20
  6.9 7.7 %collective-permute-start.2 = (bf16[160,256]{1,0:T(8,128)(2,1)S(1)}, bf16[160,256]{1,0:T(8,128)(2,1)S(1)}, u32[]{:S(2)}, u32[]{:S(2)}) collective-permute-start(bf16[160,256]{1,0:T(8,128)(2,1)S(1)} %pad_maximum_fusion.3), channel_id=1, source_target_pairs={{0,6},{1,7},{2,0},{3,1},{4,2},{5,3},{6,4},{7,5},{8,14},{9,15},{10,... | collective-permute-start | bytes 245768 | tf_op jit(solution)/shard_map/ppermute | solution.py:20
  8.3 6.2 %collective-permute-start = (bf16[160,256]{1,0:T(8,128)(2,1)S(1)}, bf16[160,256]{1,0:T(8,128)(2,1)S(1)}, u32[]{:S(2)}, u32[]{:S(2)}) collective-permute-start(bf16[160,256]{1,0:T(8,128)(2,1)S(1)} %pad_maximum_fusion.3), channel_id=1, source_target_pairs={{0,2},{1,3},{2,4},{3,5},{4,6},{5,7},{6,0},{7,1},{8,10},{9,11},{10,... | collective-permute-start | bytes 245768 | tf_op jit(solution)/shard_map/ppermute | solution.py:20
  14.8 3.2 %collective-permute-start.3 = (bf16[496,256]{1,0:T(8,128)(2,1)S(1)}, bf16[496,256]{1,0:T(8,128)(2,1)S(1)}, u32[]{:S(2)}, u32[]{:S(2)}) collective-permute-start(bf16[496,256]{1,0:T(8,128)(2,1)S(1)} %constant_dynamic-update-slice_fusion.refs_2_), channel_id=1, source_target_pairs={{0,1},{1,0},{2,3},{3,2},{4,5},{5,4},{6,7},{7,6},{8,9},{9,8},{10,11... | collective-permute-start | bytes 761864 | tf_op jit(solution)/shard_map/ppermute | solution.py:25
  14.9 14.7 %collective-permute-start.8 = (bf16[496,256]{1,0:T(8,128)(2,1)S(1)}, bf16[496,256]{1,0:T(8,128)(2,1)S(1)}, u32[]{:S(2)}, u32[]{:S(2)}) collective-permute-start(bf16[496,256]{1,0:T(8,128)(2,1)S(1)} %constant_dynamic-update-slice_fusion.refs_2_), channel_id=1, source_target_pairs={{0,16},{8,24},{16,0},{24,8},{1,17},{9,25},{17,1},{25,9},{2,18},{10... | collective-permute-start | bytes 761864 | tf_op jit(solution)/shard_map/ppermute | solution.py:30
  16.5 13.2 %collective-permute-start.7 = (bf16[496,256]{1,0:T(8,128)(2,1)S(1)}, bf16[496,256]{1,0:T(8,128)(2,1)S(1)}, u32[]{:S(2)}, u32[]{:S(2)}) collective-permute-start(bf16[496,256]{1,0:T(8,128)(2,1)S(1)} %constant_dynamic-update-slice_fusion.refs_2_), channel_id=1, source_target_pairs={{0,8},{8,0},{16,24},{24,16},{1,9},{9,1},{17,25},{25,17},{2,10},{10... | collective-permute-start | bytes 761864 | tf_op jit(solution)/shard_map/ppermute | solution.py:30
  18.0 4.7 %collective-permute-start.6 = (bf16[192,256]{1,0:T(8,128)(2,1)S(1)}, bf16[192,256]{1,0:T(8,128)(2,1)S(1)}, u32[]{:S(2)}, u32[]{:S(2)}) collective-permute-start(bf16[192,256]{1,0:T(8,128)(2,1)S(1)} %pad_maximum_fusion.2), channel_id=1, source_target_pairs={{0,6},{1,7},{2,0},{3,1},{4,2},{5,3},{6,4},{7,5},{8,14},{9,15},{10,... | collective-permute-start | bytes 294920 | tf_op jit(solution)/shard_map/ppermute | solution.py:20
  19.5 9.4 %collective-permute-start.5 = (bf16[192,256]{1,0:T(8,128)(2,1)S(1)}, bf16[192,256]{1,0:T(8,128)(2,1)S(1)}, u32[]{:S(2)}, u32[]{:S(2)}) collective-permute-start(bf16[192,256]{1,0:T(8,128)(2,1)S(1)} %pad_maximum_fusion.2), channel_id=1, source_target_pairs={{0,4},{1,5},{2,6},{3,7},{4,0},{5,1},{6,2},{7,3},{8,12},{9,13},{10,... | collective-permute-start | bytes 294920 | tf_op jit(solution)/shard_map/ppermute | solution.py:20
  19.5 9.4 %collective-permute-start.4 = (bf16[192,256]{1,0:T(8,128)(2,1)S(1)}, bf16[192,256]{1,0:T(8,128)(2,1)S(1)}, u32[]{:S(2)}, u32[]{:S(2)}) collective-permute-start(bf16[192,256]{1,0:T(8,128)(2,1)S(1)} %pad_maximum_fusion.2), channel_id=1, source_target_pairs={{0,2},{1,3},{2,4},{3,5},{4,6},{5,7},{6,0},{7,1},{8,10},{9,11},{10,... | collective-permute-start | bytes 294920 | tf_op jit(solution)/shard_map/ppermute | solution.py:20
  22.7 7.4 %collective-permute-start.9 = (bf16[304,256]{1,0:T(8,128)(2,1)S(1)}, bf16[304,256]{1,0:T(8,128)(2,1)}, u32[]{:S(2)}, u32[]{:S(2)}) collective-permute-start(bf16[304,256]{1,0:T(8,128)(2,1)S(1)} %get-tuple-element.63), channel_id=1, source_target_pairs={{0,24},{8,16},{16,8},{24,0},{1,25},{9,17},{17,9},{25,1},{2,26},{10... | collective-permute-start | bytes 466952 | tf_op jit(solution)/shard_map/ppermute | solution.py:30
  29.0 3.3 %collective-permute-start.11 = (bf16[704,256]{1,0:T(8,128)(2,1)S(1)}, bf16[704,256]{1,0:T(8,128)(2,1)S(1)}, u32[]{:S(2)}, u32[]{:S(2)}) collective-permute-start(bf16[704,256]{1,0:T(8,128)(2,1)S(1)} %pad_maximum_fusion.refs_1_), channel_id=1, source_target_pairs={{0,1},{1,0},{2,3},{3,2},{4,5},{5,4},{6,7},{7,6},{8,9},{9,8},{10,11... | collective-permute-start | bytes 1081352 | tf_op jit(solution)/shard_map/ppermute | solution.py:25
  29.1 2.1 %collective-permute-start.10 = (bf16[4,128,256]{2,1,0:T(8,128)(2,1)S(1)}, bf16[4,128,256]{2,1,0:T(8,128)(2,1)S(1)}, u32[]{:S(2)}, u32[]{:S(2)}) collective-permute-start(bf16[4,128,256]{2,1,0:T(8,128)(2,1)S(1)} %pad_maximum_fusion.1.refs_0_), channel_id=1, source_target_pairs={{0,1},{1,0},{2,3},{3,2},{4,5},{5,4},{6,7},{7,6},{8,9},{9,8},{10,11... | collective-permute-start | bytes 786440 | tf_op jit(solution)/shard_map/ppermute | solution.py:25
  29.6 2.6 %collective-permute-start.13 = (bf16[496,256]{1,0:T(8,128)(2,1)S(1)}, bf16[496,256]{1,0:T(8,128)(2,1)}, u32[]{:S(2)}, u32[]{:S(2)}) collective-permute-start(bf16[496,256]{1,0:T(8,128)(2,1)S(1)} %collective-permute-done.8.refs_4_), channel_id=1, source_target_pairs={{0,1},{1,0},{2,3},{3,2},{4,5},{5,4},{6,7},{7,6},{8,9},{9,8},{10,11... | collective-permute-start | bytes 761864 | tf_op jit(solution)/shard_map/ppermute | solution.py:25
  29.7 2.5 %collective-permute-start.12 = (bf16[496,256]{1,0:T(8,128)(2,1)S(1)}, bf16[496,256]{1,0:T(8,128)(2,1)}, u32[]{:S(2)}, u32[]{:S(2)}) collective-permute-start(bf16[496,256]{1,0:T(8,128)(2,1)S(1)} %collective-permute-done.7.refs_3_), channel_id=1, source_target_pairs={{0,1},{1,0},{2,3},{3,2},{4,5},{5,4},{6,7},{7,6},{8,9},{9,8},{10,11... | collective-permute-start | bytes 761864 | tf_op jit(solution)/shard_map/ppermute | solution.py:25
  30.2 2.1 %collective-permute-start.14 = (bf16[304,256]{1,0:T(8,128)(2,1)}, bf16[304,256]{1,0:T(8,128)(2,1)}, u32[]{:S(2)}, u32[]{:S(2)}) collective-permute-start(bf16[304,256]{1,0:T(8,128)(2,1)} %collective-permute-done.9.refs_5_), channel_id=1, source_target_pairs={{0,1},{1,0},{2,3},{3,2},{4,5},{5,4},{6,7},{7,6},{8,9},{9,8},{10,11... | collective-permute-start | bytes 466952 | tf_op jit(solution)/shard_map/ppermute | solution.py:25
  40.9 4.7 %collective-permute-start.17 = (f32[32,128]{1,0:T(8,128)S(1)}, f32[32,128]{1,0:T(8,128)S(1)}, u32[]{:S(2)}, u32[]{:S(2)}) collective-permute-start(f32[32,128]{1,0:T(8,128)S(1)} %get-tuple-element.25.refs_0_), channel_id=1, source_target_pairs={{0,24},{8,16},{16,8},{24,0},{1,25},{9,17},{17,9},{25,1},{2,26},{10... | collective-permute-start | bytes 49160 | tf_op jit(solution)/shard_map/ppermute | solution.py:30
  42.1 3.8 %collective-permute-start.16 = (f32[32,128]{1,0:T(8,128)S(1)}, f32[32,128]{1,0:T(8,128)S(1)}, u32[]{:S(2)}, u32[]{:S(2)}) collective-permute-start(f32[32,128]{1,0:T(8,128)S(1)} %get-tuple-element.25.refs_0_), channel_id=1, source_target_pairs={{0,16},{8,24},{16,0},{24,8},{1,17},{9,25},{17,1},{25,9},{2,18},{10... | collective-permute-start | bytes 49160 | tf_op jit(solution)/shard_map/ppermute | solution.py:30
  43.0 3.7 %collective-permute-start.15 = (f32[32,128]{1,0:T(8,128)S(1)}, f32[32,128]{1,0:T(8,128)S(1)}, u32[]{:S(2)}, u32[]{:S(2)}) collective-permute-start(f32[32,128]{1,0:T(8,128)S(1)} %get-tuple-element.25.refs_0_), channel_id=1, source_target_pairs={{0,8},{8,0},{16,24},{24,16},{1,9},{9,1},{17,25},{25,17},{2,10},{10... | collective-permute-start | bytes 49160 | tf_op jit(solution)/shard_map/ppermute | solution.py:30
  51.9 1.6 %collective-permute-start.18 = (bf16[4,144,256]{2,1,0:T(8,128)(2,1)S(1)}, bf16[4,144,256]{2,1,0:T(8,128)(2,1)S(1)}, u32[]{:S(2)}, u32[]{:S(2)}) collective-permute-start(bf16[4,144,256]{2,1,0:T(8,128)(2,1)S(1)} %get-tuple-element.31), channel_id=1, source_target_pairs={{0,1},{1,0},{2,3},{3,2},{4,5},{5,4},{6,7},{7,6},{8,9},{9,8},{10,11... | collective-permute-start | bytes 884744 | tf_op jit(solution)/shard_map/ppermute | solution.py:25
  53.6 7.0 %collective-permute-start.19 = (bf16[144,256]{1,0:T(8,128)(2,1)S(1)}, bf16[144,256]{1,0:T(8,128)(2,1)S(1)}, u32[]{:S(2)}, u32[]{:S(2)}) collective-permute-start(bf16[144,256]{1,0:T(8,128)(2,1)S(1)} %get-tuple-element.33), channel_id=1, source_target_pairs={{0,2},{1,3},{2,4},{3,5},{4,6},{5,7},{6,0},{7,1},{8,10},{9,11},{10,... | collective-permute-start | bytes 221192 | tf_op jit(solution)/shard_map/ppermute | solution.py:20
  53.8 9.2 %collective-permute-start.20 = (bf16[144,256]{1,0:T(8,128)(2,1)S(1)}, bf16[144,256]{1,0:T(8,128)(2,1)S(1)}, u32[]{:S(2)}, u32[]{:S(2)}) collective-permute-start(bf16[144,256]{1,0:T(8,128)(2,1)S(1)} %get-tuple-element.34), channel_id=1, source_target_pairs={{0,4},{1,5},{2,6},{3,7},{4,0},{5,1},{6,2},{7,3},{8,12},{9,13},{10,... | collective-permute-start | bytes 221192 | tf_op jit(solution)/shard_map/ppermute | solution.py:20
  57.0 6.0 %collective-permute-start.21 = (bf16[144,256]{1,0:T(8,128)(2,1)S(1)}, bf16[144,256]{1,0:T(8,128)(2,1)S(1)}, u32[]{:S(2)}, u32[]{:S(2)}) collective-permute-start(bf16[144,256]{1,0:T(8,128)(2,1)S(1)} %get-tuple-element.35), channel_id=1, source_target_pairs={{0,6},{1,7},{2,0},{3,1},{4,2},{5,3},{6,4},{7,5},{8,14},{9,15},{10,... | collective-permute-start | bytes 221192 | tf_op jit(solution)/shard_map/ppermute | solution.py:20
  63.1 5.4 %collective-permute-start.24 = (bf16[144,256]{1,0:T(8,128)(2,1)S(1)}, bf16[144,256]{1,0:T(8,128)(2,1)S(1)}, u32[]{:S(2)}, u32[]{:S(2)}) collective-permute-start(bf16[144,256]{1,0:T(8,128)(2,1)S(1)} %z_sum.1.refs_0_), channel_id=1, source_target_pairs={{0,24},{8,16},{16,8},{24,0},{1,25},{9,17},{17,9},{25,1},{2,26},{10... | collective-permute-start | bytes 221192 | tf_op jit(solution)/shard_map/ppermute | solution.py:30
  64.5 4.6 %collective-permute-start.23 = (bf16[144,256]{1,0:T(8,128)(2,1)S(1)}, bf16[144,256]{1,0:T(8,128)(2,1)S(1)}, u32[]{:S(2)}, u32[]{:S(2)}) collective-permute-start(bf16[144,256]{1,0:T(8,128)(2,1)S(1)} %z_sum.1.refs_0_), channel_id=1, source_target_pairs={{0,16},{8,24},{16,0},{24,8},{1,17},{9,25},{17,1},{25,9},{2,18},{10... | collective-permute-start | bytes 221192 | tf_op jit(solution)/shard_map/ppermute | solution.py:30
  66.1 4.4 %collective-permute-start.22 = (bf16[144,256]{1,0:T(8,128)(2,1)S(1)}, bf16[144,256]{1,0:T(8,128)(2,1)S(1)}, u32[]{:S(2)}, u32[]{:S(2)}) collective-permute-start(bf16[144,256]{1,0:T(8,128)(2,1)S(1)} %z_sum.1.refs_0_), channel_id=1, source_target_pairs={{0,8},{8,0},{16,24},{24,16},{1,9},{9,1},{17,25},{25,17},{2,10},{10... | collective-permute-start | bytes 221192 | tf_op jit(solution)/shard_map/ppermute | solution.py:30

commit v2 on v1

--- a/solution.py
+++ b/solution.py
@@ -17,7 +17,11 @@
 
 def along_z(array, by):
     devices = lax.axis_size("shard")
-    return lax.ppermute(array, "shard", [(i, (i + 2 * by) % devices) for i in range(devices)])
+    return lax.ppermute(array, "shard", [(i, i ^ (2 * by)) for i in range(devices)])
+
+
+def next_steps(n_z):
+    return [j for j in range(1, n_z) if j & (j + 1) == 0]
 
 
 def swap_core(array):
@@ -80,7 +84,8 @@
     def assemble():
         raw_cut = mine[0].shape[1] // 2
         dest_rows = (n_z - 1) * raw_cut
-        feat_rows = 3 * parts * blk
+        steps = next_steps(n_z)
+        feat_rows = (1 + len(steps)) * parts * blk
         slot_row = dest_rows + feat_rows
         slot_rows = blk if cols >= 2 * slots else 2 * blk
         anchor_base = slot_row + slot_rows
@@ -88,7 +93,7 @@
             raw, mids, planes = source[0], source[1], source[2:]
             rows_mid = hidden // (2 * n_z)
             for j in range(n_z):
-                shard_at = 2 * lax.rem(z - j + n_z, n_z) + core_at
+                shard_at = 2 * (z ^ j) + core_at
                 at = pl.ds(pl.multiple_of(shard_at * raw_cut, raw_cut), raw_cut)
                 mid = rows_mid + (j - 1) * (rows_mid + raw_cut) if j > 0 else 0
                 w_mid[unit_rows(shard_at, rows_mid, cols, region), :] = mids[mid : mid + rows_mid, :]
@@ -106,11 +111,13 @@
         one = identity(cols)
         w_mid_t[...] = turned(one, w_mid[...])
         left = lax.broadcasted_iota(jnp.int32, (lines, 128), 1) < slots
+        below_at = sum(jnp.where((z ^ (z - 1)) >= j, 1, 0) for j in steps)
+        above_at = sum(jnp.where((z ^ (z + 1)) >= j, 1, 0) for j in steps)
         for i in range(n_region):
             near, far = mine[2 + i], other[2 + i]
             for t in range(parts):
                 below, here, above = (
-                    slice(dest_rows + (k * parts + t) * blk, dest_rows + (k * parts + t + 1) * blk) for k in range(3)
+                    pl.ds(pl.multiple_of(dest_rows + (k * parts + t) * blk, blk), blk) for k in (below_at, 0, above_at)
                 )
                 lanes = slice(t * cols, (t + 1) * cols)
                 before = jnp.where(core == 0, far[below, :], far[here, :])
@@ -144,34 +151,80 @@
     group = 8
     pairs = group * slots
     spread = pairs // 128
-    chosen = ids[step]
-    lookup = tables[step]
     dest_row = lax.broadcasted_iota(jnp.int32, (2 * window, pairs), 0)
     dest_row = jnp.where(dest_row >= window, dest_row - window, dest_row).astype(F32)
     anchor_row = lax.broadcasted_iota(jnp.int32, (2 * blk, pairs), 0)
     anchor_row = jnp.where(anchor_row >= blk, anchor_row - blk, anchor_row)
     anchor_lane = lax.broadcasted_iota(jnp.int32, (2 * blk, pairs), 1) // slots
     weight = w_out[...]
-    for c in range(blk // group):
-        at = slice(c * pairs, (c + 1) * pairs)
-        spot = jnp.concatenate([chosen[c * spread + k : c * spread + k + 1, :] for k in range(spread)], axis=1)
-        dest_hot = jnp.where(dest_row == spot, 1.0, 0.0)
-        anchor_hot = jnp.where(anchor_row == anchor_lane + c * group, 1.0, 0.0)
-        onehot = jnp.concatenate([dest_hot, anchor_hot], axis=0).astype(BF)
-        first = jnp.maximum(jnp.dot(lookup, onehot, preferred_element_type=F32).astype(BF), 0)
-        first_out[:, at] = first
-        active = jnp.maximum(jnp.dot(w_mid_t[...], first, preferred_element_type=F32), 0.0)
-        act_out[:, at] = active.astype(BF)
-        score = jnp.sum(active * weight, axis=0, keepdims=True)
-        for k in range(spread):
-            score_out[c * spread + k : c * spread + k + 1, :] = score[:, k * 128 : (k + 1) * 128]
-
-
-def grad_kernel(n_region, n_z, slots, *refs):
+    for n in range(first_out.shape[1] // (blk * slots)):
+        chosen = ids[step + n]
+        lookup = tables[step + n]
+        for c in range(blk // group):
+            spot = jnp.concatenate([chosen[c * spread + k : c * spread + k + 1, :] for k in range(spread)], axis=1)
+            dest_hot = jnp.where(dest_row == spot, 1.0, 0.0)
+            anchor_hot = jnp.where(anchor_row == anchor_lane + c * group, 1.0, 0.0)
+            onehot = jnp.concatenate([dest_hot, anchor_hot], axis=0).astype(BF)
+            first = jnp.maximum(jnp.dot(lookup, onehot, preferred_element_type=F32).astype(BF), 0)
+            at = slice(n * blk * slots + c * pairs, n * blk * slots + (c + 1) * pairs)
+            first_out[:, at] = first
+            active = jnp.maximum(jnp.dot(w_mid_t[...], first, preferred_element_type=F32), 0.0)
+            act_out[:, at] = active.astype(BF)
+            score = jnp.sum(active * weight, axis=0, keepdims=True)
+            for k in range(spread):
+                row = n * lines + c * spread + k
+                score_out[row : row + 1, :] = score[:, k * 128 : (k + 1) * 128]
+
+
+def target_rows(first, targets, rows, cols):
+    z = lax.axis_index("shard") // 2
+    region = lax.axis_index("region")
+    return jnp.concatenate(
+        [first[unit_rows(z ^ j, 2 * rows, cols, region), :] for j in targets], axis=0
+    )
+
+
+def put_blocks(grad, tail, keep, send):
+    rows = keep.shape[1] - TAIL
+    core = lax.axis_index("shard") % 2
+    for n in range(keep.shape[0]):
+        for target, core_at in ((keep, core), (send, 1 - core)):
+            at = pl.ds(pl.multiple_of((2 * n + core_at) * rows, rows), rows)
+            target[n, :rows, :] = grad[at, :].astype(BF)
+            target[n, rows:, :] = tail
+
+
+def rest_kernel(targets, *refs):
+    first, pre, tail, keep, send, grad = refs
+    rows = keep.shape[1] - TAIL
+    step = pl.program_id(0)
+    part = lax.dot_general(
+        target_rows(first, targets, rows, pre.shape[0]),
+        pre[...],
+        (((1,), (1,)), ((), ())),
+        preferred_element_type=F32,
+    )
+
+    @pl.when(step == 0)
+    def begin():
+        grad[...] = part
+
+    @pl.when(step > 0)
+    def more():
+        grad[...] += part
+
+    @pl.when(step == pl.num_programs(0) - 1)
+    def finish():
+        put_blocks(grad, tail[...], keep, send)
+
+
+def grad_kernel(n_region, targets, slots, *refs):
     scores, rest = refs[:n_region], refs[n_region:]
-    ids, flows, first, act, w_out, keep, send, grad, gout, sums = rest
+    ids, flows, first, act, w_out, pre_out, tail_out, keep, send, grad, gout, sums = rest
     step = pl.program_id(0)
     cols = act.shape[0]
+    rows = keep.shape[1] - TAIL
+    lines, lanes = ids.shape[1:]
 
     @pl.when(step == 0)
     def clear():
@@ -179,41 +232,46 @@
         gout[...] = jnp.zeros_like(gout)
         sums[...] = jnp.zeros_like(sums)
 
-    score = scores[0][...]
-    for other in scores[1:]:
-        score = score + other[...]
-    valid = ids[step] >= 0
-    left = lax.broadcasted_iota(jnp.int32, score.shape, 1) < slots
+    left = lax.broadcasted_iota(jnp.int32, (lines, lanes), 1) < slots
 
     def halves(reduce, value, rest):
         low = reduce(jnp.where(left, value, rest), axis=1, keepdims=True)
         high = reduce(jnp.where(left, rest, value), axis=1, keepdims=True)
         return jnp.where(left, low, high)
 
-    top = halves(jnp.max, jnp.where(valid, score, -jnp.inf), -jnp.inf)
-    expo = jnp.where(valid, jnp.exp(score - top), 0.0)
-    mass = halves(jnp.sum, expo, 0.0)
-    probs = expo / mass
-    logp = score - top - jnp.log(mass)
-    flow = flows[step]
-    anchor_total = halves(jnp.sum, flow, 0.0)
-    sgrad = jnp.where(valid, probs * anchor_total - flow, 0.0)
-    sums[0] += flow
-    sums[1] -= jnp.where(valid, flow * logp, 0.0)
-
-    lanes = score.shape[1]
     weight = jnp.broadcast_to(w_out[...], (cols, lanes))
-    pre = []
-    for q in range(score.shape[0]):
-        line = sgrad[q : q + 1, :]
-        active = act[:, q * lanes : (q + 1) * lanes].astype(F32)
-        gained = active * line if q == 0 else gained + active * line
-        pre.append(jnp.where(active > 0, weight * line, 0.0).astype(BF))
-    gout[...] += gained
-    pre = jnp.concatenate(pre, axis=1)
-    grad[...] += lax.dot_general(first[...], pre, (((1,), (1,)), ((), ())), preferred_element_type=F32)
-
-    @pl.when(step == n_region - 1)
+    gained = gout[...]
+    trips, numer = sums[0], sums[1]
+    for n in range(act.shape[1] // (lines * lanes)):
+        score = scores[0][n * lines : (n + 1) * lines, :]
+        for k in range(1, n_region):
+            at = (n ^ k) * lines if scores[k].shape[0] > lines else 0
+            score = score + scores[k][at : at + lines, :]
+        valid = ids[step + n] >= 0
+        top = halves(jnp.max, jnp.where(valid, score, -jnp.inf), -jnp.inf)
+        expo = jnp.where(valid, jnp.exp(score - top), 0.0)
+        mass = halves(jnp.sum, expo, 0.0)
+        probs = expo / mass
+        logp = score - top - jnp.log(mass)
+        flow = flows[step + n]
+        anchor_total = halves(jnp.sum, flow, 0.0)
+        sgrad = jnp.where(valid, probs * anchor_total - flow, 0.0)
+        trips = trips + flow
+        numer = numer - jnp.where(valid, flow * logp, 0.0)
+        for q in range(lines):
+            line = sgrad[q : q + 1, :]
+            at = slice((n * lines + q) * lanes, (n * lines + q + 1) * lanes)
+            active = act[:, at].astype(F32)
+            gained = gained + active * line
+            pre_out[:, at] = jnp.where(active > 0, weight * line, 0.0).astype(BF)
+    gout[...] = gained
+    sums[0] = trips
+    sums[1] = numer
+    grad[...] += lax.dot_general(
+        target_rows(first, targets, rows, cols), pre_out[...], (((1,), (1,)), ((), ())), preferred_element_type=F32
+    )
+
+    @pl.when(step == pl.num_programs(0) - 1)
     def finish():
         out = jnp.sum(gout[...].T, axis=0, keepdims=True)
         total = jnp.sum(sums[0])
@@ -222,15 +280,8 @@
         lane = lax.broadcasted_iota(jnp.int32, (8, cols), 1)
         stats = jnp.where(lane == 0, total, jnp.where(lane == 1, numer, 0.0))
         tail = pack_tail(jnp.where(row == 0, out, jnp.where(row == 1, stats, 0.0)))
-        rows = keep.shape[1] - TAIL
-        region = lax.axis_index("region")
-        shard = lax.axis_index("shard")
-        z, core = shard // 2, shard % 2
-        for j in range(n_z):
-            z_at = lax.rem(z + j, n_z)
-            for target, core_at in ((keep, core), (send, 1 - core)):
-                target[j, :rows, :] = grad[unit_rows(2 * z_at + core_at, rows, cols, region), :].astype(BF)
-                target[j, rows:, :] = tail
+        tail_out[...] = tail
+        put_blocks(grad, tail, keep, send)
 
 
 def core_sum_kernel(keep, received, *outs):
@@ -240,7 +291,7 @@
         out[rows:, :] = pack_tail(unpack_tail(keep[j, rows:, :]) + unpack_tail(received[j, rows:, :]))
 
 
-def z_sum_kernel(*refs):
+def z_sum_kernel(steps, *refs):
     blocks, (out, tails) = refs[:-2], refs[-2:]
     n_z = len(blocks)
     rows = out.shape[0] - TAIL
@@ -248,12 +299,12 @@
     for block in blocks[1:]:
         total = total + block[:rows, :].astype(F32)
     out[:rows, :] = total.astype(BF)
-    for j, block in enumerate(blocks):
+    for j, block in zip(steps, blocks):
         tails[j] = unpack_tail(block[rows:, :])
     z = lax.axis_index("shard") // 2
     tail = tails[z]
     for z_at in range(1, n_z):
-        tail = tail + tails[lax.rem(z - z_at + n_z, n_z)]
+        tail = tail + tails[z ^ z_at]
     out[rows:, :] = pack_tail(tail)
 
 
@@ -297,9 +348,9 @@
     def along_rows(features):
         return [features[:, t * cols : (t + 1) * cols] for t in range(depth // cols)]
 
-    raw = jnp.stack([jnp.concatenate([cut(w_anchor, i), cut(w_dest, i)], axis=0) for i in range(n_region)])
     piece = jnp.concatenate([cut(w_anchor, 0), cut(w_dest, 0)], axis=0)
 
+    last_cols = cut(w_anchor, n_region - 1)
     piece, tile_block = lax.optimization_barrier((piece, tile_block))
     onehot = (tile_block[None, :] == jnp.arange(blk, dtype=jnp.int32)[:, None]).astype(BF)
     sums = jnp.dot(onehot, tiles, preferred_element_type=F32)
@@ -307,7 +358,14 @@
     features = jnp.concatenate(along_rows((sums * scale).astype(BF)), axis=0)
 
     payload = jnp.concatenate([piece, features], axis=0)
-    from_z = [along_z(payload if j in (1, n_z - 1) else piece, j) for j in range(1, n_z)]
+    from_z = [along_z(payload if j in next_steps(n_z) else piece, j) for j in range(1, n_z)]
+    w_anchor, w_dest, w_out, w_hidden, payload = lax.optimization_barrier((w_anchor, w_dest, w_out, w_hidden, payload))
+    raw = jnp.stack([jnp.concatenate([cut(w_anchor, i), cut(w_dest, i)], axis=0) for i in range(n_region)])
+    weight_out = cut(w_out, 0).astype(F32).reshape(cols, 1)
+    mid_raw = cut(w_hidden, 0)
+    mid_send = jnp.concatenate([mid_raw, last_cols], axis=0)
+    far_raw = swap_core(raw)
+    far_raw, weight_out, mid_send, *from_z = lax.optimization_barrier((far_raw, weight_out, mid_send, *from_z))
 
     spot = neighbors % (blk * n_shard) - (lax.axis_index("shard") - REACH) * blk
     valid = jnp.arange(slots, dtype=jnp.int32)[None, :] < counts[:, None]
@@ -315,32 +373,35 @@
     slot_table = jnp.pad(slot_table, ((0, 0), (0, cols - slot_table.shape[1])))
 
     held = 2 * rows_in
-    ends = [p[held:] for p in (from_z[0], from_z[-1])]
-    shared = jnp.concatenate([p[rows_in:held] for p in from_z] + [ends[0], features, ends[1], slot_table], axis=0)
+    around = [features] + [from_z[j - 1][held:] for j in next_steps(n_z)]
+    shared = jnp.concatenate([p[rows_in:held] for p in from_z] + around + [slot_table], axis=0)
     plane = jnp.concatenate([shared] + [p[:rows_in] for p in from_z], axis=0)
-    planes = [plane] + [swap_region(plane, i) for i in range(1, n_region - 1)] + [swap_region(shared, n_region - 1)]
-
-    mid_raw = cut(w_hidden, 0)
     far_plane = swap_core(plane)
-    mid_send, far_plane = lax.optimization_barrier(
-        (jnp.concatenate([mid_raw, cut(w_anchor, n_region - 1)], axis=0), far_plane)
-    )
-    mids = jnp.concatenate([mid_raw] + [along_z(mid_send, j) for j in range(1, n_z)], axis=0)
-    mine = [raw, mids, *planes]
-    other = [swap_core(raw), swap_core(mids), far_plane] + [swap_core(x) for x in planes[1:]]
-    weight_out = cut(w_out, 0).astype(F32).reshape(cols, 1)
+    mid_send, far_plane = lax.optimization_barrier((mid_send, far_plane))
+    planes = [swap_region(plane, i) for i in range(1, n_region - 1)] + [swap_region(shared, n_region - 1)]
+
+    mids = [along_z(mid_send, j) for j in range(1, n_z - 1)]
+    mid_send, mids[0] = lax.optimization_barrier((mid_send, mids[0]))
+    mids.append(along_z(mid_send, n_z - 1))
+    arrived = lax.optimization_barrier((*planes[::-1], *mids))
+    planes, mids = arrived[: n_region - 1][::-1], arrived[n_region - 1 :]
+    mids = jnp.concatenate([mid_raw, *mids], axis=0)
+    mine = [raw, mids, plane, *planes]
+    other = [far_raw, swap_core(mids), far_plane] + [swap_core(x) for x in planes]
+
+    resident = 2 * hidden * n_region * pairs <= 12 * MIB
+
+    steps = 1 if resident else n_region
+    by_lines = VMEM if resident else pl.BlockSpec((lines, 128), lambda i: (i, 0))
+
+    def by_pairs(rows):
+        return VMEM if resident else pl.BlockSpec((rows, pairs), lambda i: (0, i))
 
     first, act, score, ids, flow = pl.pallas_call(
         functools.partial(score_kernel, n_region, n_z, blk, slots),
-        grid=(n_region,),
+        grid=(steps,),
         in_specs=[VMEM] * (2 * len(mine) + 1),
-        out_specs=[
-            pl.BlockSpec((hidden, pairs), lambda i: (0, i)),
-            pl.BlockSpec((cols, pairs), lambda i: (0, i)),
-            pl.BlockSpec((lines, 128), lambda i: (i, 0)),
-            VMEM,
-            VMEM,
-        ],
+        out_specs=[by_pairs(hidden), by_pairs(cols), by_lines, VMEM, VMEM],
         scratch_shapes=[
             pltpu.VMEM((n_region * window, depth), BF),
             pltpu.VMEM((n_region * blk, depth), BF),
@@ -365,40 +426,70 @@
     parts = [score] + [swap_region(score, i) for i in range(1, n_region)]
     rows = hidden // n_shard
     block = jax.ShapeDtypeStruct((rows + TAIL, cols), BF)
-    blocks = jax.ShapeDtypeStruct((n_z, rows + TAIL, cols), BF)
-    keep, send = pl.pallas_call(
-        functools.partial(grad_kernel, n_region, n_z, slots),
-        grid=(n_region,),
-        in_specs=[pl.BlockSpec((lines, 128), functools.partial(lambda k, i: (i ^ k, 0), k)) for k in range(n_region)]
-        + [
-            VMEM,
-            VMEM,
-            pl.BlockSpec((hidden, pairs), lambda i: (0, i)),
-            pl.BlockSpec((cols, pairs), lambda i: (0, i)),
-            VMEM,
-        ],
-        out_specs=[VMEM, VMEM],
+    order = list(range(n_z))[::-1]
+    early, later, last = order[: n_z // 2], order[n_z // 2 : -1], order[-1:]
+
+    def blocks(targets):
+        return jax.ShapeDtypeStruct((len(targets), rows + TAIL, cols), BF)
+
+    def core_sum(keep, received):
+        return pl.pallas_call(
+            core_sum_kernel,
+            in_specs=[VMEM] * 2,
+            out_specs=[VMEM] * keep.shape[0],
+            out_shape=[block] * keep.shape[0],
+            compiler_params=room(4),
+            name="core_sum",
+        )(keep, received)
+
+    def rest(targets, pre):
+        return pl.pallas_call(
+            functools.partial(rest_kernel, targets),
+            grid=(steps,),
+            in_specs=[by_pairs(hidden), by_pairs(cols), VMEM],
+            out_specs=[VMEM] * 2,
+            scratch_shapes=[pltpu.VMEM((len(targets) * 2 * rows, cols), F32)],
+            out_shape=[blocks(targets)] * 2,
+            compiler_params=room(14),
+            name="gradient_rest",
+        )(first, pre, tail)
+
+    pre, tail, keep, send = pl.pallas_call(
+        functools.partial(grad_kernel, n_region, early, slots),
+        grid=(steps,),
+        in_specs=[
+            VMEM if resident else pl.BlockSpec((lines, 128), functools.partial(lambda k, i: (i ^ k, 0), k))
+            for k in range(n_region)
+        ]
+        + [VMEM, VMEM, by_pairs(hidden), by_pairs(cols), VMEM],
+        out_specs=[by_pairs(cols)] + [VMEM] * 3,
         scratch_shapes=[
-            pltpu.VMEM((hidden, cols), F32),
+            pltpu.VMEM((len(early) * 2 * rows, cols), F32),
             pltpu.VMEM((cols, 128), F32),
             pltpu.VMEM((2, lines, 128), F32),
         ],
-        out_shape=[blocks, blocks],
+        out_shape=[
+            jax.ShapeDtypeStruct((cols, n_region * pairs), BF),
+            jax.ShapeDtypeStruct((TAIL, cols), BF),
+            blocks(early),
+            blocks(early),
+        ],
         compiler_params=room(14),
         name="gradient",
     )(*parts, ids, flow, first, act, weight_out)
-
-    own_rows = pl.pallas_call(
-        core_sum_kernel,
-        in_specs=[VMEM] * 2,
-        out_specs=[VMEM] * n_z,
-        out_shape=[block] * n_z,
-        compiler_params=room(4),
-        name="core_sum",
-    )(keep, swap_core(send))
-    own_rows = [own_rows[0]] + [along_z(own_rows[j], j) for j in range(1, n_z)]
+    received = swap_core(send)
+    keep_later, send_later = rest(later, pre)
+    sums = core_sum(keep, received)
+    pre, *sums = lax.optimization_barrier((pre, *sums))
+    received_later = swap_core(send_later)
+    keep_last, send_last = rest(last, pre)
+    received_last = swap_core(send_last)
+    keep_later, received_later, keep_last = lax.optimization_barrier((keep_later, received_later, keep_last))
+    sums = lax.optimization_barrier((*sums, *core_sum(keep_later, received_later)))
+    arrived = [along_z(x, j) for x, j in zip(sums, early + later)]
+    own_rows = [*core_sum(keep_last, received_last)] + arrived
     reduced = pl.pallas_call(
-        z_sum_kernel,
+        functools.partial(z_sum_kernel, last + early + later),
         in_specs=[VMEM] * n_z,
         out_specs=VMEM,
         out_shape=block,

time: 71.7 us -> 68.9 us (0.961)
  Pallas kernels: 14.8 us -> 12.1 us
  waiting for transfers between devices: 23.3 us -> 20.7 us
  starting transfers between devices: 26.7 us -> 29.1 us
  local copies, waits for them, and re-layouts: 2.03 us -> 3.58 us
  other arithmetic: 2.5 us -> 1.19 us
    ppermute x9, waiting for transfers between devices: 14.6 us -> 11.5 us  [along_z(): lax.ppermute(array, 'shard', [(i, i ^ 2 * by) for i in range(devices)])]
    ppermute x9, starting transfers between devices: 14.2 us -> 16 us  [along_z(): lax.ppermute(array, 'shard', [(i, i ^ 2 * by) for i in range(devices)])]
    dynamic_slice x2 -> x4, local copies, waits for them, and re-layouts: 1.83 us -> 3.37 us  [cut(): lax.dynamic_slice_in_dim(array, (region ^ i) * cols, cols, array.ndim - 1)]
    pallas_call x1, Pallas kernels: 8.68 us -> 7.2 us  [shards(): pl.pallas_call(functools.partial(score_kernel, n_region, n_z, blk, slots)...]
    another operation x2, other arithmetic: 1.47 us -> 0.08 us
    ppermute x9, waiting for transfers between devices: 6.07 us -> 7.38 us  [swap_region(): return lax.ppermute(array, 'region', [(i, i ^ by) for i in range(devices)])]
    pallas_call x3 -> x7, Pallas kernels: 5.27 us -> 3.97 us  [the longest x1 2.27 us: shards(): pl.pallas_call(functools.partial(grad_kernel, n_region, early, slots), gr...]
    ppermute x7 -> x9, starting transfers between devices: 1.37 us -> 2.27 us  [swap_core(): return lax.ppermute(array, 'shard', [(i, i ^ 1) for i in range(devices)])]
  transfers between devices with their start and end apart: 25 -> 27, of which waited for: 13 -> 16; matrix products, arithmetic and copies ran while one was open for 6% -> 7% of each run, Pallas kernels for 0% -> 2%
where the time goes in v2:
time: 68.9 us; the launch traced here: 68.5 us
  starting transfers between devices  29.1 us (42%)
  waiting for transfers between devices  20.7 us (30%)
  Pallas kernels  12.1 us (18%)
  local copies, waits for them, and re-layouts  3.58 us (5%)
  other arithmetic  1.19 us (2%)
  matrix products  1.04 us (2%)
  between operations  0.95 us (1%)
    ppermute x9, starting transfers between devices, along_z(): lax.ppermute(array, 'shard', [(i, i ^ 2 * by) for i in range(devices)])  16 us
    ppermute x9, waiting for transfers between devices, along_z(): lax.ppermute(array, 'shard', [(i, i ^ 2 * by) for i in range(devices)])  11.5 us
    ppermute x9, starting transfers between devices, swap_region(): return lax.ppermute(array, 'region', [(i, i ^ by) for i in range(devices)])  10.8 us
    ppermute x9, waiting for transfers between devices, swap_region(): return lax.ppermute(array, 'region', [(i, i ^ by) for i in range(devices)])  7.38 us
    pallas_call x1, Pallas kernels, shards(): pl.pallas_call(functools.partial(score_kernel, n_region, n_z, blk, slots)...  7.2 us
    dynamic_slice x4, local copies, waits for them, and re-layouts, cut(): lax.dynamic_slice_in_dim(array, (region ^ i) * cols, cols, array.ndim - 1)  3.37 us
    ppermute x9, starting transfers between devices, swap_core(): return lax.ppermute(array, 'shard', [(i, i ^ 1) for i in range(devices)])  2.27 us
    pallas_call x1, Pallas kernels, shards(): pl.pallas_call(functools.partial(grad_kernel, n_region, early, slots), gr...  2.27 us
  transfers between devices with their start and end apart: 27, of which 16 were waited for; matrix products, arithmetic and copies ran while one was open for 7% of the time, Pallas kernels for 2%

profile of v2, /device:TPU:0, one launch (start us, length us, event | category | flops | bytes accessed | tf_op | source)
XLA Modules:
  0.0 68.5 jit_solution(14043688630737541865)
XLA Ops:
  0.7 0.9 %constant_dynamic-slice_fusion = (bf16[64,256]{1,0:T(8,128)(2,1)S(1)}, bf16[64,256]{1,0:T(8,128)(2,1)S(1)}, bf16[64,256]{1,0:T(8,128)(2,1)S(1)}) fusion(bf16[64,1024]{1,0:T(8,128)(2,1)} %param.14, s32[]{:T(128)S(6)} %select_n.35, s32[]{:T(128)S(6)} %select_n.32, bf16[64,1024]{1,0:T(8,128)(2,1)} %param.15), kind=kLoop, calls=%fused_computation.45 | loop fusion | bytes 196616 | tf_op jit(solution)/shard_map/dynamic_slice | solution.py:346
  1.6 4.1 %collective-permute-start.2 = (bf16[128,256]{1,0:T(8,128)(2,1)S(1)}, bf16[128,256]{1,0:T(8,128)(2,1)S(1)}, u32[]{:S(2)}, u32[]{:S(2)}) collective-permute-start(bf16[128,256]{1,0:T(8,128)(2,1)S(1)} %pad_maximum_fusion.4), channel_id=1, source_target_pairs={{0,4},{1,5},{2,6},{3,7},{4,0},{5,1},{6,2},{7,3},{8,12},{9,13},{10,... | collective-permute-start | bytes 196616 | tf_op jit(solution)/shard_map/ppermute | solution.py:20
  5.7 1.0 %multiply_reduce_fusion = (f32[16]{0:T(128)S(1)}, f32[16,512]{1,0:T(8,128)S(1)}) fusion(bf16[1024,512]{1,0:T(8,128)(2,1)S(1)} %copy-done, s32[1024]{0:T(1024)} %param.10), kind=kOutput, calls=%fused_computation.31 | convolution fusion | flops 16809968 | bytes 1085504 | tf_op jit(solution)/shard_map/dot_general | solution.py:356
  6.8 1.4 %collective-permute-start.3 = (bf16[160,256]{1,0:T(8,128)(2,1)S(1)}, bf16[160,256]{1,0:T(8,128)(2,1)S(1)}, u32[]{:S(2)}, u32[]{:S(2)}) collective-permute-start(bf16[160,256]{1,0:T(8,128)(2,1)S(1)} %pad_maximum_fusion.3), channel_id=1, source_target_pairs={{0,6},{1,7},{2,4},{3,5},{4,2},{5,3},{6,0},{7,1},{8,14},{9,15},{10,... | collective-permute-start | bytes 245768 | tf_op jit(solution)/shard_map/ppermute | solution.py:20
  8.3 0.3 collective-permute-start.1
  8.6 0.8 %constant_dynamic-slice_fusion.9 = (bf16[64,256]{1,0:T(8,128)(2,1)S(1)}, bf16[64,256]{1,0:T(8,128)(2,1)S(1)}, bf16[64,256]{1,0:T(8,128)(2,1)S(1)}, bf16[64,256]{1,0:T(8,128)(2,1)S(1)}) fusion(bf16[64,1024]{1,0:T(8,128)(2,1)} %param.14, s32[]{:T(128)S(6)} %select_n.32, s32[]{:T(128)S(6)} %select_n.35, s32[]{:T(128)S(6)} %select_n.34, s32[]{:T(128)S(6)} %select_n.33), kind=kLoop, calls=%fused_computation.54 | loop fusion | bytes 262160 | tf_op jit(solution)/shard_map/dynamic_slice | solution.py:346
  9.4 0.8 %constant_dynamic-slice_fusion.8 = (bf16[64,256]{1,0:T(8,128)(2,1)S(1)}, bf16[64,256]{1,0:T(8,128)(2,1)S(1)}, bf16[64,256]{1,0:T(8,128)(2,1)S(1)}, bf16[64,256]{1,0:T(8,128)(2,1)S(1)}) fusion(bf16[64,1024]{1,0:T(8,128)(2,1)} %param.15, s32[]{:T(128)S(6)} %select_n.32, s32[]{:T(128)S(6)} %select_n.35, s32[]{:T(128)S(6)} %select_n.34, s32[]{:T(128)S(6)} %select_n.33), kind=kLoop, calls=%fused_computation.53 | loop fusion | bytes 262160 | tf_op jit(solution)/shard_map/dynamic_slice | solution.py:346
  10.5 0.8 %constant_dynamic-slice_fusion.1 = bf16[128,256]{1,0:T(8,128)(2,1)S(1)} fusion(bf16[128,1024]{1,0:T(8,128)(2,1)} %param.16, s32[]{:T(128)S(6)} %select_n.32), kind=kLoop, calls=%fused_computation.46 | loop fusion | bytes 131076 | tf_op jit(solution)/shard_map/dynamic_slice | solution.py:346
  11.4 0.8 %dynamic-slice_convert_fusion = f32[256]{0:T(256)S(1)} fusion(bf16[1024]{0:T(1024)(128)(2,1)} %param.17, s32[]{:T(128)S(6)} %select_n.32), kind=kLoop, calls=%fused_computation.57 | loop fusion | flops 256 | bytes 1540 | tf_op jit(solution)/shard_map/reshape | solution.py:364
  12.1 1.5 %collective-permute-done.3 = bf16[160,256]{1,0:T(8,128)(2,1)S(1)} collective-permute-done((bf16[160,256]{1,0:T(8,128)(2,1)S(1)}, bf16[160,256]{1,0:T(8,128)(2,1)S(1)}, u32[]{:S(2)}, u32[]{:S(2)}) %collective-permute-start.3) | collective-permute-done | bytes 81952 | tf_op jit(solution)/shard_map/ppermute | solution.py:20
  13.6 0.2 collective-permute-done.1
  14.1 1.6 %collective-permute-start.6 = (bf16[496,256]{1,0:T(8,128)(2,1)S(1)}, bf16[496,256]{1,0:T(8,128)(2,1)S(1)}, u32[]{:S(2)}, u32[]{:S(2)}) collective-permute-start(bf16[496,256]{1,0:T(8,128)(2,1)S(1)} %get-tuple-element.111.refs_2_), channel_id=1, source_target_pairs={{0,8},{8,0},{16,24},{24,16},{1,9},{9,1},{17,25},{25,17},{2,10},{10... | collective-permute-start | bytes 761864 | tf_op jit(solution)/shard_map/ppermute | solution.py:34
  15.7 1.5 %collective-permute-start.5 = (bf16[496,256]{1,0:T(8,128)(2,1)S(1)}, bf16[496,256]{1,0:T(8,128)(2,1)S(1)}, u32[]{:S(2)}, u32[]{:S(2)}) collective-permute-start(bf16[496,256]{1,0:T(8,128)(2,1)S(1)} %get-tuple-element.111.refs_2_), channel_id=1, source_target_pairs={{0,16},{8,24},{16,0},{24,8},{1,17},{9,25},{17,1},{25,9},{2,18},{10... | collective-permute-start | bytes 761864 | tf_op jit(solution)/shard_map/ppermute | solution.py:34
  17.2 0.5 collective-permute-start.8
  17.8 0.6 collective-permute-start.4
  18.4 2.8 %collective-permute-start.9 = (bf16[192,256]{1,0:T(8,128)(2,1)S(1)}, bf16[192,256]{1,0:T(8,128)(2,1)S(1)}, u32[]{:S(2)}, u32[]{:S(2)}) collective-permute-start(bf16[192,256]{1,0:T(8,128)(2,1)S(1)} %pad_maximum_fusion.2), channel_id=1, source_target_pairs={{0,4},{1,5},{2,6},{3,7},{4,0},{5,1},{6,2},{7,3},{8,12},{9,13},{10,... | collective-permute-start | bytes 294920 | tf_op jit(solution)/shard_map/ppermute | solution.py:20
  21.2 1.8 %collective-permute-done.8 = bf16[192,256]{1,0:T(8,128)(2,1)S(1)} collective-permute-done((bf16[192,256]{1,0:T(8,128)(2,1)S(1)}, bf16[192,256]{1,0:T(8,128)(2,1)S(1)}, u32[]{:S(2)}, u32[]{:S(2)}) %collective-permute-start.8) | collective-permute-done | bytes 98336 | tf_op jit(solution)/shard_map/ppermute | solution.py:20
  23.0 2.5 %collective-permute-start.10 = (bf16[192,256]{1,0:T(8,128)(2,1)S(1)}, bf16[192,256]{1,0:T(8,128)(2,1)S(1)}, u32[]{:S(2)}, u32[]{:S(2)}) collective-permute-start(bf16[192,256]{1,0:T(8,128)(2,1)S(1)} %pad_maximum_fusion.2), channel_id=1, source_target_pairs={{0,6},{1,7},{2,4},{3,5},{4,2},{5,3},{6,0},{7,1},{8,14},{9,15},{10,... | collective-permute-start | bytes 294920 | tf_op jit(solution)/shard_map/ppermute | solution.py:20
  25.4 1.7 %collective-permute-done.4.refs_5_ = bf16[304,256]{1,0:T(8,128)(2,1)} collective-permute-done((bf16[304,256]{1,0:T(8,128)(2,1)S(1)}, bf16[304,256]{1,0:T(8,128)(2,1)}, u32[]{:S(2)}, u32[]{:S(2)}) %collective-permute-start.4) | collective-permute-done | bytes 155680 | tf_op jit(solution)/shard_map/ppermute | solution.py:34
  27.2 0.8 %collective-permute-done.9 = bf16[192,256]{1,0:T(8,128)(2,1)S(1)} collective-permute-done((bf16[192,256]{1,0:T(8,128)(2,1)S(1)}, bf16[192,256]{1,0:T(8,128)(2,1)S(1)}, u32[]{:S(2)}, u32[]{:S(2)}) %collective-permute-start.9) | collective-permute-done | bytes 98336 | tf_op jit(solution)/shard_map/ppermute | solution.py:20
  28.0 1.5 %collective-permute-done.10 = bf16[192,256]{1,0:T(8,128)(2,1)S(1)} collective-permute-done((bf16[192,256]{1,0:T(8,128)(2,1)S(1)}, bf16[192,256]{1,0:T(8,128)(2,1)S(1)}, u32[]{:S(2)}, u32[]{:S(2)}) %collective-permute-start.10) | collective-permute-done | bytes 98336 | tf_op jit(solution)/shard_map/ppermute | solution.py:20
  29.6 0.5 collective-permute-start.12
  30.2 0.4 collective-permute-start.14
  30.8 1.7 %collective-permute-done.14.refs_11_ = bf16[304,256]{1,0:T(8,128)(2,1)} collective-permute-done((bf16[304,256]{1,0:T(8,128)(2,1)}, bf16[304,256]{1,0:T(8,128)(2,1)}, u32[]{:S(2)}, u32[]{:S(2)}) %collective-permute-start.14) | collective-permute-done | bytes 155680 | tf_op jit(solution)/shard_map/ppermute | solution.py:29
  32.4 7.2 %scores.1 = (bf16[1024,4096]{1,0:T(8,128)(2,1)S(1)}, bf16[256,4096]{1,0:T(8,128)(2,1)S(1)}, f32[32,128]{1,0:T(8,128)S(1)}, f32[4,8,128]{2,1,0:T(8,128)S(1)}, f32[4,8,128]{2,1,0:T(8,128)S(1)}) custom-call(bf16[4,128,256]{2,1,0:T(8,128)(2,1)S(1)} %pad_maximum_fusion.1.refs_0_, bf16[704,256]{1,0:T(8,128)(2,1)S(1)} %pad_maximum_fusion.refs_1_, ...), custom_call_target="tpu_custom_call" | custom-call | tf_op jit(solution)/shard_map/scores/pallas_call | solution.py:400
  39.6 1.5 %collective-permute-start.17 = (f32[32,128]{1,0:T(8,128)S(1)}, f32[32,128]{1,0:T(8,128)S(1)}, u32[]{:S(2)}, u32[]{:S(2)}) collective-permute-start(f32[32,128]{1,0:T(8,128)S(1)} %get-tuple-element.75.refs_0_), channel_id=1, source_target_pairs={{0,24},{8,16},{16,8},{24,0},{1,25},{9,17},{17,9},{25,1},{2,26},{10... | collective-permute-start | bytes 49160 | tf_op jit(solution)/shard_map/ppermute | solution.py:34
  41.1 0.5 collective-permute-start.16
  41.6 1.6 %collective-permute-start.15 = (f32[32,128]{1,0:T(8,128)S(1)}, f32[32,128]{1,0:T(8,128)S(1)}, u32[]{:S(2)}, u32[]{:S(2)}) collective-permute-start(f32[32,128]{1,0:T(8,128)S(1)} %get-tuple-element.75.refs_0_), channel_id=1, source_target_pairs={{0,8},{8,0},{16,24},{24,16},{1,9},{9,1},{17,25},{25,17},{2,10},{10... | collective-permute-start | bytes 49160 | tf_op jit(solution)/shard_map/ppermute | solution.py:34
  43.2 1.1 %collective-permute-done.17.refs_3_ = f32[32,128]{1,0:T(8,128)S(1)} collective-permute-done((f32[32,128]{1,0:T(8,128)S(1)}, f32[32,128]{1,0:T(8,128)S(1)}, u32[]{:S(2)}, u32[]{:S(2)}) %collective-permute-start.17) | collective-permute-done | bytes 16416 | tf_op jit(solution)/shard_map/ppermute | solution.py:34
  44.4 0.5 collective-permute-done.16.refs_2_
  44.8 0.5 collective-permute-done.15.refs_1_
  45.3 2.3 %gradient.1 = (bf16[256,4096]{1,0:T(8,128)(2,1)S(1)}, bf16[16,256]{1,0:T(8,128)(2,1)S(1)}, bf16[2,144,256]{2,1,0:T(8,128)(2,1)S(1)}, bf16[2,144,256]{2,1,0:T(8,128)(2,1)S(1)}) custom-call(f32[32,128]{1,0:T(8,128)S(1)} %get-tuple-element.75.refs_0_, f32[32,128]{1,0:T(8,128)S(1)} %collective-permute-done.15.refs_1_, ...), custom_call_target="tpu_custom_call" | custom-call | tf_op jit(solution)/shard_map/gradient/pallas_call | solution.py:457
  47.7 0.8 %gradient_rest.2 = (bf16[1,144,256]{2,1,0:T(8,128)(2,1)S(1)}, bf16[1,144,256]{2,1,0:T(8,128)(2,1)S(1)}) custom-call(bf16[1024,4096]{1,0:T(8,128)(2,1)S(1)} %get-tuple-element.74.refs_6_.refs_0_, bf16[256,4096]{1,0:T(8,128)(2,1)S(1)} %get-tuple-element.87.refs_1_, bf16[16,256]{1,0:T(8,128)(2,1)S(1)} %get-tuple-element.80.refs_2_), custom_call_target="tpu_custom_call" | custom-call | tf_op jit(solution)/shard_map/gradient_rest/pallas_call | solution.py:446
  48.5 0.6 collective-permute-start.18
  49.1 0.8 %gradient_rest.3 = (bf16[1,144,256]{2,1,0:T(8,128)(2,1)S(1)}, bf16[1,144,256]{2,1,0:T(8,128)(2,1)S(1)}) custom-call(bf16[1024,4096]{1,0:T(8,128)(2,1)S(1)} %get-tuple-element.74.refs_6_.refs_0_, bf16[256,4096]{1,0:T(8,128)(2,1)S(1)} %get-tuple-element.87.refs_1_, bf16[16,256]{1,0:T(8,128)(2,1)S(1)} %get-tuple-element.80.refs_2_), custom_call_target="tpu_custom_call" | custom-call | tf_op jit(solution)/shard_map/gradient_rest/pallas_call | solution.py:446
  50.0 0.4 collective-permute-start.20
  50.4 2.5 %collective-permute-start.21 = (bf16[144,256]{1,0:T(8,128)(2,1)S(1)}, bf16[144,256]{1,0:T(8,128)(2,1)S(1)}, u32[]{:S(2)}, u32[]{:S(2)}) collective-permute-start(bf16[144,256]{1,0:T(8,128)(2,1)S(1)} %get-tuple-element.95), channel_id=1, source_target_pairs={{0,6},{1,7},{2,4},{3,5},{4,2},{5,3},{6,0},{7,1},{8,14},{9,15},{10,... | collective-permute-start | bytes 221192 | tf_op jit(solution)/shard_map/ppermute | solution.py:20
  52.9 0.5 collective-permute-start.22
  53.5 1.3 %collective-permute-start.23 = (bf16[144,256]{1,0:T(8,128)(2,1)S(1)}, bf16[144,256]{1,0:T(8,128)(2,1)S(1)}, u32[]{:S(2)}, u32[]{:S(2)}) collective-permute-start(bf16[144,256]{1,0:T(8,128)(2,1)S(1)} %core_sum.5), channel_id=1, source_target_pairs={{0,2},{1,3},{2,0},{3,1},{4,6},{5,7},{6,4},{7,5},{8,10},{9,11},{10,... | collective-permute-start | bytes 221192 | tf_op jit(solution)/shard_map/ppermute | solution.py:20
  54.8 2.0 %collective-permute-done.21.refs_1_ = bf16[144,256]{1,0:T(8,128)(2,1)S(1)} collective-permute-done((bf16[144,256]{1,0:T(8,128)(2,1)S(1)}, bf16[144,256]{1,0:T(8,128)(2,1)S(1)}, u32[]{:S(2)}, u32[]{:S(2)}) %collective-permute-start.21) | collective-permute-done | bytes 73760 | tf_op jit(solution)/shard_map/ppermute | solution.py:20
  56.8 3.8 %collective-permute-done.22.refs_2_ = bf16[144,256]{1,0:T(8,128)(2,1)S(1)} collective-permute-done((bf16[144,256]{1,0:T(8,128)(2,1)S(1)}, bf16[144,256]{1,0:T(8,128)(2,1)S(1)}, u32[]{:S(2)}, u32[]{:S(2)}) %collective-permute-start.22) | collective-permute-done | bytes 73760 | tf_op jit(solution)/shard_map/ppermute | solution.py:20
  60.6 1.5 %collective-permute-start.26 = (bf16[144,256]{1,0:T(8,128)(2,1)S(1)}, bf16[144,256]{1,0:T(8,128)(2,1)S(1)}, u32[]{:S(2)}, u32[]{:S(2)}) collective-permute-start(bf16[144,256]{1,0:T(8,128)(2,1)S(1)} %z_sum.1.refs_0_), channel_id=1, source_target_pairs={{0,24},{8,16},{16,8},{24,0},{1,25},{9,17},{17,9},{25,1},{2,26},{10... | collective-permute-start | bytes 221192 | tf_op jit(solution)/shard_map/ppermute | solution.py:34
  62.1 1.2 %collective-permute-start.25 = (bf16[144,256]{1,0:T(8,128)(2,1)S(1)}, bf16[144,256]{1,0:T(8,128)(2,1)S(1)}, u32[]{:S(2)}, u32[]{:S(2)}) collective-permute-start(bf16[144,256]{1,0:T(8,128)(2,1)S(1)} %z_sum.1.refs_0_), channel_id=1, source_target_pairs={{0,16},{8,24},{16,0},{24,8},{1,17},{9,25},{17,1},{25,9},{2,18},{10... | collective-permute-start | bytes 221192 | tf_op jit(solution)/shard_map/ppermute | solution.py:34
  63.3 0.8 %collective-permute-start.24 = (bf16[144,256]{1,0:T(8,128)(2,1)S(1)}, bf16[144,256]{1,0:T(8,128)(2,1)S(1)}, u32[]{:S(2)}, u32[]{:S(2)}) collective-permute-start(bf16[144,256]{1,0:T(8,128)(2,1)S(1)} %z_sum.1.refs_0_), channel_id=1, source_target_pairs={{0,8},{8,0},{16,24},{24,16},{1,9},{9,1},{17,25},{25,17},{2,10},{10... | collective-permute-start | bytes 221192 | tf_op jit(solution)/shard_map/ppermute | solution.py:34
  64.1 2.6 %collective-permute-done.26.refs_3_ = bf16[144,256]{1,0:T(8,128)(2,1)S(1)} collective-permute-done((bf16[144,256]{1,0:T(8,128)(2,1)S(1)}, bf16[144,256]{1,0:T(8,128)(2,1)S(1)}, u32[]{:S(2)}, u32[]{:S(2)}) %collective-permute-start.26) | collective-permute-done | bytes 73760 | tf_op jit(solution)/shard_map/ppermute | solution.py:34
  66.7 0.3 collective-permute-done.25.refs_2_
  67.0 0.7 collective-permute-done.24.refs_1_
  67.6 0.9 %finish.1 = (f32[128,1024]{1,0:T(8,128)}, f32[1,1024]{1,0:T(1,128)}, f32[1,1]{1,0:T(1,128)}) custom-call(bf16[144,256]{1,0:T(8,128)(2,1)S(1)} %z_sum.1.refs_0_, bf16[144,256]{1,0:T(8,128)(2,1)S(1)} %collective-permute-done.24.refs_1_, bf16[144,256]{1,0:T(8,128)(2,1)S(1)} %collective-permute-done.25.refs_2_, bf16[144,256]{1,0:T(8,128)(2,1)S(1)} %collective-permute-done.26.refs_3_), custom_call_target="tpu_custom_call" | custom-call | tf_op jit(solution)/shard_map/finish/pallas_call | solution.py:501
  (60 shorter events, 1.3 us)
Async XLA Ops:
  0.6 5.1 %copy-start = (bf16[1024,512]{1,0:T(8,128)(2,1)S(1)}, bf16[1024,512]{1,0:T(8,128)(2,1)}, u32[]{:S(2)}) copy-start(bf16[1024,512]{1,0:T(8,128)(2,1)} %param.9) | copy-start | bytes 3145732
  0.6 9.8 %copy-start.3 = (s32[16]{0:T(128)S(1)}, s32[16]{0:T(128)}, u32[]{:S(2)}) copy-start(s32[16]{0:T(128)} %param.12) | copy-start | bytes 196
  0.7 9.8 %copy-start.2 = (s32[16,64]{1,0:T(8,128)S(1)}, s32[16,64]{1,0:T(8,128)}, u32[]{:S(2)}) copy-start(s32[16,64]{1,0:T(8,128)} %param.11) | copy-start | bytes 12292
  0.7 10.7 %copy-start.1 = (s32[16,64]{1,0:T(8,128)S(1)}, s32[16,64]{1,0:T(8,128)}, u32[]{:S(2)}) copy-start(s32[16,64]{1,0:T(8,128)} %param.13) | copy-start | bytes 12292
  1.6 10.6 %collective-permute-start.2 = (bf16[128,256]{1,0:T(8,128)(2,1)S(1)}, bf16[128,256]{1,0:T(8,128)(2,1)S(1)}, u32[]{:S(2)}, u32[]{:S(2)}) collective-permute-start(bf16[128,256]{1,0:T(8,128)(2,1)S(1)} %pad_maximum_fusion.4), channel_id=1, source_target_pairs={{0,4},{1,5},{2,6},{3,7},{4,0},{5,1},{6,2},{7,3},{8,12},{9,13},{10,... | collective-permute-start | bytes 196616 | tf_op jit(solution)/shard_map/ppermute | solution.py:20
  6.8 6.8 %collective-permute-start.3 = (bf16[160,256]{1,0:T(8,128)(2,1)S(1)}, bf16[160,256]{1,0:T(8,128)(2,1)S(1)}, u32[]{:S(2)}, u32[]{:S(2)}) collective-permute-start(bf16[160,256]{1,0:T(8,128)(2,1)S(1)} %pad_maximum_fusion.3), channel_id=1, source_target_pairs={{0,6},{1,7},{2,4},{3,5},{4,2},{5,3},{6,0},{7,1},{8,14},{9,15},{10,... | collective-permute-start | bytes 245768 | tf_op jit(solution)/shard_map/ppermute | solution.py:20
  8.3 5.6 %collective-permute-start.1 = (bf16[160,256]{1,0:T(8,128)(2,1)S(1)}, bf16[160,256]{1,0:T(8,128)(2,1)S(1)}, u32[]{:S(2)}, u32[]{:S(2)}) collective-permute-start(bf16[160,256]{1,0:T(8,128)(2,1)S(1)} %pad_maximum_fusion.3), channel_id=1, source_target_pairs={{0,2},{1,3},{2,0},{3,1},{4,6},{5,7},{6,4},{7,5},{8,10},{9,11},{10,... | collective-permute-start | bytes 245768 | tf_op jit(solution)/shard_map/ppermute | solution.py:20
  10.3 3.5 %collective-permute-start = (bf16[4,128,256]{2,1,0:T(8,128)(2,1)S(1)}, bf16[4,128,256]{2,1,0:T(8,128)(2,1)S(1)}, u32[]{:S(2)}, u32[]{:S(2)}) collective-permute-start(bf16[4,128,256]{2,1,0:T(8,128)(2,1)S(1)} %pad_maximum_fusion.1.refs_0_), channel_id=1, source_target_pairs={{0,1},{1,0},{2,3},{3,2},{4,5},{5,4},{6,7},{7,6},{8,9},{9,8},{10,11... | collective-permute-start | bytes 786440 | tf_op jit(solution)/shard_map/ppermute | solution.py:29
  14.0 3.2 %collective-permute-start.7 = (bf16[496,256]{1,0:T(8,128)(2,1)S(1)}, bf16[496,256]{1,0:T(8,128)(2,1)S(1)}, u32[]{:S(2)}, u32[]{:S(2)}) collective-permute-start(bf16[496,256]{1,0:T(8,128)(2,1)S(1)} %get-tuple-element.111.refs_2_), channel_id=1, source_target_pairs={{0,1},{1,0},{2,3},{3,2},{4,5},{5,4},{6,7},{7,6},{8,9},{9,8},{10,11... | collective-permute-start | bytes 761864 | tf_op jit(solution)/shard_map/ppermute | solution.py:29
  14.1 13.1 %collective-permute-start.6 = (bf16[496,256]{1,0:T(8,128)(2,1)S(1)}, bf16[496,256]{1,0:T(8,128)(2,1)S(1)}, u32[]{:S(2)}, u32[]{:S(2)}) collective-permute-start(bf16[496,256]{1,0:T(8,128)(2,1)S(1)} %get-tuple-element.111.refs_2_), channel_id=1, source_target_pairs={{0,8},{8,0},{16,24},{24,16},{1,9},{9,1},{17,25},{25,17},{2,10},{10... | collective-permute-start | bytes 761864 | tf_op jit(solution)/shard_map/ppermute | solution.py:34
  15.7 11.5 %collective-permute-start.5 = (bf16[496,256]{1,0:T(8,128)(2,1)S(1)}, bf16[496,256]{1,0:T(8,128)(2,1)S(1)}, u32[]{:S(2)}, u32[]{:S(2)}) collective-permute-start(bf16[496,256]{1,0:T(8,128)(2,1)S(1)} %get-tuple-element.111.refs_2_), channel_id=1, source_target_pairs={{0,16},{8,24},{16,0},{24,8},{1,17},{9,25},{17,1},{25,9},{2,18},{10... | collective-permute-start | bytes 761864 | tf_op jit(solution)/shard_map/ppermute | solution.py:34
  17.2 5.8 %collective-permute-start.8 = (bf16[192,256]{1,0:T(8,128)(2,1)S(1)}, bf16[192,256]{1,0:T(8,128)(2,1)S(1)}, u32[]{:S(2)}, u32[]{:S(2)}) collective-permute-start(bf16[192,256]{1,0:T(8,128)(2,1)S(1)} %pad_maximum_fusion.2), channel_id=1, source_target_pairs={{0,2},{1,3},{2,0},{3,1},{4,6},{5,7},{6,4},{7,5},{8,10},{9,11},{10,... | collective-permute-start | bytes 294920 | tf_op jit(solution)/shard_map/ppermute | solution.py:20
  17.8 9.4 %collective-permute-start.4 = (bf16[304,256]{1,0:T(8,128)(2,1)S(1)}, bf16[304,256]{1,0:T(8,128)(2,1)}, u32[]{:S(2)}, u32[]{:S(2)}) collective-permute-start(bf16[304,256]{1,0:T(8,128)(2,1)S(1)} %constant_dynamic-update-slice_fusion), channel_id=1, source_target_pairs={{0,24},{8,16},{16,8},{24,0},{1,25},{9,17},{17,9},{25,1},{2,26},{10... | collective-permute-start | bytes 466952 | tf_op jit(solution)/shard_map/ppermute | solution.py:34
  18.4 9.6 %collective-permute-start.9 = (bf16[192,256]{1,0:T(8,128)(2,1)S(1)}, bf16[192,256]{1,0:T(8,128)(2,1)S(1)}, u32[]{:S(2)}, u32[]{:S(2)}) collective-permute-start(bf16[192,256]{1,0:T(8,128)(2,1)S(1)} %pad_maximum_fusion.2), channel_id=1, source_target_pairs={{0,4},{1,5},{2,6},{3,7},{4,0},{5,1},{6,2},{7,3},{8,12},{9,13},{10,... | collective-permute-start | bytes 294920 | tf_op jit(solution)/shard_map/ppermute | solution.py:20
  23.0 6.5 %collective-permute-start.10 = (bf16[192,256]{1,0:T(8,128)(2,1)S(1)}, bf16[192,256]{1,0:T(8,128)(2,1)S(1)}, u32[]{:S(2)}, u32[]{:S(2)}) collective-permute-start(bf16[192,256]{1,0:T(8,128)(2,1)S(1)} %pad_maximum_fusion.2), channel_id=1, source_target_pairs={{0,6},{1,7},{2,4},{3,5},{4,2},{5,3},{6,0},{7,1},{8,14},{9,15},{10,... | collective-permute-start | bytes 294920 | tf_op jit(solution)/shard_map/ppermute | solution.py:20
  29.5 2.9 %collective-permute-start.11 = (bf16[704,256]{1,0:T(8,128)(2,1)S(1)}, bf16[704,256]{1,0:T(8,128)(2,1)S(1)}, u32[]{:S(2)}, u32[]{:S(2)}) collective-permute-start(bf16[704,256]{1,0:T(8,128)(2,1)S(1)} %pad_maximum_fusion.refs_1_), channel_id=1, source_target_pairs={{0,1},{1,0},{2,3},{3,2},{4,5},{5,4},{6,7},{7,6},{8,9},{9,8},{10,11... | collective-permute-start | bytes 1081352 | tf_op jit(solution)/shard_map/ppermute | solution.py:29
  29.6 2.8 %collective-permute-start.12 = (bf16[496,256]{1,0:T(8,128)(2,1)S(1)}, bf16[496,256]{1,0:T(8,128)(2,1)}, u32[]{:S(2)}, u32[]{:S(2)}) collective-permute-start(bf16[496,256]{1,0:T(8,128)(2,1)S(1)} %collective-permute-done.6.refs_3_), channel_id=1, source_target_pairs={{0,1},{1,0},{2,3},{3,2},{4,5},{5,4},{6,7},{7,6},{8,9},{9,8},{10,11... | collective-permute-start | bytes 761864 | tf_op jit(solution)/shard_map/ppermute | solution.py:29
  30.1 2.3 %collective-permute-start.13 = (bf16[496,256]{1,0:T(8,128)(2,1)S(1)}, bf16[496,256]{1,0:T(8,128)(2,1)}, u32[]{:S(2)}, u32[]{:S(2)}) collective-permute-start(bf16[496,256]{1,0:T(8,128)(2,1)S(1)} %collective-permute-done.5.refs_4_), channel_id=1, source_target_pairs={{0,1},{1,0},{2,3},{3,2},{4,5},{5,4},{6,7},{7,6},{8,9},{9,8},{10,11... | collective-permute-start | bytes 761864 | tf_op jit(solution)/shard_map/ppermute | solution.py:29
  30.2 2.2 %collective-permute-start.14 = (bf16[304,256]{1,0:T(8,128)(2,1)}, bf16[304,256]{1,0:T(8,128)(2,1)}, u32[]{:S(2)}, u32[]{:S(2)}) collective-permute-start(bf16[304,256]{1,0:T(8,128)(2,1)} %collective-permute-done.4.refs_5_), channel_id=1, source_target_pairs={{0,1},{1,0},{2,3},{3,2},{4,5},{5,4},{6,7},{7,6},{8,9},{9,8},{10,11... | collective-permute-start | bytes 466952 | tf_op jit(solution)/shard_map/ppermute | solution.py:29
  39.6 4.7 %collective-permute-start.17 = (f32[32,128]{1,0:T(8,128)S(1)}, f32[32,128]{1,0:T(8,128)S(1)}, u32[]{:S(2)}, u32[]{:S(2)}) collective-permute-start(f32[32,128]{1,0:T(8,128)S(1)} %get-tuple-element.75.refs_0_), channel_id=1, source_target_pairs={{0,24},{8,16},{16,8},{24,0},{1,25},{9,17},{17,9},{25,1},{2,26},{10... | collective-permute-start | bytes 49160 | tf_op jit(solution)/shard_map/ppermute | solution.py:34
  41.1 3.7 %collective-permute-start.16 = (f32[32,128]{1,0:T(8,128)S(1)}, f32[32,128]{1,0:T(8,128)S(1)}, u32[]{:S(2)}, u32[]{:S(2)}) collective-permute-start(f32[32,128]{1,0:T(8,128)S(1)} %get-tuple-element.75.refs_0_), channel_id=1, source_target_pairs={{0,16},{8,24},{16,0},{24,8},{1,17},{9,25},{17,1},{25,9},{2,18},{10... | collective-permute-start | bytes 49160 | tf_op jit(solution)/shard_map/ppermute | solution.py:34
  41.6 3.7 %collective-permute-start.15 = (f32[32,128]{1,0:T(8,128)S(1)}, f32[32,128]{1,0:T(8,128)S(1)}, u32[]{:S(2)}, u32[]{:S(2)}) collective-permute-start(f32[32,128]{1,0:T(8,128)S(1)} %get-tuple-element.75.refs_0_), channel_id=1, source_target_pairs={{0,8},{8,0},{16,24},{24,16},{1,9},{9,1},{17,25},{25,17},{2,10},{10... | collective-permute-start | bytes 49160 | tf_op jit(solution)/shard_map/ppermute | solution.py:34
  47.6 1.4 %collective-permute-start.19 = (bf16[2,144,256]{2,1,0:T(8,128)(2,1)S(1)}, bf16[2,144,256]{2,1,0:T(8,128)(2,1)S(1)}, u32[]{:S(2)}, u32[]{:S(2)}) collective-permute-start(bf16[2,144,256]{2,1,0:T(8,128)(2,1)S(1)} %get-tuple-element.84), channel_id=1, source_target_pairs={{0,1},{1,0},{2,3},{3,2},{4,5},{5,4},{6,7},{7,6},{8,9},{9,8},{10,11... | collective-permute-start | bytes 442376 | tf_op jit(solution)/shard_map/ppermute | solution.py:29
  48.5 1.5 %collective-permute-start.18 = (bf16[1,144,256]{2,1,0:T(8,128)(2,1)S(1)}, bf16[1,144,256]{2,1,0:T(8,128)(2,1)S(1)}, u32[]{:S(2)}, u32[]{:S(2)}) collective-permute-start(bf16[1,144,256]{2,1,0:T(8,128)(2,1)S(1)} %get-tuple-element.82), channel_id=1, source_target_pairs={{0,1},{1,0},{2,3},{3,2},{4,5},{5,4},{6,7},{7,6},{8,9},{9,8},{10,11... | collective-permute-start | bytes 221192 | tf_op jit(solution)/shard_map/ppermute | solution.py:29
  50.0 4.8 %collective-permute-start.20 = (bf16[1,144,256]{2,1,0:T(8,128)(2,1)S(1)}, bf16[1,144,256]{2,1,0:T(8,128)(2,1)S(1)}, u32[]{:S(2)}, u32[]{:S(2)}) collective-permute-start(bf16[1,144,256]{2,1,0:T(8,128)(2,1)S(1)} %get-tuple-element.90), channel_id=1, source_target_pairs={{0,1},{1,0},{2,3},{3,2},{4,5},{5,4},{6,7},{7,6},{8,9},{9,8},{10,11... | collective-permute-start | bytes 221192 | tf_op jit(solution)/shard_map/ppermute | solution.py:29
  50.4 6.4 %collective-permute-start.21 = (bf16[144,256]{1,0:T(8,128)(2,1)S(1)}, bf16[144,256]{1,0:T(8,128)(2,1)S(1)}, u32[]{:S(2)}, u32[]{:S(2)}) collective-permute-start(bf16[144,256]{1,0:T(8,128)(2,1)S(1)} %get-tuple-element.95), channel_id=1, source_target_pairs={{0,6},{1,7},{2,4},{3,5},{4,2},{5,3},{6,0},{7,1},{8,14},{9,15},{10,... | collective-permute-start | bytes 221192 | tf_op jit(solution)/shard_map/ppermute | solution.py:20
  52.9 7.6 %collective-permute-start.22 = (bf16[144,256]{1,0:T(8,128)(2,1)S(1)}, bf16[144,256]{1,0:T(8,128)(2,1)S(1)}, u32[]{:S(2)}, u32[]{:S(2)}) collective-permute-start(bf16[144,256]{1,0:T(8,128)(2,1)S(1)} %get-tuple-element.96), channel_id=1, source_target_pairs={{0,4},{1,5},{2,6},{3,7},{4,0},{5,1},{6,2},{7,3},{8,12},{9,13},{10,... | collective-permute-start | bytes 221192 | tf_op jit(solution)/shard_map/ppermute | solution.py:20
  53.5 7.0 %collective-permute-start.23 = (bf16[144,256]{1,0:T(8,128)(2,1)S(1)}, bf16[144,256]{1,0:T(8,128)(2,1)S(1)}, u32[]{:S(2)}, u32[]{:S(2)}) collective-permute-start(bf16[144,256]{1,0:T(8,128)(2,1)S(1)} %core_sum.5), channel_id=1, source_target_pairs={{0,2},{1,3},{2,0},{3,1},{4,6},{5,7},{6,4},{7,5},{8,10},{9,11},{10,... | collective-permute-start | bytes 221192 | tf_op jit(solution)/shard_map/ppermute | solution.py:20
  60.6 6.1 %collective-permute-start.26 = (bf16[144,256]{1,0:T(8,128)(2,1)S(1)}, bf16[144,256]{1,0:T(8,128)(2,1)S(1)}, u32[]{:S(2)}, u32[]{:S(2)}) collective-permute-start(bf16[144,256]{1,0:T(8,128)(2,1)S(1)} %z_sum.1.refs_0_), channel_id=1, source_target_pairs={{0,24},{8,16},{16,8},{24,0},{1,25},{9,17},{17,9},{25,1},{2,26},{10... | collective-permute-start | bytes 221192 | tf_op jit(solution)/shard_map/ppermute | solution.py:34
  62.1 4.9 %collective-permute-start.25 = (bf16[144,256]{1,0:T(8,128)(2,1)S(1)}, bf16[144,256]{1,0:T(8,128)(2,1)S(1)}, u32[]{:S(2)}, u32[]{:S(2)}) collective-permute-start(bf16[144,256]{1,0:T(8,128)(2,1)S(1)} %z_sum.1.refs_0_), channel_id=1, source_target_pairs={{0,16},{8,24},{16,0},{24,8},{1,17},{9,25},{17,1},{25,9},{2,18},{10... | collective-permute-start | bytes 221192 | tf_op jit(solution)/shard_map/ppermute | solution.py:34
  63.3 4.4 %collective-permute-start.24 = (bf16[144,256]{1,0:T(8,128)(2,1)S(1)}, bf16[144,256]{1,0:T(8,128)(2,1)S(1)}, u32[]{:S(2)}, u32[]{:S(2)}) collective-permute-start(bf16[144,256]{1,0:T(8,128)(2,1)S(1)} %z_sum.1.refs_0_), channel_id=1, source_target_pairs={{0,8},{8,0},{16,24},{24,16},{1,9},{9,1},{17,25},{25,17},{2,10},{10... | collective-permute-start | bytes 221192 | tf_op jit(solution)/shard_map/ppermute | solution.py:34

commit v3 on v2

--- a/solution.py
+++ b/solution.py
@@ -95,7 +95,7 @@
             for j in range(n_z):
                 shard_at = 2 * (z ^ j) + core_at
                 at = pl.ds(pl.multiple_of(shard_at * raw_cut, raw_cut), raw_cut)
-                mid = rows_mid + (j - 1) * (rows_mid + raw_cut) if j > 0 else 0
+                mid = rows_mid + (n_z - 1 - j) * (rows_mid + raw_cut) if j > 0 else 0
                 w_mid[unit_rows(shard_at, rows_mid, cols, region), :] = mids[mid : mid + rows_mid, :]
                 for i in range(n_region):
                     base = (j - 1) * raw_cut
@@ -350,7 +350,6 @@
 
     piece = jnp.concatenate([cut(w_anchor, 0), cut(w_dest, 0)], axis=0)
 
-    last_cols = cut(w_anchor, n_region - 1)
     piece, tile_block = lax.optimization_barrier((piece, tile_block))
     onehot = (tile_block[None, :] == jnp.arange(blk, dtype=jnp.int32)[:, None]).astype(BF)
     sums = jnp.dot(onehot, tiles, preferred_element_type=F32)
@@ -359,13 +358,8 @@
 
     payload = jnp.concatenate([piece, features], axis=0)
     from_z = [along_z(payload if j in next_steps(n_z) else piece, j) for j in range(1, n_z)]
-    w_anchor, w_dest, w_out, w_hidden, payload = lax.optimization_barrier((w_anchor, w_dest, w_out, w_hidden, payload))
+    w_anchor, w_dest, payload = lax.optimization_barrier((w_anchor, w_dest, payload))
     raw = jnp.stack([jnp.concatenate([cut(w_anchor, i), cut(w_dest, i)], axis=0) for i in range(n_region)])
-    weight_out = cut(w_out, 0).astype(F32).reshape(cols, 1)
-    mid_raw = cut(w_hidden, 0)
-    mid_send = jnp.concatenate([mid_raw, last_cols], axis=0)
-    far_raw = swap_core(raw)
-    far_raw, weight_out, mid_send, *from_z = lax.optimization_barrier((far_raw, weight_out, mid_send, *from_z))
 
     spot = neighbors % (blk * n_shard) - (lax.axis_index("shard") - REACH) * blk
     valid = jnp.arange(slots, dtype=jnp.int32)[None, :] < counts[:, None]
@@ -376,18 +370,17 @@
     around = [features] + [from_z[j - 1][held:] for j in next_steps(n_z)]
     shared = jnp.concatenate([p[rows_in:held] for p in from_z] + around + [slot_table], axis=0)
     plane = jnp.concatenate([shared] + [p[:rows_in] for p in from_z], axis=0)
+    planes = [plane] + [swap_region(plane, i) for i in range(1, n_region - 1)] + [swap_region(shared, n_region - 1)]
+
+    mid_raw = cut(w_hidden, 0)
     far_plane = swap_core(plane)
-    mid_send, far_plane = lax.optimization_barrier((mid_send, far_plane))
-    planes = [swap_region(plane, i) for i in range(1, n_region - 1)] + [swap_region(shared, n_region - 1)]
-
-    mids = [along_z(mid_send, j) for j in range(1, n_z - 1)]
-    mid_send, mids[0] = lax.optimization_barrier((mid_send, mids[0]))
-    mids.append(along_z(mid_send, n_z - 1))
-    arrived = lax.optimization_barrier((*planes[::-1], *mids))
-    planes, mids = arrived[: n_region - 1][::-1], arrived[n_region - 1 :]
-    mids = jnp.concatenate([mid_raw, *mids], axis=0)
-    mine = [raw, mids, plane, *planes]
-    other = [far_raw, swap_core(mids), far_plane] + [swap_core(x) for x in planes]
+    mid_send, far_plane = lax.optimization_barrier(
+        (jnp.concatenate([mid_raw, cut(w_anchor, n_region - 1)], axis=0), far_plane)
+    )
+    mids = jnp.concatenate([mid_raw] + [along_z(mid_send, j) for j in range(1, n_z)][::-1], axis=0)
+    mine = [raw, mids, *planes]
+    other = [swap_core(raw), swap_core(mids), far_plane] + [swap_core(x) for x in planes[1:]]
+    weight_out = cut(w_out, 0).astype(F32).reshape(cols, 1)
 
     resident = 2 * hidden * n_region * pairs <= 12 * MIB
 

time: 68.9 us -> 68.4 us (level)
  starting transfers between devices: 29.1 us -> 28.2 us
  local copies, waits for them, and re-layouts: 3.58 us -> 2.78 us
    ppermute x9, waiting for transfers between devices: 11.5 us -> 13.9 us  [along_z(): lax.ppermute(array, 'shard', [(i, i ^ 2 * by) for i in range(devices)])]
    ppermute x9, starting transfers between devices: 16 us -> 14.6 us  [along_z(): lax.ppermute(array, 'shard', [(i, i ^ 2 * by) for i in range(devices)])]
    ppermute x9, waiting for transfers between devices: 7.38 us -> 6.18 us  [swap_region(): return lax.ppermute(array, 'region', [(i, i ^ by) for i in range(devices)])]
    dynamic_slice x4, local copies, waits for them, and re-layouts: 3.37 us -> 2.56 us  [cut(): lax.dynamic_slice_in_dim(array, (region ^ i) * cols, cols, array.ndim - 1)]
    another operation x2, other arithmetic: 0.08 us -> 0.78 us
  transfers between devices with their start and end apart: 27 -> 27, of which waited for: 16 -> 14; matrix products, arithmetic and copies ran while one was open for 7% -> 7% of each run, Pallas kernels for 2% -> 2%
where the time goes in v3:
time: 68.4 us; the launch traced here: 68.1 us
  starting transfers between devices  28.2 us (41%)
  waiting for transfers between devices  21.3 us (31%)
  Pallas kernels  12.1 us (18%)
  local copies, waits for them, and re-layouts  2.78 us (4%)
  other arithmetic  1.8 us (3%)
  matrix products  1.04 us (2%)
  between operations  0.95 us (1%)
    ppermute x9, starting transfers between devices, along_z(): lax.ppermute(array, 'shard', [(i, i ^ 2 * by) for i in range(devices)])  14.6 us
    ppermute x9, waiting for transfers between devices, along_z(): lax.ppermute(array, 'shard', [(i, i ^ 2 * by) for i in range(devices)])  13.9 us
    ppermute x9, starting transfers between devices, swap_region(): return lax.ppermute(array, 'region', [(i, i ^ by) for i in range(devices)])  11.3 us
    pallas_call x1, Pallas kernels, shards(): pl.pallas_call(functools.partial(score_kernel, n_region, n_z, blk, slots)...  7.19 us
    ppermute x9, waiting for transfers between devices, swap_region(): return lax.ppermute(array, 'region', [(i, i ^ by) for i in range(devices)])  6.18 us
    dynamic_slice x4, local copies, waits for them, and re-layouts, cut(): lax.dynamic_slice_in_dim(array, (region ^ i) * cols, cols, array.ndim - 1)  2.56 us
    pallas_call x1, Pallas kernels, shards(): pl.pallas_call(functools.partial(grad_kernel, n_region, early, slots), gr...  2.27 us
    ppermute x9, starting transfers between devices, swap_core(): return lax.ppermute(array, 'shard', [(i, i ^ 1) for i in range(devices)])  2.26 us
  transfers between devices with their start and end apart: 27, of which 14 were waited for; matrix products, arithmetic and copies ran while one was open for 7% of the time, Pallas kernels for 2%

profile of v3, /device:TPU:0, one launch (start us, length us, event | category | flops | bytes accessed | tf_op | source)
XLA Modules:
  0.0 68.1 jit_solution(2304700417655593323)
XLA Ops:
  0.7 0.9 %constant_dynamic-slice_fusion.9 = (bf16[64,256]{1,0:T(8,128)(2,1)S(1)}, bf16[64,256]{1,0:T(8,128)(2,1)S(1)}) fusion(bf16[64,1024]{1,0:T(8,128)(2,1)} %param.15, s32[]{:T(128)S(6)} %select_n.32, bf16[64,1024]{1,0:T(8,128)(2,1)} %param.14), kind=kLoop, calls=%fused_computation.54 | loop fusion | bytes 131076 | tf_op jit(solution)/shard_map/dynamic_slice | solution.py:346
  1.6 4.1 %collective-permute-start.1 = (bf16[128,256]{1,0:T(8,128)(2,1)S(1)}, bf16[128,256]{1,0:T(8,128)(2,1)S(1)}, u32[]{:S(2)}, u32[]{:S(2)}) collective-permute-start(bf16[128,256]{1,0:T(8,128)(2,1)S(1)} %pad_maximum_fusion.4), channel_id=1, source_target_pairs={{0,4},{1,5},{2,6},{3,7},{4,0},{5,1},{6,2},{7,3},{8,12},{9,13},{10,... | collective-permute-start | bytes 196616 | tf_op jit(solution)/shard_map/ppermute | solution.py:20
  5.7 1.0 %multiply_reduce_fusion = (f32[16]{0:T(128)S(1)}, f32[16,512]{1,0:T(8,128)S(1)}) fusion(bf16[1024,512]{1,0:T(8,128)(2,1)S(1)} %copy-done, s32[1024]{0:T(1024)} %param.10), kind=kOutput, calls=%fused_computation.31 | convolution fusion | flops 16809968 | bytes 1085504 | tf_op jit(solution)/shard_map/dot_general | solution.py:355
  6.8 1.4 %collective-permute-start.2 = (bf16[160,256]{1,0:T(8,128)(2,1)S(1)}, bf16[160,256]{1,0:T(8,128)(2,1)S(1)}, u32[]{:S(2)}, u32[]{:S(2)}) collective-permute-start(bf16[160,256]{1,0:T(8,128)(2,1)S(1)} %pad_maximum_fusion.3), channel_id=1, source_target_pairs={{0,6},{1,7},{2,4},{3,5},{4,2},{5,3},{6,0},{7,1},{8,14},{9,15},{10,... | collective-permute-start | bytes 245768 | tf_op jit(solution)/shard_map/ppermute | solution.py:20
  8.2 0.3 collective-permute-start
  8.5 0.7 %convert.8 = bf16[16,64]{1,0:T(8,128)(2,1)S(1)} convert(s32[16,64]{1,0:T(8,128)} %param.13) | non-fusion elementwise | flops 1024 | bytes 6144 | tf_op jit(solution)/shard_map/convert.2
  9.2 0.8 %constant_dynamic-slice_fusion = bf16[128,256]{1,0:T(8,128)(2,1)S(1)} fusion(bf16[128,1024]{1,0:T(8,128)(2,1)} %param.16, s32[]{:T(128)S(6)} %select_n.32), kind=kLoop, calls=%fused_computation.45 | loop fusion | bytes 131076 | tf_op jit(solution)/shard_map/dynamic_slice | solution.py:346
  10.1 0.8 %constant_dynamic-slice_fusion.8 = (bf16[64,256]{1,0:T(8,128)(2,1)S(1)}, bf16[64,256]{1,0:T(8,128)(2,1)S(1)}, bf16[64,256]{1,0:T(8,128)(2,1)S(1)}, bf16[64,256]{1,0:T(8,128)(2,1)S(1)}) fusion(bf16[64,1024]{1,0:T(8,128)(2,1)} %param.14, s32[]{:T(128)S(6)} %select_n.32, s32[]{:T(128)S(6)} %select_n.35, s32[]{:T(128)S(6)} %select_n.34, s32[]{:T(128)S(6)} %select_n.33), kind=kLoop, calls=%fused_computation.53 | loop fusion | bytes 262160 | tf_op jit(solution)/shard_map/dynamic_slice | solution.py:346
  11.1 2.8 %collective-permute-done = bf16[160,256]{1,0:T(8,128)(2,1)S(1)} collective-permute-done((bf16[160,256]{1,0:T(8,128)(2,1)S(1)}, bf16[160,256]{1,0:T(8,128)(2,1)S(1)}, u32[]{:S(2)}, u32[]{:S(2)}) %collective-permute-start) | collective-permute-done | bytes 81952 | tf_op jit(solution)/shard_map/ppermute | solution.py:20
  14.2 1.6 %collective-permute-start.8 = (bf16[496,256]{1,0:T(8,128)(2,1)S(1)}, bf16[496,256]{1,0:T(8,128)(2,1)S(1)}, u32[]{:S(2)}, u32[]{:S(2)}) collective-permute-start(bf16[496,256]{1,0:T(8,128)(2,1)S(1)} %constant_dynamic-update-slice_fusion.refs_2_), channel_id=1, source_target_pairs={{0,16},{8,24},{16,0},{24,8},{1,17},{9,25},{17,1},{25,9},{2,18},{10... | collective-permute-start | bytes 761864 | tf_op jit(solution)/shard_map/ppermute | solution.py:34
  15.8 1.5 %collective-permute-start.7 = (bf16[496,256]{1,0:T(8,128)(2,1)S(1)}, bf16[496,256]{1,0:T(8,128)(2,1)S(1)}, u32[]{:S(2)}, u32[]{:S(2)}) collective-permute-start(bf16[496,256]{1,0:T(8,128)(2,1)S(1)} %constant_dynamic-update-slice_fusion.refs_2_), channel_id=1, source_target_pairs={{0,8},{8,0},{16,24},{24,16},{1,9},{9,1},{17,25},{25,17},{2,10},{10... | collective-permute-start | bytes 761864 | tf_op jit(solution)/shard_map/ppermute | solution.py:34
  17.2 0.3 collective-permute-start.6
  17.5 2.8 %collective-permute-start.5 = (bf16[192,256]{1,0:T(8,128)(2,1)S(1)}, bf16[192,256]{1,0:T(8,128)(2,1)S(1)}, u32[]{:S(2)}, u32[]{:S(2)}) collective-permute-start(bf16[192,256]{1,0:T(8,128)(2,1)S(1)} %pad_maximum_fusion.2), channel_id=1, source_target_pairs={{0,4},{1,5},{2,6},{3,7},{4,0},{5,1},{6,2},{7,3},{8,12},{9,13},{10,... | collective-permute-start | bytes 294920 | tf_op jit(solution)/shard_map/ppermute | solution.py:20
  20.3 1.3 %collective-permute-start.4 = (bf16[192,256]{1,0:T(8,128)(2,1)S(1)}, bf16[192,256]{1,0:T(8,128)(2,1)S(1)}, u32[]{:S(2)}, u32[]{:S(2)}) collective-permute-start(bf16[192,256]{1,0:T(8,128)(2,1)S(1)} %pad_maximum_fusion.2), channel_id=1, source_target_pairs={{0,6},{1,7},{2,4},{3,5},{4,2},{5,3},{6,0},{7,1},{8,14},{9,15},{10,... | collective-permute-start | bytes 294920 | tf_op jit(solution)/shard_map/ppermute | solution.py:20
  21.6 1.6 %collective-permute-done.6 = bf16[192,256]{1,0:T(8,128)(2,1)S(1)} collective-permute-done((bf16[192,256]{1,0:T(8,128)(2,1)S(1)}, bf16[192,256]{1,0:T(8,128)(2,1)S(1)}, u32[]{:S(2)}, u32[]{:S(2)}) %collective-permute-start.6) | collective-permute-done | bytes 98336 | tf_op jit(solution)/shard_map/ppermute | solution.py:20
  23.3 1.1 %collective-permute-start.9 = (bf16[304,256]{1,0:T(8,128)(2,1)S(1)}, bf16[304,256]{1,0:T(8,128)(2,1)}, u32[]{:S(2)}, u32[]{:S(2)}) collective-permute-start(bf16[304,256]{1,0:T(8,128)(2,1)S(1)} %get-tuple-element.91), channel_id=1, source_target_pairs={{0,24},{8,16},{16,8},{24,0},{1,25},{9,17},{17,9},{25,1},{2,26},{10... | collective-permute-start | bytes 466952 | tf_op jit(solution)/shard_map/ppermute | solution.py:34
  24.4 3.8 %collective-permute-done.5 = bf16[192,256]{1,0:T(8,128)(2,1)S(1)} collective-permute-done((bf16[192,256]{1,0:T(8,128)(2,1)S(1)}, bf16[192,256]{1,0:T(8,128)(2,1)S(1)}, u32[]{:S(2)}, u32[]{:S(2)}) %collective-permute-start.5) | collective-permute-done | bytes 98336 | tf_op jit(solution)/shard_map/ppermute | solution.py:20
  28.3 0.6 collective-permute-start.10
  28.9 0.1 collective-permute-start.13
  29.0 0.4 collective-permute-start.12
  29.4 0.1 collective-permute-done.9.refs_5_
  29.5 0.8 %dynamic-slice_convert_fusion = f32[256]{0:T(256)S(1)} fusion(bf16[1024]{0:T(1024)(128)(2,1)} %param.17, s32[]{:T(128)S(6)} %select_n.32), kind=kLoop, calls=%fused_computation.56 | loop fusion | flops 256 | bytes 1540 | tf_op jit(solution)/shard_map/reshape | solution.py:383
  30.3 0.1 copy.12.refs_12_.refs_8_
  30.4 1.1 %collective-permute-done.14.refs_11_ = bf16[304,256]{1,0:T(8,128)(2,1)} collective-permute-done((bf16[304,256]{1,0:T(8,128)(2,1)}, bf16[304,256]{1,0:T(8,128)(2,1)}, u32[]{:S(2)}, u32[]{:S(2)}) %collective-permute-start.14) | collective-permute-done | bytes 155680 | tf_op jit(solution)/shard_map/ppermute | solution.py:29
  31.5 7.2 %scores.1 = (bf16[1024,4096]{1,0:T(8,128)(2,1)S(1)}, bf16[256,4096]{1,0:T(8,128)(2,1)S(1)}, f32[32,128]{1,0:T(8,128)S(1)}, f32[4,8,128]{2,1,0:T(8,128)S(1)}, f32[4,8,128]{2,1,0:T(8,128)S(1)}) custom-call(bf16[4,128,256]{2,1,0:T(8,128)(2,1)S(1)} %pad_maximum_fusion.1.refs_0_, bf16[704,256]{1,0:T(8,128)(2,1)S(1)} %pad_maximum_fusion.refs_1_, ...), custom_call_target="tpu_custom_call" | custom-call | tf_op jit(solution)/shard_map/scores/pallas_call | solution.py:393
  38.7 1.2 %collective-permute-start.17 = (f32[32,128]{1,0:T(8,128)S(1)}, f32[32,128]{1,0:T(8,128)S(1)}, u32[]{:S(2)}, u32[]{:S(2)}) collective-permute-start(f32[32,128]{1,0:T(8,128)S(1)} %get-tuple-element.43.refs_0_), channel_id=1, source_target_pairs={{0,24},{8,16},{16,8},{24,0},{1,25},{9,17},{17,9},{25,1},{2,26},{10... | collective-permute-start | bytes 49160 | tf_op jit(solution)/shard_map/ppermute | solution.py:34
  39.9 0.9 %collective-permute-start.16 = (f32[32,128]{1,0:T(8,128)S(1)}, f32[32,128]{1,0:T(8,128)S(1)}, u32[]{:S(2)}, u32[]{:S(2)}) collective-permute-start(f32[32,128]{1,0:T(8,128)S(1)} %get-tuple-element.43.refs_0_), channel_id=1, source_target_pairs={{0,16},{8,24},{16,0},{24,8},{1,17},{9,25},{17,1},{25,9},{2,18},{10... | collective-permute-start | bytes 49160 | tf_op jit(solution)/shard_map/ppermute | solution.py:34
  40.8 1.5 %collective-permute-start.15 = (f32[32,128]{1,0:T(8,128)S(1)}, f32[32,128]{1,0:T(8,128)S(1)}, u32[]{:S(2)}, u32[]{:S(2)}) collective-permute-start(f32[32,128]{1,0:T(8,128)S(1)} %get-tuple-element.43.refs_0_), channel_id=1, source_target_pairs={{0,8},{8,0},{16,24},{24,16},{1,9},{9,1},{17,25},{25,17},{2,10},{10... | collective-permute-start | bytes 49160 | tf_op jit(solution)/shard_map/ppermute | solution.py:34
  42.2 1.1 %collective-permute-done.17.refs_3_ = f32[32,128]{1,0:T(8,128)S(1)} collective-permute-done((f32[32,128]{1,0:T(8,128)S(1)}, f32[32,128]{1,0:T(8,128)S(1)}, u32[]{:S(2)}, u32[]{:S(2)}) %collective-permute-start.17) | collective-permute-done | bytes 16416 | tf_op jit(solution)/shard_map/ppermute | solution.py:34
  43.4 0.2 collective-permute-done.16.refs_2_
  43.6 0.9 %collective-permute-done.15.refs_1_ = f32[32,128]{1,0:T(8,128)S(1)} collective-permute-done((f32[32,128]{1,0:T(8,128)S(1)}, f32[32,128]{1,0:T(8,128)S(1)}, u32[]{:S(2)}, u32[]{:S(2)}) %collective-permute-start.15) | collective-permute-done | bytes 16416 | tf_op jit(solution)/shard_map/ppermute | solution.py:34
  44.5 2.3 %gradient.1 = (bf16[256,4096]{1,0:T(8,128)(2,1)S(1)}, bf16[16,256]{1,0:T(8,128)(2,1)S(1)}, bf16[2,144,256]{2,1,0:T(8,128)(2,1)S(1)}, bf16[2,144,256]{2,1,0:T(8,128)(2,1)S(1)}) custom-call(f32[32,128]{1,0:T(8,128)S(1)} %get-tuple-element.43.refs_0_, f32[32,128]{1,0:T(8,128)S(1)} %collective-permute-done.15.refs_1_, ...), custom_call_target="tpu_custom_call" | custom-call | tf_op jit(solution)/shard_map/gradient/pallas_call | solution.py:450
  46.9 0.8 %gradient_rest.2 = (bf16[1,144,256]{2,1,0:T(8,128)(2,1)S(1)}, bf16[1,144,256]{2,1,0:T(8,128)(2,1)S(1)}) custom-call(bf16[1024,4096]{1,0:T(8,128)(2,1)S(1)} %get-tuple-element.42.refs_6_.refs_0_, bf16[256,4096]{1,0:T(8,128)(2,1)S(1)} %get-tuple-element.55.refs_1_, bf16[16,256]{1,0:T(8,128)(2,1)S(1)} %get-tuple-element.48.refs_2_), custom_call_target="tpu_custom_call" | custom-call | tf_op jit(solution)/shard_map/gradient_rest/pallas_call | solution.py:439
  47.6 0.6 collective-permute-start.18
  48.3 0.8 %gradient_rest.3 = (bf16[1,144,256]{2,1,0:T(8,128)(2,1)S(1)}, bf16[1,144,256]{2,1,0:T(8,128)(2,1)S(1)}) custom-call(bf16[1024,4096]{1,0:T(8,128)(2,1)S(1)} %get-tuple-element.42.refs_6_.refs_0_, bf16[256,4096]{1,0:T(8,128)(2,1)S(1)} %get-tuple-element.55.refs_1_, bf16[16,256]{1,0:T(8,128)(2,1)S(1)} %get-tuple-element.48.refs_2_), custom_call_target="tpu_custom_call" | custom-call | tf_op jit(solution)/shard_map/gradient_rest/pallas_call | solution.py:439
  49.1 0.4 collective-permute-start.20
  49.6 2.5 %collective-permute-start.21 = (bf16[144,256]{1,0:T(8,128)(2,1)S(1)}, bf16[144,256]{1,0:T(8,128)(2,1)S(1)}, u32[]{:S(2)}, u32[]{:S(2)}) collective-permute-start(bf16[144,256]{1,0:T(8,128)(2,1)S(1)} %get-tuple-element.63), channel_id=1, source_target_pairs={{0,6},{1,7},{2,4},{3,5},{4,2},{5,3},{6,0},{7,1},{8,14},{9,15},{10,... | collective-permute-start | bytes 221192 | tf_op jit(solution)/shard_map/ppermute | solution.py:20
  52.1 0.6 collective-permute-start.22
  52.7 1.3 %collective-permute-start.23 = (bf16[144,256]{1,0:T(8,128)(2,1)S(1)}, bf16[144,256]{1,0:T(8,128)(2,1)S(1)}, u32[]{:S(2)}, u32[]{:S(2)}) collective-permute-start(bf16[144,256]{1,0:T(8,128)(2,1)S(1)} %core_sum.5), channel_id=1, source_target_pairs={{0,2},{1,3},{2,0},{3,1},{4,6},{5,7},{6,4},{7,5},{8,10},{9,11},{10,... | collective-permute-start | bytes 221192 | tf_op jit(solution)/shard_map/ppermute | solution.py:20
  54.0 2.0 %collective-permute-done.21.refs_1_ = bf16[144,256]{1,0:T(8,128)(2,1)S(1)} collective-permute-done((bf16[144,256]{1,0:T(8,128)(2,1)S(1)}, bf16[144,256]{1,0:T(8,128)(2,1)S(1)}, u32[]{:S(2)}, u32[]{:S(2)}) %collective-permute-start.21) | collective-permute-done | bytes 73760 | tf_op jit(solution)/shard_map/ppermute | solution.py:20
  56.0 3.7 %collective-permute-done.22.refs_2_ = bf16[144,256]{1,0:T(8,128)(2,1)S(1)} collective-permute-done((bf16[144,256]{1,0:T(8,128)(2,1)S(1)}, bf16[144,256]{1,0:T(8,128)(2,1)S(1)}, u32[]{:S(2)}, u32[]{:S(2)}) %collective-permute-start.22) | collective-permute-done | bytes 73760 | tf_op jit(solution)/shard_map/ppermute | solution.py:20
  59.8 1.5 %collective-permute-start.26 = (bf16[144,256]{1,0:T(8,128)(2,1)S(1)}, bf16[144,256]{1,0:T(8,128)(2,1)S(1)}, u32[]{:S(2)}, u32[]{:S(2)}) collective-permute-start(bf16[144,256]{1,0:T(8,128)(2,1)S(1)} %z_sum.1.refs_0_), channel_id=1, source_target_pairs={{0,24},{8,16},{16,8},{24,0},{1,25},{9,17},{17,9},{25,1},{2,26},{10... | collective-permute-start | bytes 221192 | tf_op jit(solution)/shard_map/ppermute | solution.py:34
  61.3 1.5 %collective-permute-start.25 = (bf16[144,256]{1,0:T(8,128)(2,1)S(1)}, bf16[144,256]{1,0:T(8,128)(2,1)S(1)}, u32[]{:S(2)}, u32[]{:S(2)}) collective-permute-start(bf16[144,256]{1,0:T(8,128)(2,1)S(1)} %z_sum.1.refs_0_), channel_id=1, source_target_pairs={{0,16},{8,24},{16,0},{24,8},{1,17},{9,25},{17,1},{25,9},{2,18},{10... | collective-permute-start | bytes 221192 | tf_op jit(solution)/shard_map/ppermute | solution.py:34
  62.8 0.5 collective-permute-start.24
  63.3 2.2 %collective-permute-done.26.refs_3_ = bf16[144,256]{1,0:T(8,128)(2,1)S(1)} collective-permute-done((bf16[144,256]{1,0:T(8,128)(2,1)S(1)}, bf16[144,256]{1,0:T(8,128)(2,1)S(1)}, u32[]{:S(2)}, u32[]{:S(2)}) %collective-permute-start.26) | collective-permute-done | bytes 73760 | tf_op jit(solution)/shard_map/ppermute | solution.py:34
  65.5 0.6 collective-permute-done.25.refs_2_
  66.1 1.0 %collective-permute-done.24.refs_1_ = bf16[144,256]{1,0:T(8,128)(2,1)S(1)} collective-permute-done((bf16[144,256]{1,0:T(8,128)(2,1)S(1)}, bf16[144,256]{1,0:T(8,128)(2,1)S(1)}, u32[]{:S(2)}, u32[]{:S(2)}) %collective-permute-start.24) | collective-permute-done | bytes 73760 | tf_op jit(solution)/shard_map/ppermute | solution.py:34
  67.2 0.9 %finish.1 = (f32[128,1024]{1,0:T(8,128)}, f32[1,1024]{1,0:T(1,128)}, f32[1,1]{1,0:T(1,128)}) custom-call(bf16[144,256]{1,0:T(8,128)(2,1)S(1)} %z_sum.1.refs_0_, bf16[144,256]{1,0:T(8,128)(2,1)S(1)} %collective-permute-done.24.refs_1_, bf16[144,256]{1,0:T(8,128)(2,1)S(1)} %collective-permute-done.25.refs_2_, bf16[144,256]{1,0:T(8,128)(2,1)S(1)} %collective-permute-done.26.refs_3_), custom_call_target="tpu_custom_call" | custom-call | tf_op jit(solution)/shard_map/finish/pallas_call | solution.py:494
  (56 shorter events, 0.9 us)
Async XLA Ops:
  0.6 5.0 %copy-start = (bf16[1024,512]{1,0:T(8,128)(2,1)S(1)}, bf16[1024,512]{1,0:T(8,128)(2,1)}, u32[]{:S(2)}) copy-start(bf16[1024,512]{1,0:T(8,128)(2,1)} %param.9) | copy-start | bytes 3145732
  0.6 10.3 %copy-start.1 = (bf16[64,1024]{1,0:T(8,128)(2,1)S(1)}, bf16[64,1024]{1,0:T(8,128)(2,1)}, u32[]{:S(2)}) copy-start(bf16[64,1024]{1,0:T(8,128)(2,1)} %param.15) | copy-start | bytes 393220
  0.7 10.3 %copy-start.3 = (s32[16]{0:T(128)S(1)}, s32[16]{0:T(128)}, u32[]{:S(2)}) copy-start(s32[16]{0:T(128)} %param.12) | copy-start | bytes 196
  0.7 10.3 %copy-start.2 = (s32[16,64]{1,0:T(8,128)S(1)}, s32[16,64]{1,0:T(8,128)}, u32[]{:S(2)}) copy-start(s32[16,64]{1,0:T(8,128)} %param.11) | copy-start | bytes 12292
  1.6 12.3 %collective-permute-start.1 = (bf16[128,256]{1,0:T(8,128)(2,1)S(1)}, bf16[128,256]{1,0:T(8,128)(2,1)S(1)}, u32[]{:S(2)}, u32[]{:S(2)}) collective-permute-start(bf16[128,256]{1,0:T(8,128)(2,1)S(1)} %pad_maximum_fusion.4), channel_id=1, source_target_pairs={{0,4},{1,5},{2,6},{3,7},{4,0},{5,1},{6,2},{7,3},{8,12},{9,13},{10,... | collective-permute-start | bytes 196616 | tf_op jit(solution)/shard_map/ppermute | solution.py:20
  6.8 7.0 %collective-permute-start.2 = (bf16[160,256]{1,0:T(8,128)(2,1)S(1)}, bf16[160,256]{1,0:T(8,128)(2,1)S(1)}, u32[]{:S(2)}, u32[]{:S(2)}) collective-permute-start(bf16[160,256]{1,0:T(8,128)(2,1)S(1)} %pad_maximum_fusion.3), channel_id=1, source_target_pairs={{0,6},{1,7},{2,4},{3,5},{4,2},{5,3},{6,0},{7,1},{8,14},{9,15},{10,... | collective-permute-start | bytes 245768 | tf_op jit(solution)/shard_map/ppermute | solution.py:20
  8.2 5.6 %collective-permute-start = (bf16[160,256]{1,0:T(8,128)(2,1)S(1)}, bf16[160,256]{1,0:T(8,128)(2,1)S(1)}, u32[]{:S(2)}, u32[]{:S(2)}) collective-permute-start(bf16[160,256]{1,0:T(8,128)(2,1)S(1)} %pad_maximum_fusion.3), channel_id=1, source_target_pairs={{0,2},{1,3},{2,0},{3,1},{4,6},{5,7},{6,4},{7,5},{8,10},{9,11},{10,... | collective-permute-start | bytes 245768 | tf_op jit(solution)/shard_map/ppermute | solution.py:20
  14.0 3.2 %collective-permute-start.3 = (bf16[496,256]{1,0:T(8,128)(2,1)S(1)}, bf16[496,256]{1,0:T(8,128)(2,1)S(1)}, u32[]{:S(2)}, u32[]{:S(2)}) collective-permute-start(bf16[496,256]{1,0:T(8,128)(2,1)S(1)} %constant_dynamic-update-slice_fusion.refs_2_), channel_id=1, source_target_pairs={{0,1},{1,0},{2,3},{3,2},{4,5},{5,4},{6,7},{7,6},{8,9},{9,8},{10,11... | collective-permute-start | bytes 761864 | tf_op jit(solution)/shard_map/ppermute | solution.py:29
  14.2 14.7 %collective-permute-start.8 = (bf16[496,256]{1,0:T(8,128)(2,1)S(1)}, bf16[496,256]{1,0:T(8,128)(2,1)S(1)}, u32[]{:S(2)}, u32[]{:S(2)}) collective-permute-start(bf16[496,256]{1,0:T(8,128)(2,1)S(1)} %constant_dynamic-update-slice_fusion.refs_2_), channel_id=1, source_target_pairs={{0,16},{8,24},{16,0},{24,8},{1,17},{9,25},{17,1},{25,9},{2,18},{10... | collective-permute-start | bytes 761864 | tf_op jit(solution)/shard_map/ppermute | solution.py:34
  15.8 13.2 %collective-permute-start.7 = (bf16[496,256]{1,0:T(8,128)(2,1)S(1)}, bf16[496,256]{1,0:T(8,128)(2,1)S(1)}, u32[]{:S(2)}, u32[]{:S(2)}) collective-permute-start(bf16[496,256]{1,0:T(8,128)(2,1)S(1)} %constant_dynamic-update-slice_fusion.refs_2_), channel_id=1, source_target_pairs={{0,8},{8,0},{16,24},{24,16},{1,9},{9,1},{17,25},{25,17},{2,10},{10... | collective-permute-start | bytes 761864 | tf_op jit(solution)/shard_map/ppermute | solution.py:34
  17.2 6.0 %collective-permute-start.6 = (bf16[192,256]{1,0:T(8,128)(2,1)S(1)}, bf16[192,256]{1,0:T(8,128)(2,1)S(1)}, u32[]{:S(2)}, u32[]{:S(2)}) collective-permute-start(bf16[192,256]{1,0:T(8,128)(2,1)S(1)} %pad_maximum_fusion.2), channel_id=1, source_target_pairs={{0,2},{1,3},{2,0},{3,1},{4,6},{5,7},{6,4},{7,5},{8,10},{9,11},{10,... | collective-permute-start | bytes 294920 | tf_op jit(solution)/shard_map/ppermute | solution.py:20
  17.5 10.7 %collective-permute-start.5 = (bf16[192,256]{1,0:T(8,128)(2,1)S(1)}, bf16[192,256]{1,0:T(8,128)(2,1)S(1)}, u32[]{:S(2)}, u32[]{:S(2)}) collective-permute-start(bf16[192,256]{1,0:T(8,128)(2,1)S(1)} %pad_maximum_fusion.2), channel_id=1, source_target_pairs={{0,4},{1,5},{2,6},{3,7},{4,0},{5,1},{6,2},{7,3},{8,12},{9,13},{10,... | collective-permute-start | bytes 294920 | tf_op jit(solution)/shard_map/ppermute | solution.py:20
  20.3 7.9 %collective-permute-start.4 = (bf16[192,256]{1,0:T(8,128)(2,1)S(1)}, bf16[192,256]{1,0:T(8,128)(2,1)S(1)}, u32[]{:S(2)}, u32[]{:S(2)}) collective-permute-start(bf16[192,256]{1,0:T(8,128)(2,1)S(1)} %pad_maximum_fusion.2), channel_id=1, source_target_pairs={{0,6},{1,7},{2,4},{3,5},{4,2},{5,3},{6,0},{7,1},{8,14},{9,15},{10,... | collective-permute-start | bytes 294920 | tf_op jit(solution)/shard_map/ppermute | solution.py:20
  23.3 6.2 %collective-permute-start.9 = (bf16[304,256]{1,0:T(8,128)(2,1)S(1)}, bf16[304,256]{1,0:T(8,128)(2,1)}, u32[]{:S(2)}, u32[]{:S(2)}) collective-permute-start(bf16[304,256]{1,0:T(8,128)(2,1)S(1)} %get-tuple-element.91), channel_id=1, source_target_pairs={{0,24},{8,16},{16,8},{24,0},{1,25},{9,17},{17,9},{25,1},{2,26},{10... | collective-permute-start | bytes 466952 | tf_op jit(solution)/shard_map/ppermute | solution.py:34
  28.2 3.3 %collective-permute-start.11 = (bf16[704,256]{1,0:T(8,128)(2,1)S(1)}, bf16[704,256]{1,0:T(8,128)(2,1)S(1)}, u32[]{:S(2)}, u32[]{:S(2)}) collective-permute-start(bf16[704,256]{1,0:T(8,128)(2,1)S(1)} %pad_maximum_fusion.refs_1_), channel_id=1, source_target_pairs={{0,1},{1,0},{2,3},{3,2},{4,5},{5,4},{6,7},{7,6},{8,9},{9,8},{10,11... | collective-permute-start | bytes 1081352 | tf_op jit(solution)/shard_map/ppermute | solution.py:29
  28.3 2.1 %collective-permute-start.10 = (bf16[4,128,256]{2,1,0:T(8,128)(2,1)S(1)}, bf16[4,128,256]{2,1,0:T(8,128)(2,1)S(1)}, u32[]{:S(2)}, u32[]{:S(2)}) collective-permute-start(bf16[4,128,256]{2,1,0:T(8,128)(2,1)S(1)} %pad_maximum_fusion.1.refs_0_), channel_id=1, source_target_pairs={{0,1},{1,0},{2,3},{3,2},{4,5},{5,4},{6,7},{7,6},{8,9},{9,8},{10,11... | collective-permute-start | bytes 786440 | tf_op jit(solution)/shard_map/ppermute | solution.py:29
  28.9 2.6 %collective-permute-start.13 = (bf16[496,256]{1,0:T(8,128)(2,1)S(1)}, bf16[496,256]{1,0:T(8,128)(2,1)}, u32[]{:S(2)}, u32[]{:S(2)}) collective-permute-start(bf16[496,256]{1,0:T(8,128)(2,1)S(1)} %collective-permute-done.8.refs_4_), channel_id=1, source_target_pairs={{0,1},{1,0},{2,3},{3,2},{4,5},{5,4},{6,7},{7,6},{8,9},{9,8},{10,11... | collective-permute-start | bytes 761864 | tf_op jit(solution)/shard_map/ppermute | solution.py:29
  29.0 2.5 %collective-permute-start.12 = (bf16[496,256]{1,0:T(8,128)(2,1)S(1)}, bf16[496,256]{1,0:T(8,128)(2,1)}, u32[]{:S(2)}, u32[]{:S(2)}) collective-permute-start(bf16[496,256]{1,0:T(8,128)(2,1)S(1)} %collective-permute-done.7.refs_3_), channel_id=1, source_target_pairs={{0,1},{1,0},{2,3},{3,2},{4,5},{5,4},{6,7},{7,6},{8,9},{9,8},{10,11... | collective-permute-start | bytes 761864 | tf_op jit(solution)/shard_map/ppermute | solution.py:29
  29.5 2.0 %collective-permute-start.14 = (bf16[304,256]{1,0:T(8,128)(2,1)}, bf16[304,256]{1,0:T(8,128)(2,1)}, u32[]{:S(2)}, u32[]{:S(2)}) collective-permute-start(bf16[304,256]{1,0:T(8,128)(2,1)} %collective-permute-done.9.refs_5_), channel_id=1, source_target_pairs={{0,1},{1,0},{2,3},{3,2},{4,5},{5,4},{6,7},{7,6},{8,9},{9,8},{10,11... | collective-permute-start | bytes 466952 | tf_op jit(solution)/shard_map/ppermute | solution.py:29
  38.7 4.7 %collective-permute-start.17 = (f32[32,128]{1,0:T(8,128)S(1)}, f32[32,128]{1,0:T(8,128)S(1)}, u32[]{:S(2)}, u32[]{:S(2)}) collective-permute-start(f32[32,128]{1,0:T(8,128)S(1)} %get-tuple-element.43.refs_0_), channel_id=1, source_target_pairs={{0,24},{8,16},{16,8},{24,0},{1,25},{9,17},{17,9},{25,1},{2,26},{10... | collective-permute-start | bytes 49160 | tf_op jit(solution)/shard_map/ppermute | solution.py:34
  39.9 3.7 %collective-permute-start.16 = (f32[32,128]{1,0:T(8,128)S(1)}, f32[32,128]{1,0:T(8,128)S(1)}, u32[]{:S(2)}, u32[]{:S(2)}) collective-permute-start(f32[32,128]{1,0:T(8,128)S(1)} %get-tuple-element.43.refs_0_), channel_id=1, source_target_pairs={{0,16},{8,24},{16,0},{24,8},{1,17},{9,25},{17,1},{25,9},{2,18},{10... | collective-permute-start | bytes 49160 | tf_op jit(solution)/shard_map/ppermute | solution.py:34
  40.8 3.7 %collective-permute-start.15 = (f32[32,128]{1,0:T(8,128)S(1)}, f32[32,128]{1,0:T(8,128)S(1)}, u32[]{:S(2)}, u32[]{:S(2)}) collective-permute-start(f32[32,128]{1,0:T(8,128)S(1)} %get-tuple-element.43.refs_0_), channel_id=1, source_target_pairs={{0,8},{8,0},{16,24},{24,16},{1,9},{9,1},{17,25},{25,17},{2,10},{10... | collective-permute-start | bytes 49160 | tf_op jit(solution)/shard_map/ppermute | solution.py:34
  46.8 1.4 %collective-permute-start.19 = (bf16[2,144,256]{2,1,0:T(8,128)(2,1)S(1)}, bf16[2,144,256]{2,1,0:T(8,128)(2,1)S(1)}, u32[]{:S(2)}, u32[]{:S(2)}) collective-permute-start(bf16[2,144,256]{2,1,0:T(8,128)(2,1)S(1)} %get-tuple-element.52), channel_id=1, source_target_pairs={{0,1},{1,0},{2,3},{3,2},{4,5},{5,4},{6,7},{7,6},{8,9},{9,8},{10,11... | collective-permute-start | bytes 442376 | tf_op jit(solution)/shard_map/ppermute | solution.py:29
  47.6 1.5 %collective-permute-start.18 = (bf16[1,144,256]{2,1,0:T(8,128)(2,1)S(1)}, bf16[1,144,256]{2,1,0:T(8,128)(2,1)S(1)}, u32[]{:S(2)}, u32[]{:S(2)}) collective-permute-start(bf16[1,144,256]{2,1,0:T(8,128)(2,1)S(1)} %get-tuple-element.50), channel_id=1, source_target_pairs={{0,1},{1,0},{2,3},{3,2},{4,5},{5,4},{6,7},{7,6},{8,9},{9,8},{10,11... | collective-permute-start | bytes 221192 | tf_op jit(solution)/shard_map/ppermute | solution.py:29
  49.1 4.8 %collective-permute-start.20 = (bf16[1,144,256]{2,1,0:T(8,128)(2,1)S(1)}, bf16[1,144,256]{2,1,0:T(8,128)(2,1)S(1)}, u32[]{:S(2)}, u32[]{:S(2)}) collective-permute-start(bf16[1,144,256]{2,1,0:T(8,128)(2,1)S(1)} %get-tuple-element.58), channel_id=1, source_target_pairs={{0,1},{1,0},{2,3},{3,2},{4,5},{5,4},{6,7},{7,6},{8,9},{9,8},{10,11... | collective-permute-start | bytes 221192 | tf_op jit(solution)/shard_map/ppermute | solution.py:29
  49.6 6.4 %collective-permute-start.21 = (bf16[144,256]{1,0:T(8,128)(2,1)S(1)}, bf16[144,256]{1,0:T(8,128)(2,1)S(1)}, u32[]{:S(2)}, u32[]{:S(2)}) collective-permute-start(bf16[144,256]{1,0:T(8,128)(2,1)S(1)} %get-tuple-element.63), channel_id=1, source_target_pairs={{0,6},{1,7},{2,4},{3,5},{4,2},{5,3},{6,0},{7,1},{8,14},{9,15},{10,... | collective-permute-start | bytes 221192 | tf_op jit(solution)/shard_map/ppermute | solution.py:20
  52.1 7.6 %collective-permute-start.22 = (bf16[144,256]{1,0:T(8,128)(2,1)S(1)}, bf16[144,256]{1,0:T(8,128)(2,1)S(1)}, u32[]{:S(2)}, u32[]{:S(2)}) collective-permute-start(bf16[144,256]{1,0:T(8,128)(2,1)S(1)} %get-tuple-element.64), channel_id=1, source_target_pairs={{0,4},{1,5},{2,6},{3,7},{4,0},{5,1},{6,2},{7,3},{8,12},{9,13},{10,... | collective-permute-start | bytes 221192 | tf_op jit(solution)/shard_map/ppermute | solution.py:20
  52.7 7.0 %collective-permute-start.23 = (bf16[144,256]{1,0:T(8,128)(2,1)S(1)}, bf16[144,256]{1,0:T(8,128)(2,1)S(1)}, u32[]{:S(2)}, u32[]{:S(2)}) collective-permute-start(bf16[144,256]{1,0:T(8,128)(2,1)S(1)} %core_sum.5), channel_id=1, source_target_pairs={{0,2},{1,3},{2,0},{3,1},{4,6},{5,7},{6,4},{7,5},{8,10},{9,11},{10,... | collective-permute-start | bytes 221192 | tf_op jit(solution)/shard_map/ppermute | solution.py:20
  59.8 5.7 %collective-permute-start.26 = (bf16[144,256]{1,0:T(8,128)(2,1)S(1)}, bf16[144,256]{1,0:T(8,128)(2,1)S(1)}, u32[]{:S(2)}, u32[]{:S(2)}) collective-permute-start(bf16[144,256]{1,0:T(8,128)(2,1)S(1)} %z_sum.1.refs_0_), channel_id=1, source_target_pairs={{0,24},{8,16},{16,8},{24,0},{1,25},{9,17},{17,9},{25,1},{2,26},{10... | collective-permute-start | bytes 221192 | tf_op jit(solution)/shard_map/ppermute | solution.py:34
  61.3 4.8 %collective-permute-start.25 = (bf16[144,256]{1,0:T(8,128)(2,1)S(1)}, bf16[144,256]{1,0:T(8,128)(2,1)S(1)}, u32[]{:S(2)}, u32[]{:S(2)}) collective-permute-start(bf16[144,256]{1,0:T(8,128)(2,1)S(1)} %z_sum.1.refs_0_), channel_id=1, source_target_pairs={{0,16},{8,24},{16,0},{24,8},{1,17},{9,25},{17,1},{25,9},{2,18},{10... | collective-permute-start | bytes 221192 | tf_op jit(solution)/shard_map/ppermute | solution.py:34
  62.8 4.4 %collective-permute-start.24 = (bf16[144,256]{1,0:T(8,128)(2,1)S(1)}, bf16[144,256]{1,0:T(8,128)(2,1)S(1)}, u32[]{:S(2)}, u32[]{:S(2)}) collective-permute-start(bf16[144,256]{1,0:T(8,128)(2,1)S(1)} %z_sum.1.refs_0_), channel_id=1, source_target_pairs={{0,8},{8,0},{16,24},{24,16},{1,9},{9,1},{17,25},{25,17},{2,10},{10... | collective-permute-start | bytes 221192 | tf_op jit(solution)/shard_map/ppermute | solution.py:34

commit v4 on v3

--- a/solution.py
+++ b/solution.py
@@ -67,16 +67,15 @@
     return pl.ds(pl.multiple_of(((first // cols) ^ region) * cols + first % cols, rows), rows)
 
 
-def score_kernel(n_region, n_z, blk, slots, *refs):
+def score_kernel(n_region, n_z, blk, *refs):
     half = 2 + n_region
     mine, other, rest = refs[:half], refs[half : 2 * half], refs[2 * half :]
-    w_out, first_out, act_out, score_out, ids, flows, feat, own, w_in, w_mid, w_mid_t, table, tables, plain = rest
+    w_out, first_out, act_out, score_out, win_out, feat, own, w_in, w_mid, w_mid_t, anchors, dests = rest
     step = pl.program_id(0)
     region = lax.axis_index("region")
     shard = lax.axis_index("shard")
     z, core = shard // 2, shard % 2
     window = (2 * REACH + 1) * blk
-    lines = blk * slots // 128
     hidden, cols = w_mid.shape
     parts = feat.shape[1] // cols
 
@@ -87,7 +86,7 @@
         steps = next_steps(n_z)
         feat_rows = (1 + len(steps)) * parts * blk
         slot_row = dest_rows + feat_rows
-        slot_rows = blk if cols >= 2 * slots else 2 * blk
+        slot_rows = -(-window // cols) * blk
         anchor_base = slot_row + slot_rows
         for source, core_at in ((mine, core), (other, 1 - core)):
             raw, mids, planes = source[0], source[1], source[2:]
@@ -96,7 +95,7 @@
                 shard_at = 2 * (z ^ j) + core_at
                 at = pl.ds(pl.multiple_of(shard_at * raw_cut, raw_cut), raw_cut)
                 mid = rows_mid + (n_z - 1 - j) * (rows_mid + raw_cut) if j > 0 else 0
-                w_mid[unit_rows(shard_at, rows_mid, cols, region), :] = mids[mid : mid + rows_mid, :]
+                w_mid[unit_rows(shard_at, rows_mid, cols, z), :] = mids[mid : mid + rows_mid, :]
                 for i in range(n_region):
                     base = (j - 1) * raw_cut
                     if j == 0:
@@ -110,7 +109,6 @@
                         w_in[i, at, cols:] = planes[i][base : base + raw_cut, :]
         one = identity(cols)
         w_mid_t[...] = turned(one, w_mid[...])
-        left = lax.broadcasted_iota(jnp.int32, (lines, 128), 1) < slots
         below_at = sum(jnp.where((z ^ (z - 1)) >= j, 1, 0) for j in steps)
         above_at = sum(jnp.where((z ^ (z + 1)) >= j, 1, 0) for j in steps)
         for i in range(n_region):
@@ -125,106 +123,79 @@
                 for k, part in enumerate((near[below, :], before, near[here, :], after, near[above, :])):
                     feat[i * window + k * blk : i * window + (k + 1) * blk, lanes] = part
                 own[i * blk : (i + 1) * blk, lanes] = near[here, :]
-            if slot_rows == blk:
-                plain[...] = near[slot_row : slot_row + blk, : 2 * slots].astype(F32)
-            else:
-                plain[:, :slots] = near[slot_row : slot_row + blk, :slots].astype(F32)
-                plain[:, slots:] = near[slot_row + blk : slot_row + 2 * blk, :slots].astype(F32)
-            even = plain[pl.ds(0, lines, stride=2), :]
-            odd = plain[pl.ds(1, lines, stride=2), :]
-            ids[i] = jnp.where(left, even, pltpu.roll(odd, slots, 1))
-            flows[i] = jnp.where(left, pltpu.roll(even, slots, 1), odd)
-        for k in range(n_region):
-            lanes = slice(k * cols, (k + 1) * cols)
-            high, low = split(jnp.dot(feat[...], w_in[k, :, cols:], preferred_element_type=F32))
-            high_a, low_a = split(jnp.dot(own[...], w_in[k, :, :cols], preferred_element_type=F32))
-            for i in range(n_region):
-                table[i, :window, lanes] = high[i * window : (i + 1) * window]
-                table[i, window : 2 * window, lanes] = low[i * window : (i + 1) * window]
-                table[i, 2 * window : 2 * window + blk, lanes] = high_a[i * blk : (i + 1) * blk]
-                table[i, 2 * window + blk :, lanes] = low_a[i * blk : (i + 1) * blk]
-        wide = one if cols == 256 else identity(256)
+            spans = [
+                near[slot_row + at : slot_row + at + blk, : min(cols, window - at // blk * cols)].astype(F32)
+                for at in range(0, slot_rows, blk)
+            ]
+            win_out[i] = jnp.concatenate(spans + [jnp.zeros((blk, 128 - window), F32)], axis=1)
         for i in range(n_region):
-            for k in range(0, hidden, 256):
-                tables[i, k : k + 256, :] = turned(wide, table[i, :, k : k + 256])
+            at = region ^ i ^ z
+            dests[at] = jnp.dot(feat[...], w_in[i, :, cols:], preferred_element_type=F32)
+            anchors[at] = jnp.dot(own[...], w_in[i, :, :cols], preferred_element_type=F32)
 
     group = 8
-    pairs = group * slots
-    spread = pairs // 128
-    dest_row = lax.broadcasted_iota(jnp.int32, (2 * window, pairs), 0)
-    dest_row = jnp.where(dest_row >= window, dest_row - window, dest_row).astype(F32)
-    anchor_row = lax.broadcasted_iota(jnp.int32, (2 * blk, pairs), 0)
-    anchor_row = jnp.where(anchor_row >= blk, anchor_row - blk, anchor_row)
-    anchor_lane = lax.broadcasted_iota(jnp.int32, (2 * blk, pairs), 1) // slots
+    pairs = group * window
     weight = w_out[...]
-    for n in range(first_out.shape[1] // (blk * slots)):
-        chosen = ids[step + n]
-        lookup = tables[step + n]
-        for c in range(blk // group):
-            spot = jnp.concatenate([chosen[c * spread + k : c * spread + k + 1, :] for k in range(spread)], axis=1)
-            dest_hot = jnp.where(dest_row == spot, 1.0, 0.0)
-            anchor_hot = jnp.where(anchor_row == anchor_lane + c * group, 1.0, 0.0)
-            onehot = jnp.concatenate([dest_hot, anchor_hot], axis=0).astype(BF)
-            first = jnp.maximum(jnp.dot(lookup, onehot, preferred_element_type=F32).astype(BF), 0)
-            at = slice(n * blk * slots + c * pairs, n * blk * slots + (c + 1) * pairs)
-            first_out[:, at] = first
-            active = jnp.maximum(jnp.dot(w_mid_t[...], first, preferred_element_type=F32), 0.0)
-            act_out[:, at] = active.astype(BF)
+    for n in range(first_out.shape[0] // (blk * window)):
+        reach_at = pl.ds(pl.multiple_of((step + n) * window, window), window)
+        own_at = pl.ds(pl.multiple_of((step + n) * blk, blk), blk)
+        for c in range(0, blk, group):
+            base = (n * blk + c) * window
+            for k in range(n_region):
+                dest = dests[k, reach_at, :]
+                line = anchors[k, own_at, :]
+                for a in range(group):
+                    total = dest + line[c + a : c + a + 1, :]
+                    at = slice(base + a * window, base + (a + 1) * window)
+                    first_out[at, k * cols : (k + 1) * cols] = jnp.maximum(total.astype(BF), 0)
+            second = lax.dot_general(
+                w_mid_t[...], first_out[base : base + pairs, :], (((1,), (1,)), ((), ())), preferred_element_type=F32
+            )
+            active = jnp.maximum(second, 0.0)
+            act_out[:, base : base + pairs] = active.astype(BF)
             score = jnp.sum(active * weight, axis=0, keepdims=True)
-            for k in range(spread):
-                row = n * lines + c * spread + k
-                score_out[row : row + 1, :] = score[:, k * 128 : (k + 1) * 128]
-
-
-def target_rows(first, targets, rows, cols):
-    z = lax.axis_index("shard") // 2
-    region = lax.axis_index("region")
-    return jnp.concatenate(
-        [first[unit_rows(z ^ j, 2 * rows, cols, region), :] for j in targets], axis=0
-    )
-
-
-def put_blocks(grad, tail, keep, send):
+            for a in range(group):
+                row = n * blk + c + a
+                score_out[row : row + 1, :] = jnp.concatenate(
+                    [score[:, a * window : (a + 1) * window], jnp.zeros((1, 128 - window), F32)], axis=1
+                )
+
+
+def add_targets(grad, pre, first, targets, width):
+    for n, j in enumerate(targets):
+        grad[n] += jnp.dot(pre[...], first[:, j * width : (j + 1) * width], preferred_element_type=F32)
+
+
+def put_blocks(grad, turn, tail, keep, send):
     rows = keep.shape[1] - TAIL
     core = lax.axis_index("shard") % 2
     for n in range(keep.shape[0]):
+        turn[n] = grad[n].T
         for target, core_at in ((keep, core), (send, 1 - core)):
-            at = pl.ds(pl.multiple_of((2 * n + core_at) * rows, rows), rows)
-            target[n, :rows, :] = grad[at, :].astype(BF)
+            target[n, :rows, :] = turn[n, pl.ds(pl.multiple_of(core_at * rows, rows), rows), :].astype(BF)
             target[n, rows:, :] = tail
 
 
 def rest_kernel(targets, *refs):
-    first, pre, tail, keep, send, grad = refs
-    rows = keep.shape[1] - TAIL
-    step = pl.program_id(0)
-    part = lax.dot_general(
-        target_rows(first, targets, rows, pre.shape[0]),
-        pre[...],
-        (((1,), (1,)), ((), ())),
-        preferred_element_type=F32,
-    )
-
-    @pl.when(step == 0)
-    def begin():
-        grad[...] = part
-
-    @pl.when(step > 0)
-    def more():
-        grad[...] += part
-
-    @pl.when(step == pl.num_programs(0) - 1)
+    first, pre, tail, keep, send, grad, turn = refs
+
+    @pl.when(pl.program_id(0) == 0)
+    def clear():
+        grad[...] = jnp.zeros_like(grad)
+
+    add_targets(grad, pre, first, targets, grad.shape[2])
+
+    @pl.when(pl.program_id(0) == pl.num_programs(0) - 1)
     def finish():
-        put_blocks(grad, tail[...], keep, send)
-
-
-def grad_kernel(n_region, targets, slots, *refs):
+        put_blocks(grad, turn, tail[...], keep, send)
+
+
+def grad_kernel(n_region, targets, window, *refs):
     scores, rest = refs[:n_region], refs[n_region:]
-    ids, flows, first, act, w_out, pre_out, tail_out, keep, send, grad, gout, sums = rest
+    win, first, act, w_out, pre_out, tail_out, keep, send, grad, turn, gout, sums = rest
     step = pl.program_id(0)
     cols = act.shape[0]
-    rows = keep.shape[1] - TAIL
-    lines, lanes = ids.shape[1:]
+    blk = win.shape[1]
 
     @pl.when(step == 0)
     def clear():
@@ -232,44 +203,39 @@
         gout[...] = jnp.zeros_like(gout)
         sums[...] = jnp.zeros_like(sums)
 
-    left = lax.broadcasted_iota(jnp.int32, (lines, lanes), 1) < slots
-
-    def halves(reduce, value, rest):
-        low = reduce(jnp.where(left, value, rest), axis=1, keepdims=True)
-        high = reduce(jnp.where(left, rest, value), axis=1, keepdims=True)
-        return jnp.where(left, low, high)
-
-    weight = jnp.broadcast_to(w_out[...], (cols, lanes))
+    weight = jnp.broadcast_to(w_out[...], (cols, 128))
     gained = gout[...]
     trips, numer = sums[0], sums[1]
-    for n in range(act.shape[1] // (lines * lanes)):
-        score = scores[0][n * lines : (n + 1) * lines, :]
+    group = 8
+    for n in range(act.shape[1] // (blk * window)):
+        score = scores[0][n * blk : (n + 1) * blk, :]
         for k in range(1, n_region):
-            at = (n ^ k) * lines if scores[k].shape[0] > lines else 0
-            score = score + scores[k][at : at + lines, :]
-        valid = ids[step + n] >= 0
-        top = halves(jnp.max, jnp.where(valid, score, -jnp.inf), -jnp.inf)
+            at = (n ^ k) * blk if scores[k].shape[0] > blk else 0
+            score = score + scores[k][at : at + blk, :]
+        table = win[step + n]
+        valid = table > 0
+        flow = jnp.where(valid, table - 1.0, 0.0)
+        top = jnp.max(jnp.where(valid, score, -jnp.inf), axis=1, keepdims=True)
         expo = jnp.where(valid, jnp.exp(score - top), 0.0)
-        mass = halves(jnp.sum, expo, 0.0)
+        mass = jnp.sum(expo, axis=1, keepdims=True)
         probs = expo / mass
         logp = score - top - jnp.log(mass)
-        flow = flows[step + n]
-        anchor_total = halves(jnp.sum, flow, 0.0)
+        anchor_total = jnp.sum(flow, axis=1, keepdims=True)
         sgrad = jnp.where(valid, probs * anchor_total - flow, 0.0)
         trips = trips + flow
         numer = numer - jnp.where(valid, flow * logp, 0.0)
-        for q in range(lines):
-            line = sgrad[q : q + 1, :]
-            at = slice((n * lines + q) * lanes, (n * lines + q + 1) * lanes)
-            active = act[:, at].astype(F32)
-            gained = gained + active * line
-            pre_out[:, at] = jnp.where(active > 0, weight * line, 0.0).astype(BF)
+        for c in range(0, blk, group):
+            wide = jnp.concatenate([sgrad[c + a : c + a + 1, :window] for a in range(group)], axis=1)
+            for q in range(0, group * window, 128):
+                line = wide[:, q : q + 128]
+                at = slice((n * blk + c) * window + q, (n * blk + c) * window + q + 128)
+                active = act[:, at].astype(F32)
+                gained = gained + active * line
+                pre_out[:, at] = jnp.where(active > 0, weight * line, 0.0).astype(BF)
     gout[...] = gained
     sums[0] = trips
     sums[1] = numer
-    grad[...] += lax.dot_general(
-        target_rows(first, targets, rows, cols), pre_out[...], (((1,), (1,)), ((), ())), preferred_element_type=F32
-    )
+    add_targets(grad, pre_out, first, targets, grad.shape[2])
 
     @pl.when(step == pl.num_programs(0) - 1)
     def finish():
@@ -281,7 +247,7 @@
         stats = jnp.where(lane == 0, total, jnp.where(lane == 1, numer, 0.0))
         tail = pack_tail(jnp.where(row == 0, out, jnp.where(row == 1, stats, 0.0)))
         tail_out[...] = tail
-        put_blocks(grad, tail, keep, send)
+        put_blocks(grad, turn, tail, keep, send)
 
 
 def core_sum_kernel(keep, received, *outs):
@@ -337,9 +303,8 @@
     rows_in = w_anchor.shape[0]
     depth = rows_in * n_shard
     cols = hidden // n_region
-    pairs = blk * slots
-    lines = pairs // 128
     window = (2 * REACH + 1) * blk
+    pairs = blk * window
     region = lax.axis_index("region")
 
     def cut(array, i):
@@ -363,8 +328,10 @@
 
     spot = neighbors % (blk * n_shard) - (lax.axis_index("shard") - REACH) * blk
     valid = jnp.arange(slots, dtype=jnp.int32)[None, :] < counts[:, None]
-    slot_table = jnp.concatenate([jnp.where(valid, spot, -1), flows], axis=1 if cols >= 2 * slots else 0).astype(BF)
-    slot_table = jnp.pad(slot_table, ((0, 0), (0, cols - slot_table.shape[1])))
+    held_by = (spot[:, :, None] == jnp.arange(window, dtype=jnp.int32)) & valid[:, :, None]
+    slot_table = jnp.sum(jnp.where(held_by, flows[:, :, None] + 1, 0), axis=1).astype(BF)
+    slot_table = jnp.pad(slot_table, ((0, 0), (0, -window % cols)))
+    slot_table = jnp.concatenate([slot_table[:, k : k + cols] for k in range(0, slot_table.shape[1], cols)], axis=0)
 
     held = 2 * rows_in
     around = [features] + [from_z[j - 1][held:] for j in next_steps(n_z)]
@@ -385,32 +352,32 @@
     resident = 2 * hidden * n_region * pairs <= 12 * MIB
 
     steps = 1 if resident else n_region
-    by_lines = VMEM if resident else pl.BlockSpec((lines, 128), lambda i: (i, 0))
+    by_anchors = VMEM if resident else pl.BlockSpec((blk, 128), lambda i: (i, 0))
 
     def by_pairs(rows):
         return VMEM if resident else pl.BlockSpec((rows, pairs), lambda i: (0, i))
 
-    first, act, score, ids, flow = pl.pallas_call(
-        functools.partial(score_kernel, n_region, n_z, blk, slots),
+    pair_rows = VMEM if resident else pl.BlockSpec((pairs, hidden), lambda i: (i, 0))
+
+    first, act, score, win = pl.pallas_call(
+        functools.partial(score_kernel, n_region, n_z, blk),
         grid=(steps,),
         in_specs=[VMEM] * (2 * len(mine) + 1),
-        out_specs=[by_pairs(hidden), by_pairs(cols), by_lines, VMEM, VMEM],
+        out_specs=[pair_rows, by_pairs(cols), by_anchors, VMEM],
         scratch_shapes=[
             pltpu.VMEM((n_region * window, depth), BF),
             pltpu.VMEM((n_region * blk, depth), BF),
             pltpu.VMEM((n_region, depth, 2 * cols), BF),
             pltpu.VMEM((hidden, cols), BF),
             pltpu.VMEM((cols, hidden), BF),
-            pltpu.VMEM((n_region, 2 * (window + blk), hidden), BF),
-            pltpu.VMEM((n_region, hidden, 2 * (window + blk)), BF),
-            pltpu.VMEM((blk, 2 * slots), F32),
+            pltpu.VMEM((n_region, n_region * blk, cols), F32),
+            pltpu.VMEM((n_region, n_region * window, cols), F32),
         ],
         out_shape=[
-            jax.ShapeDtypeStruct((hidden, n_region * pairs), BF),
+            jax.ShapeDtypeStruct((n_region * pairs, hidden), BF),
             jax.ShapeDtypeStruct((cols, n_region * pairs), BF),
-            jax.ShapeDtypeStruct((n_region * lines, 128), F32),
-            jax.ShapeDtypeStruct((n_region, lines, 128), F32),
-            jax.ShapeDtypeStruct((n_region, lines, 128), F32),
+            jax.ShapeDtypeStruct((n_region * blk, 128), F32),
+            jax.ShapeDtypeStruct((n_region, blk, 128), F32),
         ],
         compiler_params=room(14 + 1.25 * n_region),
         name="scores",
@@ -435,32 +402,31 @@
             name="core_sum",
         )(keep, received)
 
+    def turns(targets):
+        return [pltpu.VMEM((len(targets), *x), F32) for x in ((cols, 2 * rows), (2 * rows, cols))]
+
     def rest(targets, pre):
         return pl.pallas_call(
             functools.partial(rest_kernel, targets),
             grid=(steps,),
-            in_specs=[by_pairs(hidden), by_pairs(cols), VMEM],
+            in_specs=[pair_rows, by_pairs(cols), VMEM],
             out_specs=[VMEM] * 2,
-            scratch_shapes=[pltpu.VMEM((len(targets) * 2 * rows, cols), F32)],
+            scratch_shapes=turns(targets),
             out_shape=[blocks(targets)] * 2,
             compiler_params=room(14),
             name="gradient_rest",
         )(first, pre, tail)
 
     pre, tail, keep, send = pl.pallas_call(
-        functools.partial(grad_kernel, n_region, early, slots),
+        functools.partial(grad_kernel, n_region, early, window),
         grid=(steps,),
         in_specs=[
-            VMEM if resident else pl.BlockSpec((lines, 128), functools.partial(lambda k, i: (i ^ k, 0), k))
+            VMEM if resident else pl.BlockSpec((blk, 128), functools.partial(lambda k, i: (i ^ k, 0), k))
             for k in range(n_region)
         ]
-        + [VMEM, VMEM, by_pairs(hidden), by_pairs(cols), VMEM],
+        + [VMEM, pair_rows, by_pairs(cols), VMEM],
         out_specs=[by_pairs(cols)] + [VMEM] * 3,
-        scratch_shapes=[
-            pltpu.VMEM((len(early) * 2 * rows, cols), F32),
-            pltpu.VMEM((cols, 128), F32),
-            pltpu.VMEM((2, lines, 128), F32),
-        ],
+        scratch_shapes=turns(early) + [pltpu.VMEM((cols, 128), F32), pltpu.VMEM((2, blk, 128), F32)],
         out_shape=[
             jax.ShapeDtypeStruct((cols, n_region * pairs), BF),
             jax.ShapeDtypeStruct((TAIL, cols), BF),
@@ -469,7 +435,7 @@
         ],
         compiler_params=room(14),
         name="gradient",
-    )(*parts, ids, flow, first, act, weight_out)
+    )(*parts, win, first, act, weight_out)
     received = swap_core(send)
     keep_later, send_later = rest(later, pre)
     sums = core_sum(keep, received)

time: 68.4 us -> 68.6 us (level)
  waiting for transfers between devices: 21.3 us -> 19.9 us
  other arithmetic: 1.8 us -> 2.98 us
  local copies, waits for them, and re-layouts: 2.78 us -> 3.58 us
    ppermute x9, waiting for transfers between devices: 13.9 us -> 12.5 us  [along_z(): lax.ppermute(array, 'shard', [(i, i ^ 2 * by) for i in range(devices)])]
    pallas_call x2, Pallas kernels: 9.46 us -> 8.56 us  [the longest x1 5.92 us: shards(): pl.pallas_call(functools.partial(score_kernel, n_region, n_z, blk), grid=...]
    dynamic_slice x4, local copies, waits for them, and re-layouts: 2.56 us -> 3.37 us  [cut(): lax.dynamic_slice_in_dim(array, (region ^ i) * cols, cols, array.ndim - 1)]
    another operation x2 -> x0, other arithmetic: 0.78 us -> none
    lt x0 -> x1, other arithmetic: none -> 0.73 us  [shards(): valid = jnp.arange(slots, dtype=jnp.int32)[None, :] < counts[:, None]]
    sub x0 -> x1, other arithmetic: none -> 0.72 us  [shards(): spot = neighbors % (blk * n_shard) - (lax.axis_index('shard') - REACH) * blk]
  transfers between devices with their start and end apart: 27 -> 27, of which waited for: 14 -> 12; matrix products, arithmetic and copies ran while one was open for 7% -> 10% of each run, Pallas kernels for 2% -> 3%
where the time goes in v4:
time: 68.6 us; the launch traced here: 68.1 us
  starting transfers between devices  28.2 us (41%)
  waiting for transfers between devices  19.9 us (29%)
  Pallas kernels  11.5 us (17%)
  local copies, waits for them, and re-layouts  3.58 us (5%)
  other arithmetic  2.98 us (4%)
  matrix products  1.04 us (2%)
  between operations  0.94 us (1%)
    ppermute x9, starting transfers between devices, along_z(): lax.ppermute(array, 'shard', [(i, i ^ 2 * by) for i in range(devices)])  14.6 us
    ppermute x9, waiting for transfers between devices, along_z(): lax.ppermute(array, 'shard', [(i, i ^ 2 * by) for i in range(devices)])  12.5 us
    ppermute x9, starting transfers between devices, swap_region(): return lax.ppermute(array, 'region', [(i, i ^ by) for i in range(devices)])  11.4 us
    ppermute x9, waiting for transfers between devices, swap_region(): return lax.ppermute(array, 'region', [(i, i ^ by) for i in range(devices)])  6.25 us
    pallas_call x1, Pallas kernels, shards(): pl.pallas_call(functools.partial(score_kernel, n_region, n_z, blk), grid=...  5.92 us
    dynamic_slice x4, local copies, waits for them, and re-layouts, cut(): lax.dynamic_slice_in_dim(array, (region ^ i) * cols, cols, array.ndim - 1)  3.37 us
    pallas_call x1, Pallas kernels, shards(): pl.pallas_call(functools.partial(grad_kernel, n_region, early, window), g...  2.63 us
    ppermute x9, starting transfers between devices, swap_core(): return lax.ppermute(array, 'shard', [(i, i ^ 1) for i in range(devices)])  2.23 us
  transfers between devices with their start and end apart: 27, of which 12 were waited for; matrix products, arithmetic and copies ran while one was open for 10% of the time, Pallas kernels for 3%

profile of v4, /device:TPU:0, one launch (start us, length us, event | category | flops | bytes accessed | tf_op | source)
XLA Modules:
  0.0 68.1 jit_solution(4699875239953162637)
XLA Ops:
  0.7 0.9 %constant_dynamic-slice_fusion.9 = (bf16[64,256]{1,0:T(8,128)(2,1)S(1)}, bf16[64,256]{1,0:T(8,128)(2,1)S(1)}) fusion(bf16[64,1024]{1,0:T(8,128)(2,1)} %param.15, s32[]{:T(128)S(6)} %select_n.32, bf16[64,1024]{1,0:T(8,128)(2,1)} %param.14), kind=kLoop, calls=%fused_computation.52 | loop fusion | bytes 131076 | tf_op jit(solution)/shard_map/dynamic_slice | solution.py:311
  1.5 4.1 %collective-permute-start.1 = (bf16[128,256]{1,0:T(8,128)(2,1)S(1)}, bf16[128,256]{1,0:T(8,128)(2,1)S(1)}, u32[]{:S(2)}, u32[]{:S(2)}) collective-permute-start(bf16[128,256]{1,0:T(8,128)(2,1)S(1)} %pad_maximum_fusion.4), channel_id=1, source_target_pairs={{0,4},{1,5},{2,6},{3,7},{4,0},{5,1},{6,2},{7,3},{8,12},{9,13},{10,... | collective-permute-start | bytes 196616 | tf_op jit(solution)/shard_map/ppermute | solution.py:20
  5.6 1.0 %multiply_reduce_fusion = (f32[16]{0:T(128)S(1)}, f32[16,512]{1,0:T(8,128)S(1)}) fusion(bf16[1024,512]{1,0:T(8,128)(2,1)S(1)} %copy-done, s32[1024]{0:T(1024)} %param.10), kind=kOutput, calls=%fused_computation.34 | convolution fusion | flops 16809968 | bytes 1085504 | tf_op jit(solution)/shard_map/dot_general | solution.py:320
  6.8 1.4 %collective-permute-start.2 = (bf16[160,256]{1,0:T(8,128)(2,1)S(1)}, bf16[160,256]{1,0:T(8,128)(2,1)S(1)}, u32[]{:S(2)}, u32[]{:S(2)}) collective-permute-start(bf16[160,256]{1,0:T(8,128)(2,1)S(1)} %pad_maximum_fusion.3), channel_id=1, source_target_pairs={{0,6},{1,7},{2,4},{3,5},{4,2},{5,3},{6,0},{7,1},{8,14},{9,15},{10,... | collective-permute-start | bytes 245768 | tf_op jit(solution)/shard_map/ppermute | solution.py:20
  8.2 0.3 collective-permute-start
  8.5 0.7 %iota_compare_fusion.3 = pred[16,64]{1,0:T(8,128)(4,1)S(1)} fusion(s32[16]{0:T(128)} %param.12), kind=kLoop, calls=%fused_computation.41 | loop fusion | flops 1024 | bytes 1088 | tf_op jit(solution)/shard_map/lt | solution.py:330
  9.2 0.7 %fusion.4 = (s32[16,64]{1,0:T(8,128)S(1)}, s32[16,64]{1,0:T(8,128)S(1)}) fusion(s32[16,64]{1,0:T(8,128)} %param.11, s32[]{:T(128)S(6)} %mul.42, s32[16,64]{1,0:T(8,128)} %param.13), kind=kLoop, calls=%fused_computation.40 | loop fusion | flops 13312 | bytes 16388 | tf_op jit(solution)/shard_map/sub | solution.py:329
  10.0 0.6 select_reduce_fusion
  10.6 0.9 %constant_dynamic-slice_fusion = bf16[128,256]{1,0:T(8,128)(2,1)S(1)} fusion(bf16[128,1024]{1,0:T(8,128)(2,1)} %param.16, s32[]{:T(128)S(6)} %select_n.32), kind=kLoop, calls=%fused_computation.43 | loop fusion | bytes 131076 | tf_op jit(solution)/shard_map/dynamic_slice | solution.py:311
  11.4 0.8 %constant_dynamic-slice_fusion.8 = (bf16[64,256]{1,0:T(8,128)(2,1)S(1)}, bf16[64,256]{1,0:T(8,128)(2,1)S(1)}, bf16[64,256]{1,0:T(8,128)(2,1)S(1)}, bf16[64,256]{1,0:T(8,128)(2,1)S(1)}) fusion(bf16[64,1024]{1,0:T(8,128)(2,1)} %param.14, s32[]{:T(128)S(6)} %select_n.32, s32[]{:T(128)S(6)} %select_n.35, s32[]{:T(128)S(6)} %select_n.34, s32[]{:T(128)S(6)} %select_n.33), kind=kLoop, calls=%fused_computation.51 | loop fusion | bytes 262160 | tf_op jit(solution)/shard_map/dynamic_slice | solution.py:311
  12.2 0.8 %constant_dynamic-slice_fusion.7 = (bf16[64,256]{1,0:T(8,128)(2,1)S(1)}, bf16[64,256]{1,0:T(8,128)(2,1)S(1)}, bf16[64,256]{1,0:T(8,128)(2,1)S(1)}, bf16[64,256]{1,0:T(8,128)(2,1)S(1)}) fusion(bf16[64,1024]{1,0:T(8,128)(2,1)} %param.15, s32[]{:T(128)S(6)} %select_n.32, s32[]{:T(128)S(6)} %select_n.35, s32[]{:T(128)S(6)} %select_n.34, s32[]{:T(128)S(6)} %select_n.33), kind=kLoop, calls=%fused_computation.50 | loop fusion | bytes 262160 | tf_op jit(solution)/shard_map/dynamic_slice | solution.py:311
  13.1 0.7 %collective-permute-done = bf16[160,256]{1,0:T(8,128)(2,1)S(1)} collective-permute-done((bf16[160,256]{1,0:T(8,128)(2,1)S(1)}, bf16[160,256]{1,0:T(8,128)(2,1)S(1)}, u32[]{:S(2)}, u32[]{:S(2)}) %collective-permute-start) | collective-permute-done | bytes 81952 | tf_op jit(solution)/shard_map/ppermute | solution.py:20
  14.1 1.6 %collective-permute-start.8 = (bf16[496,256]{1,0:T(8,128)(2,1)S(1)}, bf16[496,256]{1,0:T(8,128)(2,1)S(1)}, u32[]{:S(2)}, u32[]{:S(2)}) collective-permute-start(bf16[496,256]{1,0:T(8,128)(2,1)S(1)} %constant_dynamic-update-slice_fusion.refs_2_), channel_id=1, source_target_pairs={{0,16},{8,24},{16,0},{24,8},{1,17},{9,25},{17,1},{25,9},{2,18},{10... | collective-permute-start | bytes 761864 | tf_op jit(solution)/shard_map/ppermute | solution.py:34
  15.7 1.5 %collective-permute-start.7 = (bf16[496,256]{1,0:T(8,128)(2,1)S(1)}, bf16[496,256]{1,0:T(8,128)(2,1)S(1)}, u32[]{:S(2)}, u32[]{:S(2)}) collective-permute-start(bf16[496,256]{1,0:T(8,128)(2,1)S(1)} %constant_dynamic-update-slice_fusion.refs_2_), channel_id=1, source_target_pairs={{0,8},{8,0},{16,24},{24,16},{1,9},{9,1},{17,25},{25,17},{2,10},{10... | collective-permute-start | bytes 761864 | tf_op jit(solution)/shard_map/ppermute | solution.py:34
  17.2 1.0 %collective-permute-start.6 = (bf16[192,256]{1,0:T(8,128)(2,1)S(1)}, bf16[192,256]{1,0:T(8,128)(2,1)S(1)}, u32[]{:S(2)}, u32[]{:S(2)}) collective-permute-start(bf16[192,256]{1,0:T(8,128)(2,1)S(1)} %pad_maximum_fusion.2), channel_id=1, source_target_pairs={{0,2},{1,3},{2,0},{3,1},{4,6},{5,7},{6,4},{7,5},{8,10},{9,11},{10,... | collective-permute-start | bytes 294920 | tf_op jit(solution)/shard_map/ppermute | solution.py:20
  18.2 2.1 %collective-permute-start.5 = (bf16[192,256]{1,0:T(8,128)(2,1)S(1)}, bf16[192,256]{1,0:T(8,128)(2,1)S(1)}, u32[]{:S(2)}, u32[]{:S(2)}) collective-permute-start(bf16[192,256]{1,0:T(8,128)(2,1)S(1)} %pad_maximum_fusion.2), channel_id=1, source_target_pairs={{0,4},{1,5},{2,6},{3,7},{4,0},{5,1},{6,2},{7,3},{8,12},{9,13},{10,... | collective-permute-start | bytes 294920 | tf_op jit(solution)/shard_map/ppermute | solution.py:20
  20.3 1.3 %collective-permute-start.4 = (bf16[192,256]{1,0:T(8,128)(2,1)S(1)}, bf16[192,256]{1,0:T(8,128)(2,1)S(1)}, u32[]{:S(2)}, u32[]{:S(2)}) collective-permute-start(bf16[192,256]{1,0:T(8,128)(2,1)S(1)} %pad_maximum_fusion.2), channel_id=1, source_target_pairs={{0,6},{1,7},{2,4},{3,5},{4,2},{5,3},{6,0},{7,1},{8,14},{9,15},{10,... | collective-permute-start | bytes 294920 | tf_op jit(solution)/shard_map/ppermute | solution.py:20
  21.6 1.4 %collective-permute-done.6 = bf16[192,256]{1,0:T(8,128)(2,1)S(1)} collective-permute-done((bf16[192,256]{1,0:T(8,128)(2,1)S(1)}, bf16[192,256]{1,0:T(8,128)(2,1)S(1)}, u32[]{:S(2)}, u32[]{:S(2)}) %collective-permute-start.6) | collective-permute-done | bytes 98336 | tf_op jit(solution)/shard_map/ppermute | solution.py:20
  22.9 1.2 %collective-permute-start.9 = (bf16[304,256]{1,0:T(8,128)(2,1)S(1)}, bf16[304,256]{1,0:T(8,128)(2,1)}, u32[]{:S(2)}, u32[]{:S(2)}) collective-permute-start(bf16[304,256]{1,0:T(8,128)(2,1)S(1)} %get-tuple-element.89), channel_id=1, source_target_pairs={{0,24},{8,16},{16,8},{24,0},{1,25},{9,17},{17,9},{25,1},{2,26},{10... | collective-permute-start | bytes 466952 | tf_op jit(solution)/shard_map/ppermute | solution.py:34
  24.1 4.6 %collective-permute-done.5 = bf16[192,256]{1,0:T(8,128)(2,1)S(1)} collective-permute-done((bf16[192,256]{1,0:T(8,128)(2,1)S(1)}, bf16[192,256]{1,0:T(8,128)(2,1)S(1)}, u32[]{:S(2)}, u32[]{:S(2)}) %collective-permute-start.5) | collective-permute-done | bytes 98336 | tf_op jit(solution)/shard_map/ppermute | solution.py:20
  28.9 0.6 collective-permute-start.10
  29.5 0.4 collective-permute-start.12
  30.1 0.8 %dynamic-slice_convert_fusion = f32[256]{0:T(256)S(1)} fusion(bf16[1024]{0:T(1024)(128)(2,1)} %param.17, s32[]{:T(128)S(6)} %select_n.32), kind=kLoop, calls=%fused_computation.54 | loop fusion | flops 256 | bytes 1540 | tf_op jit(solution)/shard_map/reshape | solution.py:350
  31.0 1.1 %collective-permute-done.14.refs_11_ = bf16[304,256]{1,0:T(8,128)(2,1)} collective-permute-done((bf16[304,256]{1,0:T(8,128)(2,1)}, bf16[304,256]{1,0:T(8,128)(2,1)}, u32[]{:S(2)}, u32[]{:S(2)}) %collective-permute-start.14) | collective-permute-done | bytes 155680 | tf_op jit(solution)/shard_map/ppermute | solution.py:29
  32.1 5.9 %scores.1 = (bf16[5120,1024]{1,0:T(8,128)(2,1)S(1)}, bf16[256,5120]{1,0:T(8,128)(2,1)S(1)}, f32[64,128]{1,0:T(8,128)S(1)}, f32[4,16,128]{2,1,0:T(8,128)S(1)}) custom-call(bf16[4,128,256]{2,1,0:T(8,128)(2,1)S(1)} %pad_maximum_fusion.1.refs_0_, bf16[704,256]{1,0:T(8,128)(2,1)S(1)} %pad_maximum_fusion.refs_1_, ...), custom_call_target="tpu_custom_call" | custom-call | tf_op jit(solution)/shard_map/scores/pallas_call | solution.py:362
  38.0 1.0 %collective-permute-start.17 = (f32[64,128]{1,0:T(8,128)S(1)}, f32[64,128]{1,0:T(8,128)S(1)}, u32[]{:S(2)}, u32[]{:S(2)}) collective-permute-start(f32[64,128]{1,0:T(8,128)S(1)} %get-tuple-element.42.refs_0_), channel_id=1, source_target_pairs={{0,24},{8,16},{16,8},{24,0},{1,25},{9,17},{17,9},{25,1},{2,26},{10... | collective-permute-start | bytes 98312 | tf_op jit(solution)/shard_map/ppermute | solution.py:34
  39.0 1.0 %collective-permute-start.16 = (f32[64,128]{1,0:T(8,128)S(1)}, f32[64,128]{1,0:T(8,128)S(1)}, u32[]{:S(2)}, u32[]{:S(2)}) collective-permute-start(f32[64,128]{1,0:T(8,128)S(1)} %get-tuple-element.42.refs_0_), channel_id=1, source_target_pairs={{0,16},{8,24},{16,0},{24,8},{1,17},{9,25},{17,1},{25,9},{2,18},{10... | collective-permute-start | bytes 98312 | tf_op jit(solution)/shard_map/ppermute | solution.py:34
  40.0 1.5 %collective-permute-start.15 = (f32[64,128]{1,0:T(8,128)S(1)}, f32[64,128]{1,0:T(8,128)S(1)}, u32[]{:S(2)}, u32[]{:S(2)}) collective-permute-start(f32[64,128]{1,0:T(8,128)S(1)} %get-tuple-element.42.refs_0_), channel_id=1, source_target_pairs={{0,8},{8,0},{16,24},{24,16},{1,9},{9,1},{17,25},{25,17},{2,10},{10... | collective-permute-start | bytes 98312 | tf_op jit(solution)/shard_map/ppermute | solution.py:34
  41.5 1.5 %collective-permute-done.17.refs_3_ = f32[64,128]{1,0:T(8,128)S(1)} collective-permute-done((f32[64,128]{1,0:T(8,128)S(1)}, f32[64,128]{1,0:T(8,128)S(1)}, u32[]{:S(2)}, u32[]{:S(2)}) %collective-permute-start.17) | collective-permute-done | bytes 32800 | tf_op jit(solution)/shard_map/ppermute | solution.py:34
  43.0 0.1 collective-permute-done.16.refs_2_
  43.2 0.7 %collective-permute-done.15.refs_1_ = f32[64,128]{1,0:T(8,128)S(1)} collective-permute-done((f32[64,128]{1,0:T(8,128)S(1)}, f32[64,128]{1,0:T(8,128)S(1)}, u32[]{:S(2)}, u32[]{:S(2)}) %collective-permute-start.15) | collective-permute-done | bytes 32800 | tf_op jit(solution)/shard_map/ppermute | solution.py:34
  43.9 2.6 %gradient.1 = (bf16[256,5120]{1,0:T(8,128)(2,1)S(1)}, bf16[16,256]{1,0:T(8,128)(2,1)S(1)}, bf16[2,144,256]{2,1,0:T(8,128)(2,1)S(1)}, bf16[2,144,256]{2,1,0:T(8,128)(2,1)S(1)}) custom-call(f32[64,128]{1,0:T(8,128)S(1)} %get-tuple-element.42.refs_0_, f32[64,128]{1,0:T(8,128)S(1)} %collective-permute-done.15.refs_1_, ...), custom_call_target="tpu_custom_call" | custom-call | tf_op jit(solution)/shard_map/gradient/pallas_call | solution.py:420
  46.7 0.9 %gradient_rest.2 = (bf16[1,144,256]{2,1,0:T(8,128)(2,1)S(1)}, bf16[1,144,256]{2,1,0:T(8,128)(2,1)S(1)}) custom-call(bf16[5120,1024]{1,0:T(8,128)(2,1)S(1)} %get-tuple-element.41.refs_5_.refs_0_, bf16[256,5120]{1,0:T(8,128)(2,1)S(1)} %get-tuple-element.53.refs_1_, bf16[16,256]{1,0:T(8,128)(2,1)S(1)} %get-tuple-element.46.refs_2_), custom_call_target="tpu_custom_call" | custom-call | tf_op jit(solution)/shard_map/gradient_rest/pallas_call | solution.py:409
  47.6 0.6 collective-permute-start.18
  48.2 1.0 %gradient_rest.3 = (bf16[1,144,256]{2,1,0:T(8,128)(2,1)S(1)}, bf16[1,144,256]{2,1,0:T(8,128)(2,1)S(1)}) custom-call(bf16[5120,1024]{1,0:T(8,128)(2,1)S(1)} %get-tuple-element.41.refs_5_.refs_0_, bf16[256,5120]{1,0:T(8,128)(2,1)S(1)} %get-tuple-element.53.refs_1_, bf16[16,256]{1,0:T(8,128)(2,1)S(1)} %get-tuple-element.46.refs_2_), custom_call_target="tpu_custom_call" | custom-call | tf_op jit(solution)/shard_map/gradient_rest/pallas_call | solution.py:409
  49.2 0.3 collective-permute-start.20
  49.5 2.2 %collective-permute-start.21 = (bf16[144,256]{1,0:T(8,128)(2,1)S(1)}, bf16[144,256]{1,0:T(8,128)(2,1)S(1)}, u32[]{:S(2)}, u32[]{:S(2)}) collective-permute-start(bf16[144,256]{1,0:T(8,128)(2,1)S(1)} %get-tuple-element.61), channel_id=1, source_target_pairs={{0,6},{1,7},{2,4},{3,5},{4,2},{5,3},{6,0},{7,1},{8,14},{9,15},{10,... | collective-permute-start | bytes 221192 | tf_op jit(solution)/shard_map/ppermute | solution.py:20
  51.8 0.8 %collective-permute-start.22 = (bf16[144,256]{1,0:T(8,128)(2,1)S(1)}, bf16[144,256]{1,0:T(8,128)(2,1)S(1)}, u32[]{:S(2)}, u32[]{:S(2)}) collective-permute-start(bf16[144,256]{1,0:T(8,128)(2,1)S(1)} %get-tuple-element.62), channel_id=1, source_target_pairs={{0,4},{1,5},{2,6},{3,7},{4,0},{5,1},{6,2},{7,3},{8,12},{9,13},{10,... | collective-permute-start | bytes 221192 | tf_op jit(solution)/shard_map/ppermute | solution.py:20
  52.6 1.3 %collective-permute-start.23 = (bf16[144,256]{1,0:T(8,128)(2,1)S(1)}, bf16[144,256]{1,0:T(8,128)(2,1)S(1)}, u32[]{:S(2)}, u32[]{:S(2)}) collective-permute-start(bf16[144,256]{1,0:T(8,128)(2,1)S(1)} %core_sum.5), channel_id=1, source_target_pairs={{0,2},{1,3},{2,0},{3,1},{4,6},{5,7},{6,4},{7,5},{8,10},{9,11},{10,... | collective-permute-start | bytes 221192 | tf_op jit(solution)/shard_map/ppermute | solution.py:20
  53.9 2.2 %collective-permute-done.21.refs_1_ = bf16[144,256]{1,0:T(8,128)(2,1)S(1)} collective-permute-done((bf16[144,256]{1,0:T(8,128)(2,1)S(1)}, bf16[144,256]{1,0:T(8,128)(2,1)S(1)}, u32[]{:S(2)}, u32[]{:S(2)}) %collective-permute-start.21) | collective-permute-done | bytes 73760 | tf_op jit(solution)/shard_map/ppermute | solution.py:20
  56.1 3.6 %collective-permute-done.22.refs_2_ = bf16[144,256]{1,0:T(8,128)(2,1)S(1)} collective-permute-done((bf16[144,256]{1,0:T(8,128)(2,1)S(1)}, bf16[144,256]{1,0:T(8,128)(2,1)S(1)}, u32[]{:S(2)}, u32[]{:S(2)}) %collective-permute-start.22) | collective-permute-done | bytes 73760 | tf_op jit(solution)/shard_map/ppermute | solution.py:20
  59.8 1.5 %collective-permute-start.26 = (bf16[144,256]{1,0:T(8,128)(2,1)S(1)}, bf16[144,256]{1,0:T(8,128)(2,1)S(1)}, u32[]{:S(2)}, u32[]{:S(2)}) collective-permute-start(bf16[144,256]{1,0:T(8,128)(2,1)S(1)} %z_sum.1.refs_0_), channel_id=1, source_target_pairs={{0,24},{8,16},{16,8},{24,0},{1,25},{9,17},{17,9},{25,1},{2,26},{10... | collective-permute-start | bytes 221192 | tf_op jit(solution)/shard_map/ppermute | solution.py:34
  61.3 1.5 %collective-permute-start.25 = (bf16[144,256]{1,0:T(8,128)(2,1)S(1)}, bf16[144,256]{1,0:T(8,128)(2,1)S(1)}, u32[]{:S(2)}, u32[]{:S(2)}) collective-permute-start(bf16[144,256]{1,0:T(8,128)(2,1)S(1)} %z_sum.1.refs_0_), channel_id=1, source_target_pairs={{0,16},{8,24},{16,0},{24,8},{1,17},{9,25},{17,1},{25,9},{2,18},{10... | collective-permute-start | bytes 221192 | tf_op jit(solution)/shard_map/ppermute | solution.py:34
  62.8 0.5 collective-permute-start.24
  63.4 2.6 %collective-permute-done.26.refs_3_ = bf16[144,256]{1,0:T(8,128)(2,1)S(1)} collective-permute-done((bf16[144,256]{1,0:T(8,128)(2,1)S(1)}, bf16[144,256]{1,0:T(8,128)(2,1)S(1)}, u32[]{:S(2)}, u32[]{:S(2)}) %collective-permute-start.26) | collective-permute-done | bytes 73760 | tf_op jit(solution)/shard_map/ppermute | solution.py:34
  66.0 0.2 collective-permute-done.25.refs_2_
  66.2 1.0 %collective-permute-done.24.refs_1_ = bf16[144,256]{1,0:T(8,128)(2,1)S(1)} collective-permute-done((bf16[144,256]{1,0:T(8,128)(2,1)S(1)}, bf16[144,256]{1,0:T(8,128)(2,1)S(1)}, u32[]{:S(2)}, u32[]{:S(2)}) %collective-permute-start.24) | collective-permute-done | bytes 73760 | tf_op jit(solution)/shard_map/ppermute | solution.py:34
  67.2 0.9 %finish.1 = (f32[128,1024]{1,0:T(8,128)}, f32[1,1024]{1,0:T(1,128)}, f32[1,1]{1,0:T(1,128)}) custom-call(bf16[144,256]{1,0:T(8,128)(2,1)S(1)} %z_sum.1.refs_0_, bf16[144,256]{1,0:T(8,128)(2,1)S(1)} %collective-permute-done.24.refs_1_, bf16[144,256]{1,0:T(8,128)(2,1)S(1)} %collective-permute-done.25.refs_2_, bf16[144,256]{1,0:T(8,128)(2,1)S(1)} %collective-permute-done.26.refs_3_), custom_call_target="tpu_custom_call" | custom-call | tf_op jit(solution)/shard_map/finish/pallas_call | solution.py:460
  (52 shorter events, 1.0 us)
Async XLA Ops:
  0.6 5.0 %copy-start = (bf16[1024,512]{1,0:T(8,128)(2,1)S(1)}, bf16[1024,512]{1,0:T(8,128)(2,1)}, u32[]{:S(2)}) copy-start(bf16[1024,512]{1,0:T(8,128)(2,1)} %param.9) | copy-start | bytes 3145732
  1.5 12.3 %collective-permute-start.1 = (bf16[128,256]{1,0:T(8,128)(2,1)S(1)}, bf16[128,256]{1,0:T(8,128)(2,1)S(1)}, u32[]{:S(2)}, u32[]{:S(2)}) collective-permute-start(bf16[128,256]{1,0:T(8,128)(2,1)S(1)} %pad_maximum_fusion.4), channel_id=1, source_target_pairs={{0,4},{1,5},{2,6},{3,7},{4,0},{5,1},{6,2},{7,3},{8,12},{9,13},{10,... | collective-permute-start | bytes 196616 | tf_op jit(solution)/shard_map/ppermute | solution.py:20
  6.8 7.1 %collective-permute-start.2 = (bf16[160,256]{1,0:T(8,128)(2,1)S(1)}, bf16[160,256]{1,0:T(8,128)(2,1)S(1)}, u32[]{:S(2)}, u32[]{:S(2)}) collective-permute-start(bf16[160,256]{1,0:T(8,128)(2,1)S(1)} %pad_maximum_fusion.3), channel_id=1, source_target_pairs={{0,6},{1,7},{2,4},{3,5},{4,2},{5,3},{6,0},{7,1},{8,14},{9,15},{10,... | collective-permute-start | bytes 245768 | tf_op jit(solution)/shard_map/ppermute | solution.py:20
  8.2 5.6 %collective-permute-start = (bf16[160,256]{1,0:T(8,128)(2,1)S(1)}, bf16[160,256]{1,0:T(8,128)(2,1)S(1)}, u32[]{:S(2)}, u32[]{:S(2)}) collective-permute-start(bf16[160,256]{1,0:T(8,128)(2,1)S(1)} %pad_maximum_fusion.3), channel_id=1, source_target_pairs={{0,2},{1,3},{2,0},{3,1},{4,6},{5,7},{6,4},{7,5},{8,10},{9,11},{10,... | collective-permute-start | bytes 245768 | tf_op jit(solution)/shard_map/ppermute | solution.py:20
  14.0 3.2 %collective-permute-start.3 = (bf16[496,256]{1,0:T(8,128)(2,1)S(1)}, bf16[496,256]{1,0:T(8,128)(2,1)S(1)}, u32[]{:S(2)}, u32[]{:S(2)}) collective-permute-start(bf16[496,256]{1,0:T(8,128)(2,1)S(1)} %constant_dynamic-update-slice_fusion.refs_2_), channel_id=1, source_target_pairs={{0,1},{1,0},{2,3},{3,2},{4,5},{5,4},{6,7},{7,6},{8,9},{9,8},{10,11... | collective-permute-start | bytes 761864 | tf_op jit(solution)/shard_map/ppermute | solution.py:29
  14.1 15.3 %collective-permute-start.8 = (bf16[496,256]{1,0:T(8,128)(2,1)S(1)}, bf16[496,256]{1,0:T(8,128)(2,1)S(1)}, u32[]{:S(2)}, u32[]{:S(2)}) collective-permute-start(bf16[496,256]{1,0:T(8,128)(2,1)S(1)} %constant_dynamic-update-slice_fusion.refs_2_), channel_id=1, source_target_pairs={{0,16},{8,24},{16,0},{24,8},{1,17},{9,25},{17,1},{25,9},{2,18},{10... | collective-permute-start | bytes 761864 | tf_op jit(solution)/shard_map/ppermute | solution.py:34
  15.7 13.8 %collective-permute-start.7 = (bf16[496,256]{1,0:T(8,128)(2,1)S(1)}, bf16[496,256]{1,0:T(8,128)(2,1)S(1)}, u32[]{:S(2)}, u32[]{:S(2)}) collective-permute-start(bf16[496,256]{1,0:T(8,128)(2,1)S(1)} %constant_dynamic-update-slice_fusion.refs_2_), channel_id=1, source_target_pairs={{0,8},{8,0},{16,24},{24,16},{1,9},{9,1},{17,25},{25,17},{2,10},{10... | collective-permute-start | bytes 761864 | tf_op jit(solution)/shard_map/ppermute | solution.py:34
  17.2 5.7 %collective-permute-start.6 = (bf16[192,256]{1,0:T(8,128)(2,1)S(1)}, bf16[192,256]{1,0:T(8,128)(2,1)S(1)}, u32[]{:S(2)}, u32[]{:S(2)}) collective-permute-start(bf16[192,256]{1,0:T(8,128)(2,1)S(1)} %pad_maximum_fusion.2), channel_id=1, source_target_pairs={{0,2},{1,3},{2,0},{3,1},{4,6},{5,7},{6,4},{7,5},{8,10},{9,11},{10,... | collective-permute-start | bytes 294920 | tf_op jit(solution)/shard_map/ppermute | solution.py:20
  18.2 10.5 %collective-permute-start.5 = (bf16[192,256]{1,0:T(8,128)(2,1)S(1)}, bf16[192,256]{1,0:T(8,128)(2,1)S(1)}, u32[]{:S(2)}, u32[]{:S(2)}) collective-permute-start(bf16[192,256]{1,0:T(8,128)(2,1)S(1)} %pad_maximum_fusion.2), channel_id=1, source_target_pairs={{0,4},{1,5},{2,6},{3,7},{4,0},{5,1},{6,2},{7,3},{8,12},{9,13},{10,... | collective-permute-start | bytes 294920 | tf_op jit(solution)/shard_map/ppermute | solution.py:20
  20.3 8.5 %collective-permute-start.4 = (bf16[192,256]{1,0:T(8,128)(2,1)S(1)}, bf16[192,256]{1,0:T(8,128)(2,1)S(1)}, u32[]{:S(2)}, u32[]{:S(2)}) collective-permute-start(bf16[192,256]{1,0:T(8,128)(2,1)S(1)} %pad_maximum_fusion.2), channel_id=1, source_target_pairs={{0,6},{1,7},{2,4},{3,5},{4,2},{5,3},{6,0},{7,1},{8,14},{9,15},{10,... | collective-permute-start | bytes 294920 | tf_op jit(solution)/shard_map/ppermute | solution.py:20
  22.9 7.0 %collective-permute-start.9 = (bf16[304,256]{1,0:T(8,128)(2,1)S(1)}, bf16[304,256]{1,0:T(8,128)(2,1)}, u32[]{:S(2)}, u32[]{:S(2)}) collective-permute-start(bf16[304,256]{1,0:T(8,128)(2,1)S(1)} %get-tuple-element.89), channel_id=1, source_target_pairs={{0,24},{8,16},{16,8},{24,0},{1,25},{9,17},{17,9},{25,1},{2,26},{10... | collective-permute-start | bytes 466952 | tf_op jit(solution)/shard_map/ppermute | solution.py:34
  28.8 3.3 %collective-permute-start.11 = (bf16[704,256]{1,0:T(8,128)(2,1)S(1)}, bf16[704,256]{1,0:T(8,128)(2,1)S(1)}, u32[]{:S(2)}, u32[]{:S(2)}) collective-permute-start(bf16[704,256]{1,0:T(8,128)(2,1)S(1)} %pad_maximum_fusion.refs_1_), channel_id=1, source_target_pairs={{0,1},{1,0},{2,3},{3,2},{4,5},{5,4},{6,7},{7,6},{8,9},{9,8},{10,11... | collective-permute-start | bytes 1081352 | tf_op jit(solution)/shard_map/ppermute | solution.py:29
  28.9 2.1 %collective-permute-start.10 = (bf16[4,128,256]{2,1,0:T(8,128)(2,1)S(1)}, bf16[4,128,256]{2,1,0:T(8,128)(2,1)S(1)}, u32[]{:S(2)}, u32[]{:S(2)}) collective-permute-start(bf16[4,128,256]{2,1,0:T(8,128)(2,1)S(1)} %pad_maximum_fusion.1.refs_0_), channel_id=1, source_target_pairs={{0,1},{1,0},{2,3},{3,2},{4,5},{5,4},{6,7},{7,6},{8,9},{9,8},{10,11... | collective-permute-start | bytes 786440 | tf_op jit(solution)/shard_map/ppermute | solution.py:29
  29.5 2.6 %collective-permute-start.13 = (bf16[496,256]{1,0:T(8,128)(2,1)S(1)}, bf16[496,256]{1,0:T(8,128)(2,1)}, u32[]{:S(2)}, u32[]{:S(2)}) collective-permute-start(bf16[496,256]{1,0:T(8,128)(2,1)S(1)} %collective-permute-done.8.refs_4_), channel_id=1, source_target_pairs={{0,1},{1,0},{2,3},{3,2},{4,5},{5,4},{6,7},{7,6},{8,9},{9,8},{10,11... | collective-permute-start | bytes 761864 | tf_op jit(solution)/shard_map/ppermute | solution.py:29
  29.5 2.5 %collective-permute-start.12 = (bf16[496,256]{1,0:T(8,128)(2,1)S(1)}, bf16[496,256]{1,0:T(8,128)(2,1)}, u32[]{:S(2)}, u32[]{:S(2)}) collective-permute-start(bf16[496,256]{1,0:T(8,128)(2,1)S(1)} %collective-permute-done.7.refs_3_), channel_id=1, source_target_pairs={{0,1},{1,0},{2,3},{3,2},{4,5},{5,4},{6,7},{7,6},{8,9},{9,8},{10,11... | collective-permute-start | bytes 761864 | tf_op jit(solution)/shard_map/ppermute | solution.py:29
  30.0 2.1 %collective-permute-start.14 = (bf16[304,256]{1,0:T(8,128)(2,1)}, bf16[304,256]{1,0:T(8,128)(2,1)}, u32[]{:S(2)}, u32[]{:S(2)}) collective-permute-start(bf16[304,256]{1,0:T(8,128)(2,1)} %collective-permute-done.9.refs_5_), channel_id=1, source_target_pairs={{0,1},{1,0},{2,3},{3,2},{4,5},{5,4},{6,7},{7,6},{8,9},{9,8},{10,11... | collective-permute-start | bytes 466952 | tf_op jit(solution)/shard_map/ppermute | solution.py:29
  38.0 5.1 %collective-permute-start.17 = (f32[64,128]{1,0:T(8,128)S(1)}, f32[64,128]{1,0:T(8,128)S(1)}, u32[]{:S(2)}, u32[]{:S(2)}) collective-permute-start(f32[64,128]{1,0:T(8,128)S(1)} %get-tuple-element.42.refs_0_), channel_id=1, source_target_pairs={{0,24},{8,16},{16,8},{24,0},{1,25},{9,17},{17,9},{25,1},{2,26},{10... | collective-permute-start | bytes 98312 | tf_op jit(solution)/shard_map/ppermute | solution.py:34
  39.0 4.2 %collective-permute-start.16 = (f32[64,128]{1,0:T(8,128)S(1)}, f32[64,128]{1,0:T(8,128)S(1)}, u32[]{:S(2)}, u32[]{:S(2)}) collective-permute-start(f32[64,128]{1,0:T(8,128)S(1)} %get-tuple-element.42.refs_0_), channel_id=1, source_target_pairs={{0,16},{8,24},{16,0},{24,8},{1,17},{9,25},{17,1},{25,9},{2,18},{10... | collective-permute-start | bytes 98312 | tf_op jit(solution)/shard_map/ppermute | solution.py:34
  40.0 3.9 %collective-permute-start.15 = (f32[64,128]{1,0:T(8,128)S(1)}, f32[64,128]{1,0:T(8,128)S(1)}, u32[]{:S(2)}, u32[]{:S(2)}) collective-permute-start(f32[64,128]{1,0:T(8,128)S(1)} %get-tuple-element.42.refs_0_), channel_id=1, source_target_pairs={{0,8},{8,0},{16,24},{24,16},{1,9},{9,1},{17,25},{25,17},{2,10},{10... | collective-permute-start | bytes 98312 | tf_op jit(solution)/shard_map/ppermute | solution.py:34
  46.6 1.6 %collective-permute-start.19 = (bf16[2,144,256]{2,1,0:T(8,128)(2,1)S(1)}, bf16[2,144,256]{2,1,0:T(8,128)(2,1)S(1)}, u32[]{:S(2)}, u32[]{:S(2)}) collective-permute-start(bf16[2,144,256]{2,1,0:T(8,128)(2,1)S(1)} %get-tuple-element.50), channel_id=1, source_target_pairs={{0,1},{1,0},{2,3},{3,2},{4,5},{5,4},{6,7},{7,6},{8,9},{9,8},{10,11... | collective-permute-start | bytes 442376 | tf_op jit(solution)/shard_map/ppermute | solution.py:29
  47.6 1.6 %collective-permute-start.18 = (bf16[1,144,256]{2,1,0:T(8,128)(2,1)S(1)}, bf16[1,144,256]{2,1,0:T(8,128)(2,1)S(1)}, u32[]{:S(2)}, u32[]{:S(2)}) collective-permute-start(bf16[1,144,256]{2,1,0:T(8,128)(2,1)S(1)} %get-tuple-element.48), channel_id=1, source_target_pairs={{0,1},{1,0},{2,3},{3,2},{4,5},{5,4},{6,7},{7,6},{8,9},{9,8},{10,11... | collective-permute-start | bytes 221192 | tf_op jit(solution)/shard_map/ppermute | solution.py:29
  49.2 4.7 %collective-permute-start.20 = (bf16[1,144,256]{2,1,0:T(8,128)(2,1)S(1)}, bf16[1,144,256]{2,1,0:T(8,128)(2,1)S(1)}, u32[]{:S(2)}, u32[]{:S(2)}) collective-permute-start(bf16[1,144,256]{2,1,0:T(8,128)(2,1)S(1)} %get-tuple-element.56), channel_id=1, source_target_pairs={{0,1},{1,0},{2,3},{3,2},{4,5},{5,4},{6,7},{7,6},{8,9},{9,8},{10,11... | collective-permute-start | bytes 221192 | tf_op jit(solution)/shard_map/ppermute | solution.py:29
  49.5 6.6 %collective-permute-start.21 = (bf16[144,256]{1,0:T(8,128)(2,1)S(1)}, bf16[144,256]{1,0:T(8,128)(2,1)S(1)}, u32[]{:S(2)}, u32[]{:S(2)}) collective-permute-start(bf16[144,256]{1,0:T(8,128)(2,1)S(1)} %get-tuple-element.61), channel_id=1, source_target_pairs={{0,6},{1,7},{2,4},{3,5},{4,2},{5,3},{6,0},{7,1},{8,14},{9,15},{10,... | collective-permute-start | bytes 221192 | tf_op jit(solution)/shard_map/ppermute | solution.py:20
  51.8 8.0 %collective-permute-start.22 = (bf16[144,256]{1,0:T(8,128)(2,1)S(1)}, bf16[144,256]{1,0:T(8,128)(2,1)S(1)}, u32[]{:S(2)}, u32[]{:S(2)}) collective-permute-start(bf16[144,256]{1,0:T(8,128)(2,1)S(1)} %get-tuple-element.62), channel_id=1, source_target_pairs={{0,4},{1,5},{2,6},{3,7},{4,0},{5,1},{6,2},{7,3},{8,12},{9,13},{10,... | collective-permute-start | bytes 221192 | tf_op jit(solution)/shard_map/ppermute | solution.py:20
  52.6 7.2 %collective-permute-start.23 = (bf16[144,256]{1,0:T(8,128)(2,1)S(1)}, bf16[144,256]{1,0:T(8,128)(2,1)S(1)}, u32[]{:S(2)}, u32[]{:S(2)}) collective-permute-start(bf16[144,256]{1,0:T(8,128)(2,1)S(1)} %core_sum.5), channel_id=1, source_target_pairs={{0,2},{1,3},{2,0},{3,1},{4,6},{5,7},{6,4},{7,5},{8,10},{9,11},{10,... | collective-permute-start | bytes 221192 | tf_op jit(solution)/shard_map/ppermute | solution.py:20
  59.8 6.1 %collective-permute-start.26 = (bf16[144,256]{1,0:T(8,128)(2,1)S(1)}, bf16[144,256]{1,0:T(8,128)(2,1)S(1)}, u32[]{:S(2)}, u32[]{:S(2)}) collective-permute-start(bf16[144,256]{1,0:T(8,128)(2,1)S(1)} %z_sum.1.refs_0_), channel_id=1, source_target_pairs={{0,24},{8,16},{16,8},{24,0},{1,25},{9,17},{17,9},{25,1},{2,26},{10... | collective-permute-start | bytes 221192 | tf_op jit(solution)/shard_map/ppermute | solution.py:34
  61.3 4.9 %collective-permute-start.25 = (bf16[144,256]{1,0:T(8,128)(2,1)S(1)}, bf16[144,256]{1,0:T(8,128)(2,1)S(1)}, u32[]{:S(2)}, u32[]{:S(2)}) collective-permute-start(bf16[144,256]{1,0:T(8,128)(2,1)S(1)} %z_sum.1.refs_0_), channel_id=1, source_target_pairs={{0,16},{8,24},{16,0},{24,8},{1,17},{9,25},{17,1},{25,9},{2,18},{10... | collective-permute-start | bytes 221192 | tf_op jit(solution)/shard_map/ppermute | solution.py:34
  62.8 4.4 %collective-permute-start.24 = (bf16[144,256]{1,0:T(8,128)(2,1)S(1)}, bf16[144,256]{1,0:T(8,128)(2,1)S(1)}, u32[]{:S(2)}, u32[]{:S(2)}) collective-permute-start(bf16[144,256]{1,0:T(8,128)(2,1)S(1)} %z_sum.1.refs_0_), channel_id=1, source_target_pairs={{0,8},{8,0},{16,24},{24,16},{1,9},{9,1},{17,25},{25,17},{2,10},{10... | collective-permute-start | bytes 221192 | tf_op jit(solution)/shard_map/ppermute | solution.py:34

commit v5 on v4

--- a/solution.py
+++ b/solution.py
@@ -133,7 +133,7 @@
             dests[at] = jnp.dot(feat[...], w_in[i, :, cols:], preferred_element_type=F32)
             anchors[at] = jnp.dot(own[...], w_in[i, :, :cols], preferred_element_type=F32)
 
-    group = 8
+    group = 16
     pairs = group * window
     weight = w_out[...]
     for n in range(first_out.shape[0] // (blk * window)):
@@ -387,7 +387,7 @@
     rows = hidden // n_shard
     block = jax.ShapeDtypeStruct((rows + TAIL, cols), BF)
     order = list(range(n_z))[::-1]
-    early, later, last = order[: n_z // 2], order[n_z // 2 : -1], order[-1:]
+    early, late = order[: n_z // 2], order[n_z // 2 :]
 
     def blocks(targets):
         return jax.ShapeDtypeStruct((len(targets), rows + TAIL, cols), BF)
@@ -437,18 +437,15 @@
         name="gradient",
     )(*parts, win, first, act, weight_out)
     received = swap_core(send)
-    keep_later, send_later = rest(later, pre)
+    keep_late, send_late = rest(late, pre)
+    received, keep_late, send_late = lax.optimization_barrier((received, keep_late, send_late))
     sums = core_sum(keep, received)
-    pre, *sums = lax.optimization_barrier((pre, *sums))
-    received_later = swap_core(send_later)
-    keep_last, send_last = rest(last, pre)
-    received_last = swap_core(send_last)
-    keep_later, received_later, keep_last = lax.optimization_barrier((keep_later, received_later, keep_last))
-    sums = lax.optimization_barrier((*sums, *core_sum(keep_later, received_later)))
-    arrived = [along_z(x, j) for x, j in zip(sums, early + later)]
-    own_rows = [*core_sum(keep_last, received_last)] + arrived
+    arrived = [along_z(x, j) for x, j in zip(sums, early)]
+    *nearer, own = core_sum(keep_late, swap_core(send_late))
+    arrived += [along_z(x, j) for x, j in zip(nearer, late)]
+    own_rows = [own] + arrived
     reduced = pl.pallas_call(
-        functools.partial(z_sum_kernel, last + early + later),
+        functools.partial(z_sum_kernel, order[-1:] + order[:-1]),
         in_specs=[VMEM] * n_z,
         out_specs=VMEM,
         out_shape=block,

time: 68.6 us -> 67.3 us (0.981)
  Pallas kernels: 11.5 us -> 10.8 us
    ppermute x9 -> x8, starting transfers between devices: 2.23 us -> 1.93 us  [swap_core(): return lax.ppermute(array, 'shard', [(i, i ^ 1) for i in range(devices)])]
    pallas_call x2 -> x1, Pallas kernels: 1.9 us -> 1.77 us  [rest(): pl.pallas_call(functools.partial(rest_kernel, targets), grid=(steps,), in...]
  transfers between devices with their start and end apart: 27 -> 26, of which waited for: 12 -> 12; matrix products, arithmetic and copies ran while one was open for 10% -> 10% of each run, Pallas kernels for 3% -> 3%
where the time goes in v5:
time: 67.3 us; the launch traced here: 66.9 us
  starting transfers between devices  28 us (42%)
  waiting for transfers between devices  19.5 us (29%)
  Pallas kernels  10.8 us (16%)
  local copies, waits for them, and re-layouts  3.58 us (5%)
  other arithmetic  2.98 us (4%)
  matrix products  1.04 us (2%)
  between operations  0.93 us (1%)
    ppermute x9, starting transfers between devices, along_z(): lax.ppermute(array, 'shard', [(i, i ^ 2 * by) for i in range(devices)])  14.7 us
    ppermute x9, waiting for transfers between devices, along_z(): lax.ppermute(array, 'shard', [(i, i ^ 2 * by) for i in range(devices)])  12.2 us
    ppermute x9, starting transfers between devices, swap_region(): return lax.ppermute(array, 'region', [(i, i ^ by) for i in range(devices)])  11.4 us
    ppermute x9, waiting for transfers between devices, swap_region(): return lax.ppermute(array, 'region', [(i, i ^ by) for i in range(devices)])  6.25 us
    pallas_call x1, Pallas kernels, shards(): pl.pallas_call(functools.partial(score_kernel, n_region, n_z, blk), grid=...  5.34 us
    dynamic_slice x4, local copies, waits for them, and re-layouts, cut(): lax.dynamic_slice_in_dim(array, (region ^ i) * cols, cols, array.ndim - 1)  3.37 us
    pallas_call x1, Pallas kernels, shards(): pl.pallas_call(functools.partial(grad_kernel, n_region, early, window), g...  2.68 us
    ppermute x8, starting transfers between devices, swap_core(): return lax.ppermute(array, 'shard', [(i, i ^ 1) for i in range(devices)])  1.93 us
  transfers between devices with their start and end apart: 26, of which 12 were waited for; matrix products, arithmetic and copies ran while one was open for 10% of the time, Pallas kernels for 3%

profile of v5, /device:TPU:0, one launch (start us, length us, event | category | flops | bytes accessed | tf_op | source)
XLA Modules:
  0.0 66.9 jit_solution(13649651524290449508)
XLA Ops:
  0.7 0.9 %constant_dynamic-slice_fusion.9 = (bf16[64,256]{1,0:T(8,128)(2,1)S(1)}, bf16[64,256]{1,0:T(8,128)(2,1)S(1)}) fusion(bf16[64,1024]{1,0:T(8,128)(2,1)} %param.15, s32[]{:T(128)S(6)} %select_n.32, bf16[64,1024]{1,0:T(8,128)(2,1)} %param.14), kind=kLoop, calls=%fused_computation.52 | loop fusion | bytes 131076 | tf_op jit(solution)/shard_map/dynamic_slice | solution.py:311
  1.5 4.1 %collective-permute-start.1 = (bf16[128,256]{1,0:T(8,128)(2,1)S(1)}, bf16[128,256]{1,0:T(8,128)(2,1)S(1)}, u32[]{:S(2)}, u32[]{:S(2)}) collective-permute-start(bf16[128,256]{1,0:T(8,128)(2,1)S(1)} %pad_maximum_fusion.4), channel_id=1, source_target_pairs={{0,4},{1,5},{2,6},{3,7},{4,0},{5,1},{6,2},{7,3},{8,12},{9,13},{10,... | collective-permute-start | bytes 196616 | tf_op jit(solution)/shard_map/ppermute | solution.py:20
  5.6 1.0 %multiply_reduce_fusion = (f32[16]{0:T(128)S(1)}, f32[16,512]{1,0:T(8,128)S(1)}) fusion(bf16[1024,512]{1,0:T(8,128)(2,1)S(1)} %copy-done, s32[1024]{0:T(1024)} %param.10), kind=kOutput, calls=%fused_computation.34 | convolution fusion | flops 16809968 | bytes 1085504 | tf_op jit(solution)/shard_map/dot_general | solution.py:320
  6.8 1.4 %collective-permute-start.2 = (bf16[160,256]{1,0:T(8,128)(2,1)S(1)}, bf16[160,256]{1,0:T(8,128)(2,1)S(1)}, u32[]{:S(2)}, u32[]{:S(2)}) collective-permute-start(bf16[160,256]{1,0:T(8,128)(2,1)S(1)} %pad_maximum_fusion.3), channel_id=1, source_target_pairs={{0,6},{1,7},{2,4},{3,5},{4,2},{5,3},{6,0},{7,1},{8,14},{9,15},{10,... | collective-permute-start | bytes 245768 | tf_op jit(solution)/shard_map/ppermute | solution.py:20
  8.2 0.3 collective-permute-start
  8.5 0.7 %iota_compare_fusion.3 = pred[16,64]{1,0:T(8,128)(4,1)S(1)} fusion(s32[16]{0:T(128)} %param.12), kind=kLoop, calls=%fused_computation.41 | loop fusion | flops 1024 | bytes 1088 | tf_op jit(solution)/shard_map/lt | solution.py:330
  9.2 0.7 %fusion.4 = (s32[16,64]{1,0:T(8,128)S(1)}, s32[16,64]{1,0:T(8,128)S(1)}) fusion(s32[16,64]{1,0:T(8,128)} %param.11, s32[]{:T(128)S(6)} %mul.42, s32[16,64]{1,0:T(8,128)} %param.13), kind=kLoop, calls=%fused_computation.40 | loop fusion | flops 13312 | bytes 16388 | tf_op jit(solution)/shard_map/sub | solution.py:329
  10.0 0.6 select_reduce_fusion
  10.6 0.9 %constant_dynamic-slice_fusion = bf16[128,256]{1,0:T(8,128)(2,1)S(1)} fusion(bf16[128,1024]{1,0:T(8,128)(2,1)} %param.16, s32[]{:T(128)S(6)} %select_n.32), kind=kLoop, calls=%fused_computation.43 | loop fusion | bytes 131076 | tf_op jit(solution)/shard_map/dynamic_slice | solution.py:311
  11.4 0.8 %constant_dynamic-slice_fusion.8 = (bf16[64,256]{1,0:T(8,128)(2,1)S(1)}, bf16[64,256]{1,0:T(8,128)(2,1)S(1)}, bf16[64,256]{1,0:T(8,128)(2,1)S(1)}, bf16[64,256]{1,0:T(8,128)(2,1)S(1)}) fusion(bf16[64,1024]{1,0:T(8,128)(2,1)} %param.14, s32[]{:T(128)S(6)} %select_n.32, s32[]{:T(128)S(6)} %select_n.35, s32[]{:T(128)S(6)} %select_n.34, s32[]{:T(128)S(6)} %select_n.33), kind=kLoop, calls=%fused_computation.51 | loop fusion | bytes 262160 | tf_op jit(solution)/shard_map/dynamic_slice | solution.py:311
  12.2 0.8 %constant_dynamic-slice_fusion.7 = (bf16[64,256]{1,0:T(8,128)(2,1)S(1)}, bf16[64,256]{1,0:T(8,128)(2,1)S(1)}, bf16[64,256]{1,0:T(8,128)(2,1)S(1)}, bf16[64,256]{1,0:T(8,128)(2,1)S(1)}) fusion(bf16[64,1024]{1,0:T(8,128)(2,1)} %param.15, s32[]{:T(128)S(6)} %select_n.32, s32[]{:T(128)S(6)} %select_n.35, s32[]{:T(128)S(6)} %select_n.34, s32[]{:T(128)S(6)} %select_n.33), kind=kLoop, calls=%fused_computation.50 | loop fusion | bytes 262160 | tf_op jit(solution)/shard_map/dynamic_slice | solution.py:311
  13.1 0.7 %collective-permute-done = bf16[160,256]{1,0:T(8,128)(2,1)S(1)} collective-permute-done((bf16[160,256]{1,0:T(8,128)(2,1)S(1)}, bf16[160,256]{1,0:T(8,128)(2,1)S(1)}, u32[]{:S(2)}, u32[]{:S(2)}) %collective-permute-start) | collective-permute-done | bytes 81952 | tf_op jit(solution)/shard_map/ppermute | solution.py:20
  14.1 1.6 %collective-permute-start.8 = (bf16[496,256]{1,0:T(8,128)(2,1)S(1)}, bf16[496,256]{1,0:T(8,128)(2,1)S(1)}, u32[]{:S(2)}, u32[]{:S(2)}) collective-permute-start(bf16[496,256]{1,0:T(8,128)(2,1)S(1)} %constant_dynamic-update-slice_fusion.refs_2_), channel_id=1, source_target_pairs={{0,16},{8,24},{16,0},{24,8},{1,17},{9,25},{17,1},{25,9},{2,18},{10... | collective-permute-start | bytes 761864 | tf_op jit(solution)/shard_map/ppermute | solution.py:34
  15.7 1.5 %collective-permute-start.7 = (bf16[496,256]{1,0:T(8,128)(2,1)S(1)}, bf16[496,256]{1,0:T(8,128)(2,1)S(1)}, u32[]{:S(2)}, u32[]{:S(2)}) collective-permute-start(bf16[496,256]{1,0:T(8,128)(2,1)S(1)} %constant_dynamic-update-slice_fusion.refs_2_), channel_id=1, source_target_pairs={{0,8},{8,0},{16,24},{24,16},{1,9},{9,1},{17,25},{25,17},{2,10},{10... | collective-permute-start | bytes 761864 | tf_op jit(solution)/shard_map/ppermute | solution.py:34
  17.2 1.0 %collective-permute-start.6 = (bf16[192,256]{1,0:T(8,128)(2,1)S(1)}, bf16[192,256]{1,0:T(8,128)(2,1)S(1)}, u32[]{:S(2)}, u32[]{:S(2)}) collective-permute-start(bf16[192,256]{1,0:T(8,128)(2,1)S(1)} %pad_maximum_fusion.2), channel_id=1, source_target_pairs={{0,2},{1,3},{2,0},{3,1},{4,6},{5,7},{6,4},{7,5},{8,10},{9,11},{10,... | collective-permute-start | bytes 294920 | tf_op jit(solution)/shard_map/ppermute | solution.py:20
  18.2 2.1 %collective-permute-start.5 = (bf16[192,256]{1,0:T(8,128)(2,1)S(1)}, bf16[192,256]{1,0:T(8,128)(2,1)S(1)}, u32[]{:S(2)}, u32[]{:S(2)}) collective-permute-start(bf16[192,256]{1,0:T(8,128)(2,1)S(1)} %pad_maximum_fusion.2), channel_id=1, source_target_pairs={{0,4},{1,5},{2,6},{3,7},{4,0},{5,1},{6,2},{7,3},{8,12},{9,13},{10,... | collective-permute-start | bytes 294920 | tf_op jit(solution)/shard_map/ppermute | solution.py:20
  20.3 1.3 %collective-permute-start.4 = (bf16[192,256]{1,0:T(8,128)(2,1)S(1)}, bf16[192,256]{1,0:T(8,128)(2,1)S(1)}, u32[]{:S(2)}, u32[]{:S(2)}) collective-permute-start(bf16[192,256]{1,0:T(8,128)(2,1)S(1)} %pad_maximum_fusion.2), channel_id=1, source_target_pairs={{0,6},{1,7},{2,4},{3,5},{4,2},{5,3},{6,0},{7,1},{8,14},{9,15},{10,... | collective-permute-start | bytes 294920 | tf_op jit(solution)/shard_map/ppermute | solution.py:20
  21.6 1.4 %collective-permute-done.6 = bf16[192,256]{1,0:T(8,128)(2,1)S(1)} collective-permute-done((bf16[192,256]{1,0:T(8,128)(2,1)S(1)}, bf16[192,256]{1,0:T(8,128)(2,1)S(1)}, u32[]{:S(2)}, u32[]{:S(2)}) %collective-permute-start.6) | collective-permute-done | bytes 98336 | tf_op jit(solution)/shard_map/ppermute | solution.py:20
  22.9 1.2 %collective-permute-start.9 = (bf16[304,256]{1,0:T(8,128)(2,1)S(1)}, bf16[304,256]{1,0:T(8,128)(2,1)}, u32[]{:S(2)}, u32[]{:S(2)}) collective-permute-start(bf16[304,256]{1,0:T(8,128)(2,1)S(1)} %get-tuple-element.77), channel_id=1, source_target_pairs={{0,24},{8,16},{16,8},{24,0},{1,25},{9,17},{17,9},{25,1},{2,26},{10... | collective-permute-start | bytes 466952 | tf_op jit(solution)/shard_map/ppermute | solution.py:34
  24.1 4.6 %collective-permute-done.5 = bf16[192,256]{1,0:T(8,128)(2,1)S(1)} collective-permute-done((bf16[192,256]{1,0:T(8,128)(2,1)S(1)}, bf16[192,256]{1,0:T(8,128)(2,1)S(1)}, u32[]{:S(2)}, u32[]{:S(2)}) %collective-permute-start.5) | collective-permute-done | bytes 98336 | tf_op jit(solution)/shard_map/ppermute | solution.py:20
  28.9 0.6 collective-permute-start.10
  29.5 0.1 collective-permute-start.13
  29.5 0.4 collective-permute-start.12
  30.1 0.8 %dynamic-slice_convert_fusion = f32[256]{0:T(256)S(1)} fusion(bf16[1024]{0:T(1024)(128)(2,1)} %param.17, s32[]{:T(128)S(6)} %select_n.32), kind=kLoop, calls=%fused_computation.54 | loop fusion | flops 256 | bytes 1540 | tf_op jit(solution)/shard_map/reshape | solution.py:350
  30.8 0.1 copy.14.refs_12_.refs_7_
  31.0 1.1 %collective-permute-done.14.refs_11_ = bf16[304,256]{1,0:T(8,128)(2,1)} collective-permute-done((bf16[304,256]{1,0:T(8,128)(2,1)}, bf16[304,256]{1,0:T(8,128)(2,1)}, u32[]{:S(2)}, u32[]{:S(2)}) %collective-permute-start.14) | collective-permute-done | bytes 155680 | tf_op jit(solution)/shard_map/ppermute | solution.py:29
  32.1 5.3 %scores.1 = (bf16[5120,1024]{1,0:T(8,128)(2,1)S(1)}, bf16[256,5120]{1,0:T(8,128)(2,1)S(1)}, f32[64,128]{1,0:T(8,128)S(1)}, f32[4,16,128]{2,1,0:T(8,128)S(1)}) custom-call(bf16[4,128,256]{2,1,0:T(8,128)(2,1)S(1)} %pad_maximum_fusion.1.refs_0_, bf16[704,256]{1,0:T(8,128)(2,1)S(1)} %pad_maximum_fusion.refs_1_, ...), custom_call_target="tpu_custom_call" | custom-call | tf_op jit(solution)/shard_map/scores/pallas_call | solution.py:362
  37.4 1.0 %collective-permute-start.17 = (f32[64,128]{1,0:T(8,128)S(1)}, f32[64,128]{1,0:T(8,128)S(1)}, u32[]{:S(2)}, u32[]{:S(2)}) collective-permute-start(f32[64,128]{1,0:T(8,128)S(1)} %get-tuple-element.35.refs_0_), channel_id=1, source_target_pairs={{0,24},{8,16},{16,8},{24,0},{1,25},{9,17},{17,9},{25,1},{2,26},{10... | collective-permute-start | bytes 98312 | tf_op jit(solution)/shard_map/ppermute | solution.py:34
  38.4 1.0 %collective-permute-start.16 = (f32[64,128]{1,0:T(8,128)S(1)}, f32[64,128]{1,0:T(8,128)S(1)}, u32[]{:S(2)}, u32[]{:S(2)}) collective-permute-start(f32[64,128]{1,0:T(8,128)S(1)} %get-tuple-element.35.refs_0_), channel_id=1, source_target_pairs={{0,16},{8,24},{16,0},{24,8},{1,17},{9,25},{17,1},{25,9},{2,18},{10... | collective-permute-start | bytes 98312 | tf_op jit(solution)/shard_map/ppermute | solution.py:34
  39.4 1.5 %collective-permute-start.15 = (f32[64,128]{1,0:T(8,128)S(1)}, f32[64,128]{1,0:T(8,128)S(1)}, u32[]{:S(2)}, u32[]{:S(2)}) collective-permute-start(f32[64,128]{1,0:T(8,128)S(1)} %get-tuple-element.35.refs_0_), channel_id=1, source_target_pairs={{0,8},{8,0},{16,24},{24,16},{1,9},{9,1},{17,25},{25,17},{2,10},{10... | collective-permute-start | bytes 98312 | tf_op jit(solution)/shard_map/ppermute | solution.py:34
  40.9 1.5 %collective-permute-done.17.refs_3_ = f32[64,128]{1,0:T(8,128)S(1)} collective-permute-done((f32[64,128]{1,0:T(8,128)S(1)}, f32[64,128]{1,0:T(8,128)S(1)}, u32[]{:S(2)}, u32[]{:S(2)}) %collective-permute-start.17) | collective-permute-done | bytes 32800 | tf_op jit(solution)/shard_map/ppermute | solution.py:34
  42.5 0.1 collective-permute-done.16.refs_2_
  42.6 0.7 %collective-permute-done.15.refs_1_ = f32[64,128]{1,0:T(8,128)S(1)} collective-permute-done((f32[64,128]{1,0:T(8,128)S(1)}, f32[64,128]{1,0:T(8,128)S(1)}, u32[]{:S(2)}, u32[]{:S(2)}) %collective-permute-start.15) | collective-permute-done | bytes 32800 | tf_op jit(solution)/shard_map/ppermute | solution.py:34
  43.4 2.7 %gradient.1 = (bf16[256,5120]{1,0:T(8,128)(2,1)S(1)}, bf16[16,256]{1,0:T(8,128)(2,1)S(1)}, bf16[2,144,256]{2,1,0:T(8,128)(2,1)S(1)}, bf16[2,144,256]{2,1,0:T(8,128)(2,1)S(1)}) custom-call(f32[64,128]{1,0:T(8,128)S(1)} %get-tuple-element.35.refs_0_, f32[64,128]{1,0:T(8,128)S(1)} %collective-permute-done.15.refs_1_, ...), custom_call_target="tpu_custom_call" | custom-call | tf_op jit(solution)/shard_map/gradient/pallas_call | solution.py:420
  46.1 1.8 %gradient_rest.1 = (bf16[2,144,256]{2,1,0:T(8,128)(2,1)S(1)}, bf16[2,144,256]{2,1,0:T(8,128)(2,1)S(1)}) custom-call(bf16[5120,1024]{1,0:T(8,128)(2,1)S(1)} %get-tuple-element.37.refs_5_.refs_0_, bf16[256,5120]{1,0:T(8,128)(2,1)S(1)} %get-tuple-element.40.refs_1_, bf16[16,256]{1,0:T(8,128)(2,1)S(1)} %get-tuple-element.41.refs_2_), custom_call_target="tpu_custom_call" | custom-call | tf_op jit(solution)/shard_map/gradient_rest/pallas_call | solution.py:409
  47.9 0.6 collective-permute-start.19
  48.5 2.3 %collective-permute-start.20 = (bf16[144,256]{1,0:T(8,128)(2,1)S(1)}, bf16[144,256]{1,0:T(8,128)(2,1)S(1)}, u32[]{:S(2)}, u32[]{:S(2)}) collective-permute-start(bf16[144,256]{1,0:T(8,128)(2,1)S(1)} %get-tuple-element.49), channel_id=1, source_target_pairs={{0,6},{1,7},{2,4},{3,5},{4,2},{5,3},{6,0},{7,1},{8,14},{9,15},{10,... | collective-permute-start | bytes 221192 | tf_op jit(solution)/shard_map/ppermute | solution.py:20
  50.8 0.8 %collective-permute-start.21 = (bf16[144,256]{1,0:T(8,128)(2,1)S(1)}, bf16[144,256]{1,0:T(8,128)(2,1)S(1)}, u32[]{:S(2)}, u32[]{:S(2)}) collective-permute-start(bf16[144,256]{1,0:T(8,128)(2,1)S(1)} %get-tuple-element.50), channel_id=1, source_target_pairs={{0,4},{1,5},{2,6},{3,7},{4,0},{5,1},{6,2},{7,3},{8,12},{9,13},{10,... | collective-permute-start | bytes 221192 | tf_op jit(solution)/shard_map/ppermute | solution.py:20
  51.7 1.4 %collective-permute-start.22 = (bf16[144,256]{1,0:T(8,128)(2,1)S(1)}, bf16[144,256]{1,0:T(8,128)(2,1)S(1)}, u32[]{:S(2)}, u32[]{:S(2)}) collective-permute-start(bf16[144,256]{1,0:T(8,128)(2,1)S(1)} %get-tuple-element.51), channel_id=1, source_target_pairs={{0,2},{1,3},{2,0},{3,1},{4,6},{5,7},{6,4},{7,5},{8,10},{9,11},{10,... | collective-permute-start | bytes 221192 | tf_op jit(solution)/shard_map/ppermute | solution.py:20
  53.1 2.1 %collective-permute-done.20.refs_1_ = bf16[144,256]{1,0:T(8,128)(2,1)S(1)} collective-permute-done((bf16[144,256]{1,0:T(8,128)(2,1)S(1)}, bf16[144,256]{1,0:T(8,128)(2,1)S(1)}, u32[]{:S(2)}, u32[]{:S(2)}) %collective-permute-start.20) | collective-permute-done | bytes 73760 | tf_op jit(solution)/shard_map/ppermute | solution.py:20
  55.1 3.4 %collective-permute-done.21.refs_2_ = bf16[144,256]{1,0:T(8,128)(2,1)S(1)} collective-permute-done((bf16[144,256]{1,0:T(8,128)(2,1)S(1)}, bf16[144,256]{1,0:T(8,128)(2,1)S(1)}, u32[]{:S(2)}, u32[]{:S(2)}) %collective-permute-start.21) | collective-permute-done | bytes 73760 | tf_op jit(solution)/shard_map/ppermute | solution.py:20
  58.6 1.5 %collective-permute-start.25 = (bf16[144,256]{1,0:T(8,128)(2,1)S(1)}, bf16[144,256]{1,0:T(8,128)(2,1)S(1)}, u32[]{:S(2)}, u32[]{:S(2)}) collective-permute-start(bf16[144,256]{1,0:T(8,128)(2,1)S(1)} %z_sum.1.refs_0_), channel_id=1, source_target_pairs={{0,24},{8,16},{16,8},{24,0},{1,25},{9,17},{17,9},{25,1},{2,26},{10... | collective-permute-start | bytes 221192 | tf_op jit(solution)/shard_map/ppermute | solution.py:34
  60.1 1.5 %collective-permute-start.24 = (bf16[144,256]{1,0:T(8,128)(2,1)S(1)}, bf16[144,256]{1,0:T(8,128)(2,1)S(1)}, u32[]{:S(2)}, u32[]{:S(2)}) collective-permute-start(bf16[144,256]{1,0:T(8,128)(2,1)S(1)} %z_sum.1.refs_0_), channel_id=1, source_target_pairs={{0,16},{8,24},{16,0},{24,8},{1,17},{9,25},{17,1},{25,9},{2,18},{10... | collective-permute-start | bytes 221192 | tf_op jit(solution)/shard_map/ppermute | solution.py:34
  61.6 0.5 collective-permute-start.23
  62.2 2.6 %collective-permute-done.25.refs_3_ = bf16[144,256]{1,0:T(8,128)(2,1)S(1)} collective-permute-done((bf16[144,256]{1,0:T(8,128)(2,1)S(1)}, bf16[144,256]{1,0:T(8,128)(2,1)S(1)}, u32[]{:S(2)}, u32[]{:S(2)}) %collective-permute-start.25) | collective-permute-done | bytes 73760 | tf_op jit(solution)/shard_map/ppermute | solution.py:34
  64.8 0.2 collective-permute-done.24.refs_2_
  65.0 1.0 %collective-permute-done.23.refs_1_ = bf16[144,256]{1,0:T(8,128)(2,1)S(1)} collective-permute-done((bf16[144,256]{1,0:T(8,128)(2,1)S(1)}, bf16[144,256]{1,0:T(8,128)(2,1)S(1)}, u32[]{:S(2)}, u32[]{:S(2)}) %collective-permute-start.23) | collective-permute-done | bytes 73760 | tf_op jit(solution)/shard_map/ppermute | solution.py:34
  66.0 0.9 %finish.1 = (f32[128,1024]{1,0:T(8,128)}, f32[1,1024]{1,0:T(1,128)}, f32[1,1]{1,0:T(1,128)}) custom-call(bf16[144,256]{1,0:T(8,128)(2,1)S(1)} %z_sum.1.refs_0_, bf16[144,256]{1,0:T(8,128)(2,1)S(1)} %collective-permute-done.23.refs_1_, bf16[144,256]{1,0:T(8,128)(2,1)S(1)} %collective-permute-done.24.refs_2_, bf16[144,256]{1,0:T(8,128)(2,1)S(1)} %collective-permute-done.25.refs_3_), custom_call_target="tpu_custom_call" | custom-call | tf_op jit(solution)/shard_map/finish/pallas_call | solution.py:457
  (48 shorter events, 0.8 us)
Async XLA Ops:
  0.6 5.0 %copy-start = (bf16[1024,512]{1,0:T(8,128)(2,1)S(1)}, bf16[1024,512]{1,0:T(8,128)(2,1)}, u32[]{:S(2)}) copy-start(bf16[1024,512]{1,0:T(8,128)(2,1)} %param.9) | copy-start | bytes 3145732
  1.5 12.3 %collective-permute-start.1 = (bf16[128,256]{1,0:T(8,128)(2,1)S(1)}, bf16[128,256]{1,0:T(8,128)(2,1)S(1)}, u32[]{:S(2)}, u32[]{:S(2)}) collective-permute-start(bf16[128,256]{1,0:T(8,128)(2,1)S(1)} %pad_maximum_fusion.4), channel_id=1, source_target_pairs={{0,4},{1,5},{2,6},{3,7},{4,0},{5,1},{6,2},{7,3},{8,12},{9,13},{10,... | collective-permute-start | bytes 196616 | tf_op jit(solution)/shard_map/ppermute | solution.py:20
  6.8 7.1 %collective-permute-start.2 = (bf16[160,256]{1,0:T(8,128)(2,1)S(1)}, bf16[160,256]{1,0:T(8,128)(2,1)S(1)}, u32[]{:S(2)}, u32[]{:S(2)}) collective-permute-start(bf16[160,256]{1,0:T(8,128)(2,1)S(1)} %pad_maximum_fusion.3), channel_id=1, source_target_pairs={{0,6},{1,7},{2,4},{3,5},{4,2},{5,3},{6,0},{7,1},{8,14},{9,15},{10,... | collective-permute-start | bytes 245768 | tf_op jit(solution)/shard_map/ppermute | solution.py:20
  8.2 5.6 %collective-permute-start = (bf16[160,256]{1,0:T(8,128)(2,1)S(1)}, bf16[160,256]{1,0:T(8,128)(2,1)S(1)}, u32[]{:S(2)}, u32[]{:S(2)}) collective-permute-start(bf16[160,256]{1,0:T(8,128)(2,1)S(1)} %pad_maximum_fusion.3), channel_id=1, source_target_pairs={{0,2},{1,3},{2,0},{3,1},{4,6},{5,7},{6,4},{7,5},{8,10},{9,11},{10,... | collective-permute-start | bytes 245768 | tf_op jit(solution)/shard_map/ppermute | solution.py:20
  14.0 3.2 %collective-permute-start.3 = (bf16[496,256]{1,0:T(8,128)(2,1)S(1)}, bf16[496,256]{1,0:T(8,128)(2,1)S(1)}, u32[]{:S(2)}, u32[]{:S(2)}) collective-permute-start(bf16[496,256]{1,0:T(8,128)(2,1)S(1)} %constant_dynamic-update-slice_fusion.refs_2_), channel_id=1, source_target_pairs={{0,1},{1,0},{2,3},{3,2},{4,5},{5,4},{6,7},{7,6},{8,9},{9,8},{10,11... | collective-permute-start | bytes 761864 | tf_op jit(solution)/shard_map/ppermute | solution.py:29
  14.1 15.3 %collective-permute-start.8 = (bf16[496,256]{1,0:T(8,128)(2,1)S(1)}, bf16[496,256]{1,0:T(8,128)(2,1)S(1)}, u32[]{:S(2)}, u32[]{:S(2)}) collective-permute-start(bf16[496,256]{1,0:T(8,128)(2,1)S(1)} %constant_dynamic-update-slice_fusion.refs_2_), channel_id=1, source_target_pairs={{0,16},{8,24},{16,0},{24,8},{1,17},{9,25},{17,1},{25,9},{2,18},{10... | collective-permute-start | bytes 761864 | tf_op jit(solution)/shard_map/ppermute | solution.py:34
  15.7 13.8 %collective-permute-start.7 = (bf16[496,256]{1,0:T(8,128)(2,1)S(1)}, bf16[496,256]{1,0:T(8,128)(2,1)S(1)}, u32[]{:S(2)}, u32[]{:S(2)}) collective-permute-start(bf16[496,256]{1,0:T(8,128)(2,1)S(1)} %constant_dynamic-update-slice_fusion.refs_2_), channel_id=1, source_target_pairs={{0,8},{8,0},{16,24},{24,16},{1,9},{9,1},{17,25},{25,17},{2,10},{10... | collective-permute-start | bytes 761864 | tf_op jit(solution)/shard_map/ppermute | solution.py:34
  17.2 5.7 %collective-permute-start.6 = (bf16[192,256]{1,0:T(8,128)(2,1)S(1)}, bf16[192,256]{1,0:T(8,128)(2,1)S(1)}, u32[]{:S(2)}, u32[]{:S(2)}) collective-permute-start(bf16[192,256]{1,0:T(8,128)(2,1)S(1)} %pad_maximum_fusion.2), channel_id=1, source_target_pairs={{0,2},{1,3},{2,0},{3,1},{4,6},{5,7},{6,4},{7,5},{8,10},{9,11},{10,... | collective-permute-start | bytes 294920 | tf_op jit(solution)/shard_map/ppermute | solution.py:20
  18.2 10.5 %collective-permute-start.5 = (bf16[192,256]{1,0:T(8,128)(2,1)S(1)}, bf16[192,256]{1,0:T(8,128)(2,1)S(1)}, u32[]{:S(2)}, u32[]{:S(2)}) collective-permute-start(bf16[192,256]{1,0:T(8,128)(2,1)S(1)} %pad_maximum_fusion.2), channel_id=1, source_target_pairs={{0,4},{1,5},{2,6},{3,7},{4,0},{5,1},{6,2},{7,3},{8,12},{9,13},{10,... | collective-permute-start | bytes 294920 | tf_op jit(solution)/shard_map/ppermute | solution.py:20
  20.3 8.5 %collective-permute-start.4 = (bf16[192,256]{1,0:T(8,128)(2,1)S(1)}, bf16[192,256]{1,0:T(8,128)(2,1)S(1)}, u32[]{:S(2)}, u32[]{:S(2)}) collective-permute-start(bf16[192,256]{1,0:T(8,128)(2,1)S(1)} %pad_maximum_fusion.2), channel_id=1, source_target_pairs={{0,6},{1,7},{2,4},{3,5},{4,2},{5,3},{6,0},{7,1},{8,14},{9,15},{10,... | collective-permute-start | bytes 294920 | tf_op jit(solution)/shard_map/ppermute | solution.py:20
  22.9 7.0 %collective-permute-start.9 = (bf16[304,256]{1,0:T(8,128)(2,1)S(1)}, bf16[304,256]{1,0:T(8,128)(2,1)}, u32[]{:S(2)}, u32[]{:S(2)}) collective-permute-start(bf16[304,256]{1,0:T(8,128)(2,1)S(1)} %get-tuple-element.77), channel_id=1, source_target_pairs={{0,24},{8,16},{16,8},{24,0},{1,25},{9,17},{17,9},{25,1},{2,26},{10... | collective-permute-start | bytes 466952 | tf_op jit(solution)/shard_map/ppermute | solution.py:34
  28.8 3.3 %collective-permute-start.11 = (bf16[704,256]{1,0:T(8,128)(2,1)S(1)}, bf16[704,256]{1,0:T(8,128)(2,1)S(1)}, u32[]{:S(2)}, u32[]{:S(2)}) collective-permute-start(bf16[704,256]{1,0:T(8,128)(2,1)S(1)} %pad_maximum_fusion.refs_1_), channel_id=1, source_target_pairs={{0,1},{1,0},{2,3},{3,2},{4,5},{5,4},{6,7},{7,6},{8,9},{9,8},{10,11... | collective-permute-start | bytes 1081352 | tf_op jit(solution)/shard_map/ppermute | solution.py:29
  28.9 2.1 %collective-permute-start.10 = (bf16[4,128,256]{2,1,0:T(8,128)(2,1)S(1)}, bf16[4,128,256]{2,1,0:T(8,128)(2,1)S(1)}, u32[]{:S(2)}, u32[]{:S(2)}) collective-permute-start(bf16[4,128,256]{2,1,0:T(8,128)(2,1)S(1)} %pad_maximum_fusion.1.refs_0_), channel_id=1, source_target_pairs={{0,1},{1,0},{2,3},{3,2},{4,5},{5,4},{6,7},{7,6},{8,9},{9,8},{10,11... | collective-permute-start | bytes 786440 | tf_op jit(solution)/shard_map/ppermute | solution.py:29
  29.5 2.6 %collective-permute-start.13 = (bf16[496,256]{1,0:T(8,128)(2,1)S(1)}, bf16[496,256]{1,0:T(8,128)(2,1)}, u32[]{:S(2)}, u32[]{:S(2)}) collective-permute-start(bf16[496,256]{1,0:T(8,128)(2,1)S(1)} %collective-permute-done.8.refs_4_), channel_id=1, source_target_pairs={{0,1},{1,0},{2,3},{3,2},{4,5},{5,4},{6,7},{7,6},{8,9},{9,8},{10,11... | collective-permute-start | bytes 761864 | tf_op jit(solution)/shard_map/ppermute | solution.py:29
  29.5 2.5 %collective-permute-start.12 = (bf16[496,256]{1,0:T(8,128)(2,1)S(1)}, bf16[496,256]{1,0:T(8,128)(2,1)}, u32[]{:S(2)}, u32[]{:S(2)}) collective-permute-start(bf16[496,256]{1,0:T(8,128)(2,1)S(1)} %collective-permute-done.7.refs_3_), channel_id=1, source_target_pairs={{0,1},{1,0},{2,3},{3,2},{4,5},{5,4},{6,7},{7,6},{8,9},{9,8},{10,11... | collective-permute-start | bytes 761864 | tf_op jit(solution)/shard_map/ppermute | solution.py:29
  30.0 2.1 %collective-permute-start.14 = (bf16[304,256]{1,0:T(8,128)(2,1)}, bf16[304,256]{1,0:T(8,128)(2,1)}, u32[]{:S(2)}, u32[]{:S(2)}) collective-permute-start(bf16[304,256]{1,0:T(8,128)(2,1)} %collective-permute-done.9.refs_5_), channel_id=1, source_target_pairs={{0,1},{1,0},{2,3},{3,2},{4,5},{5,4},{6,7},{7,6},{8,9},{9,8},{10,11... | collective-permute-start | bytes 466952 | tf_op jit(solution)/shard_map/ppermute | solution.py:29
  37.4 5.1 %collective-permute-start.17 = (f32[64,128]{1,0:T(8,128)S(1)}, f32[64,128]{1,0:T(8,128)S(1)}, u32[]{:S(2)}, u32[]{:S(2)}) collective-permute-start(f32[64,128]{1,0:T(8,128)S(1)} %get-tuple-element.35.refs_0_), channel_id=1, source_target_pairs={{0,24},{8,16},{16,8},{24,0},{1,25},{9,17},{17,9},{25,1},{2,26},{10... | collective-permute-start | bytes 98312 | tf_op jit(solution)/shard_map/ppermute | solution.py:34
  38.4 4.2 %collective-permute-start.16 = (f32[64,128]{1,0:T(8,128)S(1)}, f32[64,128]{1,0:T(8,128)S(1)}, u32[]{:S(2)}, u32[]{:S(2)}) collective-permute-start(f32[64,128]{1,0:T(8,128)S(1)} %get-tuple-element.35.refs_0_), channel_id=1, source_target_pairs={{0,16},{8,24},{16,0},{24,8},{1,17},{9,25},{17,1},{25,9},{2,18},{10... | collective-permute-start | bytes 98312 | tf_op jit(solution)/shard_map/ppermute | solution.py:34
  39.4 3.9 %collective-permute-start.15 = (f32[64,128]{1,0:T(8,128)S(1)}, f32[64,128]{1,0:T(8,128)S(1)}, u32[]{:S(2)}, u32[]{:S(2)}) collective-permute-start(f32[64,128]{1,0:T(8,128)S(1)} %get-tuple-element.35.refs_0_), channel_id=1, source_target_pairs={{0,8},{8,0},{16,24},{24,16},{1,9},{9,1},{17,25},{25,17},{2,10},{10... | collective-permute-start | bytes 98312 | tf_op jit(solution)/shard_map/ppermute | solution.py:34
  46.0 1.9 %collective-permute-start.18 = (bf16[2,144,256]{2,1,0:T(8,128)(2,1)S(1)}, bf16[2,144,256]{2,1,0:T(8,128)(2,1)S(1)}, u32[]{:S(2)}, u32[]{:S(2)}) collective-permute-start(bf16[2,144,256]{2,1,0:T(8,128)(2,1)S(1)} %get-tuple-element.39), channel_id=1, source_target_pairs={{0,1},{1,0},{2,3},{3,2},{4,5},{5,4},{6,7},{7,6},{8,9},{9,8},{10,11... | collective-permute-start | bytes 442376 | tf_op jit(solution)/shard_map/ppermute | solution.py:29
  47.9 3.7 %collective-permute-start.19 = (bf16[2,144,256]{2,1,0:T(8,128)(2,1)S(1)}, bf16[2,144,256]{2,1,0:T(8,128)(2,1)S(1)}, u32[]{:S(2)}, u32[]{:S(2)}) collective-permute-start(bf16[2,144,256]{2,1,0:T(8,128)(2,1)S(1)} %get-tuple-element.45), channel_id=1, source_target_pairs={{0,1},{1,0},{2,3},{3,2},{4,5},{5,4},{6,7},{7,6},{8,9},{9,8},{10,11... | collective-permute-start | bytes 442376 | tf_op jit(solution)/shard_map/ppermute | solution.py:29
  48.5 6.6 %collective-permute-start.20 = (bf16[144,256]{1,0:T(8,128)(2,1)S(1)}, bf16[144,256]{1,0:T(8,128)(2,1)S(1)}, u32[]{:S(2)}, u32[]{:S(2)}) collective-permute-start(bf16[144,256]{1,0:T(8,128)(2,1)S(1)} %get-tuple-element.49), channel_id=1, source_target_pairs={{0,6},{1,7},{2,4},{3,5},{4,2},{5,3},{6,0},{7,1},{8,14},{9,15},{10,... | collective-permute-start | bytes 221192 | tf_op jit(solution)/shard_map/ppermute | solution.py:20
  50.8 7.7 %collective-permute-start.21 = (bf16[144,256]{1,0:T(8,128)(2,1)S(1)}, bf16[144,256]{1,0:T(8,128)(2,1)S(1)}, u32[]{:S(2)}, u32[]{:S(2)}) collective-permute-start(bf16[144,256]{1,0:T(8,128)(2,1)S(1)} %get-tuple-element.50), channel_id=1, source_target_pairs={{0,4},{1,5},{2,6},{3,7},{4,0},{5,1},{6,2},{7,3},{8,12},{9,13},{10,... | collective-permute-start | bytes 221192 | tf_op jit(solution)/shard_map/ppermute | solution.py:20
  51.7 6.9 %collective-permute-start.22 = (bf16[144,256]{1,0:T(8,128)(2,1)S(1)}, bf16[144,256]{1,0:T(8,128)(2,1)S(1)}, u32[]{:S(2)}, u32[]{:S(2)}) collective-permute-start(bf16[144,256]{1,0:T(8,128)(2,1)S(1)} %get-tuple-element.51), channel_id=1, source_target_pairs={{0,2},{1,3},{2,0},{3,1},{4,6},{5,7},{6,4},{7,5},{8,10},{9,11},{10,... | collective-permute-start | bytes 221192 | tf_op jit(solution)/shard_map/ppermute | solution.py:20
  58.6 6.1 %collective-permute-start.25 = (bf16[144,256]{1,0:T(8,128)(2,1)S(1)}, bf16[144,256]{1,0:T(8,128)(2,1)S(1)}, u32[]{:S(2)}, u32[]{:S(2)}) collective-permute-start(bf16[144,256]{1,0:T(8,128)(2,1)S(1)} %z_sum.1.refs_0_), channel_id=1, source_target_pairs={{0,24},{8,16},{16,8},{24,0},{1,25},{9,17},{17,9},{25,1},{2,26},{10... | collective-permute-start | bytes 221192 | tf_op jit(solution)/shard_map/ppermute | solution.py:34
  60.1 4.9 %collective-permute-start.24 = (bf16[144,256]{1,0:T(8,128)(2,1)S(1)}, bf16[144,256]{1,0:T(8,128)(2,1)S(1)}, u32[]{:S(2)}, u32[]{:S(2)}) collective-permute-start(bf16[144,256]{1,0:T(8,128)(2,1)S(1)} %z_sum.1.refs_0_), channel_id=1, source_target_pairs={{0,16},{8,24},{16,0},{24,8},{1,17},{9,25},{17,1},{25,9},{2,18},{10... | collective-permute-start | bytes 221192 | tf_op jit(solution)/shard_map/ppermute | solution.py:34
  61.6 4.4 %collective-permute-start.23 = (bf16[144,256]{1,0:T(8,128)(2,1)S(1)}, bf16[144,256]{1,0:T(8,128)(2,1)S(1)}, u32[]{:S(2)}, u32[]{:S(2)}) collective-permute-start(bf16[144,256]{1,0:T(8,128)(2,1)S(1)} %z_sum.1.refs_0_), channel_id=1, source_target_pairs={{0,8},{8,0},{16,24},{24,16},{1,9},{9,1},{17,25},{25,17},{2,10},{10... | collective-permute-start | bytes 221192 | tf_op jit(solution)/shard_map/ppermute | solution.py:34

commit v6 on v5

--- a/solution.py
+++ b/solution.py
@@ -133,32 +133,32 @@
             dests[at] = jnp.dot(feat[...], w_in[i, :, cols:], preferred_element_type=F32)
             anchors[at] = jnp.dot(own[...], w_in[i, :, :cols], preferred_element_type=F32)
 
-    group = 16
-    pairs = group * window
     weight = w_out[...]
-    for n in range(first_out.shape[0] // (blk * window)):
-        reach_at = pl.ds(pl.multiple_of((step + n) * window, window), window)
-        own_at = pl.ds(pl.multiple_of((step + n) * blk, blk), blk)
-        for c in range(0, blk, group):
-            base = (n * blk + c) * window
+    regions = first_out.shape[0] // (blk * window)
+    together = 2 if regions % 2 == 0 else 1
+    pairs = together * blk * window
+    for n in range(0, regions, together):
+        for m in range(n, n + together):
+            reach_at = pl.ds(pl.multiple_of((step + m) * window, window), window)
+            own_at = pl.ds(pl.multiple_of((step + m) * blk, blk), blk)
             for k in range(n_region):
                 dest = dests[k, reach_at, :]
                 line = anchors[k, own_at, :]
-                for a in range(group):
-                    total = dest + line[c + a : c + a + 1, :]
-                    at = slice(base + a * window, base + (a + 1) * window)
+                for a in range(blk):
+                    total = dest + line[a : a + 1, :]
+                    at = slice((m * blk + a) * window, (m * blk + a + 1) * window)
                     first_out[at, k * cols : (k + 1) * cols] = jnp.maximum(total.astype(BF), 0)
-            second = lax.dot_general(
-                w_mid_t[...], first_out[base : base + pairs, :], (((1,), (1,)), ((), ())), preferred_element_type=F32
+        base = n * blk * window
+        second = lax.dot_general(
+            w_mid_t[...], first_out[base : base + pairs, :], (((1,), (1,)), ((), ())), preferred_element_type=F32
+        )
+        active = jnp.maximum(second, 0.0)
+        act_out[:, base : base + pairs] = active.astype(BF)
+        score = jnp.sum(active * weight, axis=0, keepdims=True)
+        for a in range(together * blk):
+            score_out[n * blk + a : n * blk + a + 1, :] = jnp.concatenate(
+                [score[:, a * window : (a + 1) * window], jnp.zeros((1, 128 - window), F32)], axis=1
             )
-            active = jnp.maximum(second, 0.0)
-            act_out[:, base : base + pairs] = active.astype(BF)
-            score = jnp.sum(active * weight, axis=0, keepdims=True)
-            for a in range(group):
-                row = n * blk + c + a
-                score_out[row : row + 1, :] = jnp.concatenate(
-                    [score[:, a * window : (a + 1) * window], jnp.zeros((1, 128 - window), F32)], axis=1
-                )
 
 
 def add_targets(grad, pre, first, targets, width):

time: 67.3 us -> 67.4 us (level)
  no operation moved by 1% of the time
where the time goes in v6:
time: 67.4 us; the launch traced here: 66.9 us
  starting transfers between devices  28 us (42%)
  waiting for transfers between devices  19.5 us (29%)
  Pallas kernels  10.8 us (16%)
  local copies, waits for them, and re-layouts  3.58 us (5%)
  other arithmetic  2.98 us (4%)
  matrix products  1.04 us (2%)
  between operations  0.93 us (1%)
    ppermute x9, starting transfers between devices, along_z(): lax.ppermute(array, 'shard', [(i, i ^ 2 * by) for i in range(devices)])  14.7 us
    ppermute x9, waiting for transfers between devices, along_z(): lax.ppermute(array, 'shard', [(i, i ^ 2 * by) for i in range(devices)])  12.2 us
    ppermute x9, starting transfers between devices, swap_region(): return lax.ppermute(array, 'region', [(i, i ^ by) for i in range(devices)])  11.4 us
    ppermute x9, waiting for transfers between devices, swap_region(): return lax.ppermute(array, 'region', [(i, i ^ by) for i in range(devices)])  6.25 us
    pallas_call x1, Pallas kernels, shards(): pl.pallas_call(functools.partial(score_kernel, n_region, n_z, blk), grid=...  5.33 us
    dynamic_slice x4, local copies, waits for them, and re-layouts, cut(): lax.dynamic_slice_in_dim(array, (region ^ i) * cols, cols, array.ndim - 1)  3.37 us
    pallas_call x1, Pallas kernels, shards(): pl.pallas_call(functools.partial(grad_kernel, n_region, early, window), g...  2.68 us
    ppermute x8, starting transfers between devices, swap_core(): return lax.ppermute(array, 'shard', [(i, i ^ 1) for i in range(devices)])  1.93 us
  transfers between devices with their start and end apart: 26, of which 12 were waited for; matrix products, arithmetic and copies ran while one was open for 10% of the time, Pallas kernels for 3%

profile of v6, /device:TPU:0, one launch (start us, length us, event | category | flops | bytes accessed | tf_op | source)
XLA Modules:
  0.0 66.9 jit_solution(13778808597320800424)
XLA Ops:
  0.7 0.9 %constant_dynamic-slice_fusion.9 = (bf16[64,256]{1,0:T(8,128)(2,1)S(1)}, bf16[64,256]{1,0:T(8,128)(2,1)S(1)}) fusion(bf16[64,1024]{1,0:T(8,128)(2,1)} %param.15, s32[]{:T(128)S(6)} %select_n.32, bf16[64,1024]{1,0:T(8,128)(2,1)} %param.14), kind=kLoop, calls=%fused_computation.52 | loop fusion | bytes 131076 | tf_op jit(solution)/shard_map/dynamic_slice | solution.py:311
  1.5 4.1 %collective-permute-start.1 = (bf16[128,256]{1,0:T(8,128)(2,1)S(1)}, bf16[128,256]{1,0:T(8,128)(2,1)S(1)}, u32[]{:S(2)}, u32[]{:S(2)}) collective-permute-start(bf16[128,256]{1,0:T(8,128)(2,1)S(1)} %pad_maximum_fusion.4), channel_id=1, source_target_pairs={{0,4},{1,5},{2,6},{3,7},{4,0},{5,1},{6,2},{7,3},{8,12},{9,13},{10,... | collective-permute-start | bytes 196616 | tf_op jit(solution)/shard_map/ppermute | solution.py:20
  5.6 1.0 %multiply_reduce_fusion = (f32[16]{0:T(128)S(1)}, f32[16,512]{1,0:T(8,128)S(1)}) fusion(bf16[1024,512]{1,0:T(8,128)(2,1)S(1)} %copy-done, s32[1024]{0:T(1024)} %param.10), kind=kOutput, calls=%fused_computation.34 | convolution fusion | flops 16809968 | bytes 1085504 | tf_op jit(solution)/shard_map/dot_general | solution.py:320
  6.8 1.4 %collective-permute-start.2 = (bf16[160,256]{1,0:T(8,128)(2,1)S(1)}, bf16[160,256]{1,0:T(8,128)(2,1)S(1)}, u32[]{:S(2)}, u32[]{:S(2)}) collective-permute-start(bf16[160,256]{1,0:T(8,128)(2,1)S(1)} %pad_maximum_fusion.3), channel_id=1, source_target_pairs={{0,6},{1,7},{2,4},{3,5},{4,2},{5,3},{6,0},{7,1},{8,14},{9,15},{10,... | collective-permute-start | bytes 245768 | tf_op jit(solution)/shard_map/ppermute | solution.py:20
  8.2 0.3 collective-permute-start
  8.5 0.7 %iota_compare_fusion.3 = pred[16,64]{1,0:T(8,128)(4,1)S(1)} fusion(s32[16]{0:T(128)} %param.12), kind=kLoop, calls=%fused_computation.41 | loop fusion | flops 1024 | bytes 1088 | tf_op jit(solution)/shard_map/lt | solution.py:330
  9.2 0.7 %fusion.4 = (s32[16,64]{1,0:T(8,128)S(1)}, s32[16,64]{1,0:T(8,128)S(1)}) fusion(s32[16,64]{1,0:T(8,128)} %param.11, s32[]{:T(128)S(6)} %mul.42, s32[16,64]{1,0:T(8,128)} %param.13), kind=kLoop, calls=%fused_computation.40 | loop fusion | flops 13312 | bytes 16388 | tf_op jit(solution)/shard_map/sub | solution.py:329
  10.0 0.6 select_reduce_fusion
  10.6 0.9 %constant_dynamic-slice_fusion = bf16[128,256]{1,0:T(8,128)(2,1)S(1)} fusion(bf16[128,1024]{1,0:T(8,128)(2,1)} %param.16, s32[]{:T(128)S(6)} %select_n.32), kind=kLoop, calls=%fused_computation.43 | loop fusion | bytes 131076 | tf_op jit(solution)/shard_map/dynamic_slice | solution.py:311
  11.4 0.8 %constant_dynamic-slice_fusion.8 = (bf16[64,256]{1,0:T(8,128)(2,1)S(1)}, bf16[64,256]{1,0:T(8,128)(2,1)S(1)}, bf16[64,256]{1,0:T(8,128)(2,1)S(1)}, bf16[64,256]{1,0:T(8,128)(2,1)S(1)}) fusion(bf16[64,1024]{1,0:T(8,128)(2,1)} %param.14, s32[]{:T(128)S(6)} %select_n.32, s32[]{:T(128)S(6)} %select_n.35, s32[]{:T(128)S(6)} %select_n.34, s32[]{:T(128)S(6)} %select_n.33), kind=kLoop, calls=%fused_computation.51 | loop fusion | bytes 262160 | tf_op jit(solution)/shard_map/dynamic_slice | solution.py:311
  12.2 0.8 %constant_dynamic-slice_fusion.7 = (bf16[64,256]{1,0:T(8,128)(2,1)S(1)}, bf16[64,256]{1,0:T(8,128)(2,1)S(1)}, bf16[64,256]{1,0:T(8,128)(2,1)S(1)}, bf16[64,256]{1,0:T(8,128)(2,1)S(1)}) fusion(bf16[64,1024]{1,0:T(8,128)(2,1)} %param.15, s32[]{:T(128)S(6)} %select_n.32, s32[]{:T(128)S(6)} %select_n.35, s32[]{:T(128)S(6)} %select_n.34, s32[]{:T(128)S(6)} %select_n.33), kind=kLoop, calls=%fused_computation.50 | loop fusion | bytes 262160 | tf_op jit(solution)/shard_map/dynamic_slice | solution.py:311
  13.1 0.7 %collective-permute-done = bf16[160,256]{1,0:T(8,128)(2,1)S(1)} collective-permute-done((bf16[160,256]{1,0:T(8,128)(2,1)S(1)}, bf16[160,256]{1,0:T(8,128)(2,1)S(1)}, u32[]{:S(2)}, u32[]{:S(2)}) %collective-permute-start) | collective-permute-done | bytes 81952 | tf_op jit(solution)/shard_map/ppermute | solution.py:20
  14.1 1.6 %collective-permute-start.8 = (bf16[496,256]{1,0:T(8,128)(2,1)S(1)}, bf16[496,256]{1,0:T(8,128)(2,1)S(1)}, u32[]{:S(2)}, u32[]{:S(2)}) collective-permute-start(bf16[496,256]{1,0:T(8,128)(2,1)S(1)} %constant_dynamic-update-slice_fusion.refs_2_), channel_id=1, source_target_pairs={{0,16},{8,24},{16,0},{24,8},{1,17},{9,25},{17,1},{25,9},{2,18},{10... | collective-permute-start | bytes 761864 | tf_op jit(solution)/shard_map/ppermute | solution.py:34
  15.7 1.5 %collective-permute-start.7 = (bf16[496,256]{1,0:T(8,128)(2,1)S(1)}, bf16[496,256]{1,0:T(8,128)(2,1)S(1)}, u32[]{:S(2)}, u32[]{:S(2)}) collective-permute-start(bf16[496,256]{1,0:T(8,128)(2,1)S(1)} %constant_dynamic-update-slice_fusion.refs_2_), channel_id=1, source_target_pairs={{0,8},{8,0},{16,24},{24,16},{1,9},{9,1},{17,25},{25,17},{2,10},{10... | collective-permute-start | bytes 761864 | tf_op jit(solution)/shard_map/ppermute | solution.py:34
  17.2 1.0 %collective-permute-start.6 = (bf16[192,256]{1,0:T(8,128)(2,1)S(1)}, bf16[192,256]{1,0:T(8,128)(2,1)S(1)}, u32[]{:S(2)}, u32[]{:S(2)}) collective-permute-start(bf16[192,256]{1,0:T(8,128)(2,1)S(1)} %pad_maximum_fusion.2), channel_id=1, source_target_pairs={{0,2},{1,3},{2,0},{3,1},{4,6},{5,7},{6,4},{7,5},{8,10},{9,11},{10,... | collective-permute-start | bytes 294920 | tf_op jit(solution)/shard_map/ppermute | solution.py:20
  18.2 2.1 %collective-permute-start.5 = (bf16[192,256]{1,0:T(8,128)(2,1)S(1)}, bf16[192,256]{1,0:T(8,128)(2,1)S(1)}, u32[]{:S(2)}, u32[]{:S(2)}) collective-permute-start(bf16[192,256]{1,0:T(8,128)(2,1)S(1)} %pad_maximum_fusion.2), channel_id=1, source_target_pairs={{0,4},{1,5},{2,6},{3,7},{4,0},{5,1},{6,2},{7,3},{8,12},{9,13},{10,... | collective-permute-start | bytes 294920 | tf_op jit(solution)/shard_map/ppermute | solution.py:20
  20.3 1.3 %collective-permute-start.4 = (bf16[192,256]{1,0:T(8,128)(2,1)S(1)}, bf16[192,256]{1,0:T(8,128)(2,1)S(1)}, u32[]{:S(2)}, u32[]{:S(2)}) collective-permute-start(bf16[192,256]{1,0:T(8,128)(2,1)S(1)} %pad_maximum_fusion.2), channel_id=1, source_target_pairs={{0,6},{1,7},{2,4},{3,5},{4,2},{5,3},{6,0},{7,1},{8,14},{9,15},{10,... | collective-permute-start | bytes 294920 | tf_op jit(solution)/shard_map/ppermute | solution.py:20
  21.6 1.4 %collective-permute-done.6 = bf16[192,256]{1,0:T(8,128)(2,1)S(1)} collective-permute-done((bf16[192,256]{1,0:T(8,128)(2,1)S(1)}, bf16[192,256]{1,0:T(8,128)(2,1)S(1)}, u32[]{:S(2)}, u32[]{:S(2)}) %collective-permute-start.6) | collective-permute-done | bytes 98336 | tf_op jit(solution)/shard_map/ppermute | solution.py:20
  22.9 1.2 %collective-permute-start.9 = (bf16[304,256]{1,0:T(8,128)(2,1)S(1)}, bf16[304,256]{1,0:T(8,128)(2,1)}, u32[]{:S(2)}, u32[]{:S(2)}) collective-permute-start(bf16[304,256]{1,0:T(8,128)(2,1)S(1)} %get-tuple-element.77), channel_id=1, source_target_pairs={{0,24},{8,16},{16,8},{24,0},{1,25},{9,17},{17,9},{25,1},{2,26},{10... | collective-permute-start | bytes 466952 | tf_op jit(solution)/shard_map/ppermute | solution.py:34
  24.1 4.6 %collective-permute-done.5 = bf16[192,256]{1,0:T(8,128)(2,1)S(1)} collective-permute-done((bf16[192,256]{1,0:T(8,128)(2,1)S(1)}, bf16[192,256]{1,0:T(8,128)(2,1)S(1)}, u32[]{:S(2)}, u32[]{:S(2)}) %collective-permute-start.5) | collective-permute-done | bytes 98336 | tf_op jit(solution)/shard_map/ppermute | solution.py:20
  28.9 0.6 collective-permute-start.10
  29.5 0.1 collective-permute-start.13
  29.5 0.4 collective-permute-start.12
  30.1 0.8 %dynamic-slice_convert_fusion = f32[256]{0:T(256)S(1)} fusion(bf16[1024]{0:T(1024)(128)(2,1)} %param.17, s32[]{:T(128)S(6)} %select_n.32), kind=kLoop, calls=%fused_computation.54 | loop fusion | flops 256 | bytes 1540 | tf_op jit(solution)/shard_map/reshape | solution.py:350
  30.8 0.1 copy.14.refs_12_.refs_7_
  31.0 1.1 %collective-permute-done.14.refs_11_ = bf16[304,256]{1,0:T(8,128)(2,1)} collective-permute-done((bf16[304,256]{1,0:T(8,128)(2,1)}, bf16[304,256]{1,0:T(8,128)(2,1)}, u32[]{:S(2)}, u32[]{:S(2)}) %collective-permute-start.14) | collective-permute-done | bytes 155680 | tf_op jit(solution)/shard_map/ppermute | solution.py:29
  32.1 5.3 %scores.1 = (bf16[5120,1024]{1,0:T(8,128)(2,1)S(1)}, bf16[256,5120]{1,0:T(8,128)(2,1)S(1)}, f32[64,128]{1,0:T(8,128)S(1)}, f32[4,16,128]{2,1,0:T(8,128)S(1)}) custom-call(bf16[4,128,256]{2,1,0:T(8,128)(2,1)S(1)} %pad_maximum_fusion.1.refs_0_, bf16[704,256]{1,0:T(8,128)(2,1)S(1)} %pad_maximum_fusion.refs_1_, ...), custom_call_target="tpu_custom_call" | custom-call | tf_op jit(solution)/shard_map/scores/pallas_call | solution.py:362
  37.4 1.0 %collective-permute-start.17 = (f32[64,128]{1,0:T(8,128)S(1)}, f32[64,128]{1,0:T(8,128)S(1)}, u32[]{:S(2)}, u32[]{:S(2)}) collective-permute-start(f32[64,128]{1,0:T(8,128)S(1)} %get-tuple-element.35.refs_0_), channel_id=1, source_target_pairs={{0,24},{8,16},{16,8},{24,0},{1,25},{9,17},{17,9},{25,1},{2,26},{10... | collective-permute-start | bytes 98312 | tf_op jit(solution)/shard_map/ppermute | solution.py:34
  38.4 1.0 %collective-permute-start.16 = (f32[64,128]{1,0:T(8,128)S(1)}, f32[64,128]{1,0:T(8,128)S(1)}, u32[]{:S(2)}, u32[]{:S(2)}) collective-permute-start(f32[64,128]{1,0:T(8,128)S(1)} %get-tuple-element.35.refs_0_), channel_id=1, source_target_pairs={{0,16},{8,24},{16,0},{24,8},{1,17},{9,25},{17,1},{25,9},{2,18},{10... | collective-permute-start | bytes 98312 | tf_op jit(solution)/shard_map/ppermute | solution.py:34
  39.4 1.5 %collective-permute-start.15 = (f32[64,128]{1,0:T(8,128)S(1)}, f32[64,128]{1,0:T(8,128)S(1)}, u32[]{:S(2)}, u32[]{:S(2)}) collective-permute-start(f32[64,128]{1,0:T(8,128)S(1)} %get-tuple-element.35.refs_0_), channel_id=1, source_target_pairs={{0,8},{8,0},{16,24},{24,16},{1,9},{9,1},{17,25},{25,17},{2,10},{10... | collective-permute-start | bytes 98312 | tf_op jit(solution)/shard_map/ppermute | solution.py:34
  40.9 1.5 %collective-permute-done.17.refs_3_ = f32[64,128]{1,0:T(8,128)S(1)} collective-permute-done((f32[64,128]{1,0:T(8,128)S(1)}, f32[64,128]{1,0:T(8,128)S(1)}, u32[]{:S(2)}, u32[]{:S(2)}) %collective-permute-start.17) | collective-permute-done | bytes 32800 | tf_op jit(solution)/shard_map/ppermute | solution.py:34
  42.5 0.1 collective-permute-done.16.refs_2_
  42.6 0.7 %collective-permute-done.15.refs_1_ = f32[64,128]{1,0:T(8,128)S(1)} collective-permute-done((f32[64,128]{1,0:T(8,128)S(1)}, f32[64,128]{1,0:T(8,128)S(1)}, u32[]{:S(2)}, u32[]{:S(2)}) %collective-permute-start.15) | collective-permute-done | bytes 32800 | tf_op jit(solution)/shard_map/ppermute | solution.py:34
  43.4 2.7 %gradient.1 = (bf16[256,5120]{1,0:T(8,128)(2,1)S(1)}, bf16[16,256]{1,0:T(8,128)(2,1)S(1)}, bf16[2,144,256]{2,1,0:T(8,128)(2,1)S(1)}, bf16[2,144,256]{2,1,0:T(8,128)(2,1)S(1)}) custom-call(f32[64,128]{1,0:T(8,128)S(1)} %get-tuple-element.35.refs_0_, f32[64,128]{1,0:T(8,128)S(1)} %collective-permute-done.15.refs_1_, ...), custom_call_target="tpu_custom_call" | custom-call | tf_op jit(solution)/shard_map/gradient/pallas_call | solution.py:420
  46.1 1.8 %gradient_rest.1 = (bf16[2,144,256]{2,1,0:T(8,128)(2,1)S(1)}, bf16[2,144,256]{2,1,0:T(8,128)(2,1)S(1)}) custom-call(bf16[5120,1024]{1,0:T(8,128)(2,1)S(1)} %get-tuple-element.37.refs_5_.refs_0_, bf16[256,5120]{1,0:T(8,128)(2,1)S(1)} %get-tuple-element.40.refs_1_, bf16[16,256]{1,0:T(8,128)(2,1)S(1)} %get-tuple-element.41.refs_2_), custom_call_target="tpu_custom_call" | custom-call | tf_op jit(solution)/shard_map/gradient_rest/pallas_call | solution.py:409
  47.9 0.6 collective-permute-start.19
  48.5 2.3 %collective-permute-start.20 = (bf16[144,256]{1,0:T(8,128)(2,1)S(1)}, bf16[144,256]{1,0:T(8,128)(2,1)S(1)}, u32[]{:S(2)}, u32[]{:S(2)}) collective-permute-start(bf16[144,256]{1,0:T(8,128)(2,1)S(1)} %get-tuple-element.49), channel_id=1, source_target_pairs={{0,6},{1,7},{2,4},{3,5},{4,2},{5,3},{6,0},{7,1},{8,14},{9,15},{10,... | collective-permute-start | bytes 221192 | tf_op jit(solution)/shard_map/ppermute | solution.py:20
  50.8 0.8 %collective-permute-start.21 = (bf16[144,256]{1,0:T(8,128)(2,1)S(1)}, bf16[144,256]{1,0:T(8,128)(2,1)S(1)}, u32[]{:S(2)}, u32[]{:S(2)}) collective-permute-start(bf16[144,256]{1,0:T(8,128)(2,1)S(1)} %get-tuple-element.50), channel_id=1, source_target_pairs={{0,4},{1,5},{2,6},{3,7},{4,0},{5,1},{6,2},{7,3},{8,12},{9,13},{10,... | collective-permute-start | bytes 221192 | tf_op jit(solution)/shard_map/ppermute | solution.py:20
  51.7 1.4 %collective-permute-start.22 = (bf16[144,256]{1,0:T(8,128)(2,1)S(1)}, bf16[144,256]{1,0:T(8,128)(2,1)S(1)}, u32[]{:S(2)}, u32[]{:S(2)}) collective-permute-start(bf16[144,256]{1,0:T(8,128)(2,1)S(1)} %get-tuple-element.51), channel_id=1, source_target_pairs={{0,2},{1,3},{2,0},{3,1},{4,6},{5,7},{6,4},{7,5},{8,10},{9,11},{10,... | collective-permute-start | bytes 221192 | tf_op jit(solution)/shard_map/ppermute | solution.py:20
  53.1 2.1 %collective-permute-done.20.refs_1_ = bf16[144,256]{1,0:T(8,128)(2,1)S(1)} collective-permute-done((bf16[144,256]{1,0:T(8,128)(2,1)S(1)}, bf16[144,256]{1,0:T(8,128)(2,1)S(1)}, u32[]{:S(2)}, u32[]{:S(2)}) %collective-permute-start.20) | collective-permute-done | bytes 73760 | tf_op jit(solution)/shard_map/ppermute | solution.py:20
  55.2 3.4 %collective-permute-done.21.refs_2_ = bf16[144,256]{1,0:T(8,128)(2,1)S(1)} collective-permute-done((bf16[144,256]{1,0:T(8,128)(2,1)S(1)}, bf16[144,256]{1,0:T(8,128)(2,1)S(1)}, u32[]{:S(2)}, u32[]{:S(2)}) %collective-permute-start.21) | collective-permute-done | bytes 73760 | tf_op jit(solution)/shard_map/ppermute | solution.py:20
  58.6 1.5 %collective-permute-start.25 = (bf16[144,256]{1,0:T(8,128)(2,1)S(1)}, bf16[144,256]{1,0:T(8,128)(2,1)S(1)}, u32[]{:S(2)}, u32[]{:S(2)}) collective-permute-start(bf16[144,256]{1,0:T(8,128)(2,1)S(1)} %z_sum.1.refs_0_), channel_id=1, source_target_pairs={{0,24},{8,16},{16,8},{24,0},{1,25},{9,17},{17,9},{25,1},{2,26},{10... | collective-permute-start | bytes 221192 | tf_op jit(solution)/shard_map/ppermute | solution.py:34
  60.1 1.5 %collective-permute-start.24 = (bf16[144,256]{1,0:T(8,128)(2,1)S(1)}, bf16[144,256]{1,0:T(8,128)(2,1)S(1)}, u32[]{:S(2)}, u32[]{:S(2)}) collective-permute-start(bf16[144,256]{1,0:T(8,128)(2,1)S(1)} %z_sum.1.refs_0_), channel_id=1, source_target_pairs={{0,16},{8,24},{16,0},{24,8},{1,17},{9,25},{17,1},{25,9},{2,18},{10... | collective-permute-start | bytes 221192 | tf_op jit(solution)/shard_map/ppermute | solution.py:34
  61.6 0.5 collective-permute-start.23
  62.2 2.6 %collective-permute-done.25.refs_3_ = bf16[144,256]{1,0:T(8,128)(2,1)S(1)} collective-permute-done((bf16[144,256]{1,0:T(8,128)(2,1)S(1)}, bf16[144,256]{1,0:T(8,128)(2,1)S(1)}, u32[]{:S(2)}, u32[]{:S(2)}) %collective-permute-start.25) | collective-permute-done | bytes 73760 | tf_op jit(solution)/shard_map/ppermute | solution.py:34
  64.8 0.2 collective-permute-done.24.refs_2_
  65.0 1.0 %collective-permute-done.23.refs_1_ = bf16[144,256]{1,0:T(8,128)(2,1)S(1)} collective-permute-done((bf16[144,256]{1,0:T(8,128)(2,1)S(1)}, bf16[144,256]{1,0:T(8,128)(2,1)S(1)}, u32[]{:S(2)}, u32[]{:S(2)}) %collective-permute-start.23) | collective-permute-done | bytes 73760 | tf_op jit(solution)/shard_map/ppermute | solution.py:34
  66.0 0.9 %finish.1 = (f32[128,1024]{1,0:T(8,128)}, f32[1,1024]{1,0:T(1,128)}, f32[1,1]{1,0:T(1,128)}) custom-call(bf16[144,256]{1,0:T(8,128)(2,1)S(1)} %z_sum.1.refs_0_, bf16[144,256]{1,0:T(8,128)(2,1)S(1)} %collective-permute-done.23.refs_1_, bf16[144,256]{1,0:T(8,128)(2,1)S(1)} %collective-permute-done.24.refs_2_, bf16[144,256]{1,0:T(8,128)(2,1)S(1)} %collective-permute-done.25.refs_3_), custom_call_target="tpu_custom_call" | custom-call | tf_op jit(solution)/shard_map/finish/pallas_call | solution.py:457
  (48 shorter events, 0.8 us)
Async XLA Ops:
  0.6 5.0 %copy-start = (bf16[1024,512]{1,0:T(8,128)(2,1)S(1)}, bf16[1024,512]{1,0:T(8,128)(2,1)}, u32[]{:S(2)}) copy-start(bf16[1024,512]{1,0:T(8,128)(2,1)} %param.9) | copy-start | bytes 3145732
  1.5 12.3 %collective-permute-start.1 = (bf16[128,256]{1,0:T(8,128)(2,1)S(1)}, bf16[128,256]{1,0:T(8,128)(2,1)S(1)}, u32[]{:S(2)}, u32[]{:S(2)}) collective-permute-start(bf16[128,256]{1,0:T(8,128)(2,1)S(1)} %pad_maximum_fusion.4), channel_id=1, source_target_pairs={{0,4},{1,5},{2,6},{3,7},{4,0},{5,1},{6,2},{7,3},{8,12},{9,13},{10,... | collective-permute-start | bytes 196616 | tf_op jit(solution)/shard_map/ppermute | solution.py:20
  6.8 7.1 %collective-permute-start.2 = (bf16[160,256]{1,0:T(8,128)(2,1)S(1)}, bf16[160,256]{1,0:T(8,128)(2,1)S(1)}, u32[]{:S(2)}, u32[]{:S(2)}) collective-permute-start(bf16[160,256]{1,0:T(8,128)(2,1)S(1)} %pad_maximum_fusion.3), channel_id=1, source_target_pairs={{0,6},{1,7},{2,4},{3,5},{4,2},{5,3},{6,0},{7,1},{8,14},{9,15},{10,... | collective-permute-start | bytes 245768 | tf_op jit(solution)/shard_map/ppermute | solution.py:20
  8.2 5.6 %collective-permute-start = (bf16[160,256]{1,0:T(8,128)(2,1)S(1)}, bf16[160,256]{1,0:T(8,128)(2,1)S(1)}, u32[]{:S(2)}, u32[]{:S(2)}) collective-permute-start(bf16[160,256]{1,0:T(8,128)(2,1)S(1)} %pad_maximum_fusion.3), channel_id=1, source_target_pairs={{0,2},{1,3},{2,0},{3,1},{4,6},{5,7},{6,4},{7,5},{8,10},{9,11},{10,... | collective-permute-start | bytes 245768 | tf_op jit(solution)/shard_map/ppermute | solution.py:20
  14.0 3.2 %collective-permute-start.3 = (bf16[496,256]{1,0:T(8,128)(2,1)S(1)}, bf16[496,256]{1,0:T(8,128)(2,1)S(1)}, u32[]{:S(2)}, u32[]{:S(2)}) collective-permute-start(bf16[496,256]{1,0:T(8,128)(2,1)S(1)} %constant_dynamic-update-slice_fusion.refs_2_), channel_id=1, source_target_pairs={{0,1},{1,0},{2,3},{3,2},{4,5},{5,4},{6,7},{7,6},{8,9},{9,8},{10,11... | collective-permute-start | bytes 761864 | tf_op jit(solution)/shard_map/ppermute | solution.py:29
  14.1 15.3 %collective-permute-start.8 = (bf16[496,256]{1,0:T(8,128)(2,1)S(1)}, bf16[496,256]{1,0:T(8,128)(2,1)S(1)}, u32[]{:S(2)}, u32[]{:S(2)}) collective-permute-start(bf16[496,256]{1,0:T(8,128)(2,1)S(1)} %constant_dynamic-update-slice_fusion.refs_2_), channel_id=1, source_target_pairs={{0,16},{8,24},{16,0},{24,8},{1,17},{9,25},{17,1},{25,9},{2,18},{10... | collective-permute-start | bytes 761864 | tf_op jit(solution)/shard_map/ppermute | solution.py:34
  15.7 13.8 %collective-permute-start.7 = (bf16[496,256]{1,0:T(8,128)(2,1)S(1)}, bf16[496,256]{1,0:T(8,128)(2,1)S(1)}, u32[]{:S(2)}, u32[]{:S(2)}) collective-permute-start(bf16[496,256]{1,0:T(8,128)(2,1)S(1)} %constant_dynamic-update-slice_fusion.refs_2_), channel_id=1, source_target_pairs={{0,8},{8,0},{16,24},{24,16},{1,9},{9,1},{17,25},{25,17},{2,10},{10... | collective-permute-start | bytes 761864 | tf_op jit(solution)/shard_map/ppermute | solution.py:34
  17.2 5.7 %collective-permute-start.6 = (bf16[192,256]{1,0:T(8,128)(2,1)S(1)}, bf16[192,256]{1,0:T(8,128)(2,1)S(1)}, u32[]{:S(2)}, u32[]{:S(2)}) collective-permute-start(bf16[192,256]{1,0:T(8,128)(2,1)S(1)} %pad_maximum_fusion.2), channel_id=1, source_target_pairs={{0,2},{1,3},{2,0},{3,1},{4,6},{5,7},{6,4},{7,5},{8,10},{9,11},{10,... | collective-permute-start | bytes 294920 | tf_op jit(solution)/shard_map/ppermute | solution.py:20
  18.2 10.5 %collective-permute-start.5 = (bf16[192,256]{1,0:T(8,128)(2,1)S(1)}, bf16[192,256]{1,0:T(8,128)(2,1)S(1)}, u32[]{:S(2)}, u32[]{:S(2)}) collective-permute-start(bf16[192,256]{1,0:T(8,128)(2,1)S(1)} %pad_maximum_fusion.2), channel_id=1, source_target_pairs={{0,4},{1,5},{2,6},{3,7},{4,0},{5,1},{6,2},{7,3},{8,12},{9,13},{10,... | collective-permute-start | bytes 294920 | tf_op jit(solution)/shard_map/ppermute | solution.py:20
  20.3 8.5 %collective-permute-start.4 = (bf16[192,256]{1,0:T(8,128)(2,1)S(1)}, bf16[192,256]{1,0:T(8,128)(2,1)S(1)}, u32[]{:S(2)}, u32[]{:S(2)}) collective-permute-start(bf16[192,256]{1,0:T(8,128)(2,1)S(1)} %pad_maximum_fusion.2), channel_id=1, source_target_pairs={{0,6},{1,7},{2,4},{3,5},{4,2},{5,3},{6,0},{7,1},{8,14},{9,15},{10,... | collective-permute-start | bytes 294920 | tf_op jit(solution)/shard_map/ppermute | solution.py:20
  22.9 7.0 %collective-permute-start.9 = (bf16[304,256]{1,0:T(8,128)(2,1)S(1)}, bf16[304,256]{1,0:T(8,128)(2,1)}, u32[]{:S(2)}, u32[]{:S(2)}) collective-permute-start(bf16[304,256]{1,0:T(8,128)(2,1)S(1)} %get-tuple-element.77), channel_id=1, source_target_pairs={{0,24},{8,16},{16,8},{24,0},{1,25},{9,17},{17,9},{25,1},{2,26},{10... | collective-permute-start | bytes 466952 | tf_op jit(solution)/shard_map/ppermute | solution.py:34
  28.8 3.3 %collective-permute-start.11 = (bf16[704,256]{1,0:T(8,128)(2,1)S(1)}, bf16[704,256]{1,0:T(8,128)(2,1)S(1)}, u32[]{:S(2)}, u32[]{:S(2)}) collective-permute-start(bf16[704,256]{1,0:T(8,128)(2,1)S(1)} %pad_maximum_fusion.refs_1_), channel_id=1, source_target_pairs={{0,1},{1,0},{2,3},{3,2},{4,5},{5,4},{6,7},{7,6},{8,9},{9,8},{10,11... | collective-permute-start | bytes 1081352 | tf_op jit(solution)/shard_map/ppermute | solution.py:29
  28.9 2.1 %collective-permute-start.10 = (bf16[4,128,256]{2,1,0:T(8,128)(2,1)S(1)}, bf16[4,128,256]{2,1,0:T(8,128)(2,1)S(1)}, u32[]{:S(2)}, u32[]{:S(2)}) collective-permute-start(bf16[4,128,256]{2,1,0:T(8,128)(2,1)S(1)} %pad_maximum_fusion.1.refs_0_), channel_id=1, source_target_pairs={{0,1},{1,0},{2,3},{3,2},{4,5},{5,4},{6,7},{7,6},{8,9},{9,8},{10,11... | collective-permute-start | bytes 786440 | tf_op jit(solution)/shard_map/ppermute | solution.py:29
  29.5 2.6 %collective-permute-start.13 = (bf16[496,256]{1,0:T(8,128)(2,1)S(1)}, bf16[496,256]{1,0:T(8,128)(2,1)}, u32[]{:S(2)}, u32[]{:S(2)}) collective-permute-start(bf16[496,256]{1,0:T(8,128)(2,1)S(1)} %collective-permute-done.8.refs_4_), channel_id=1, source_target_pairs={{0,1},{1,0},{2,3},{3,2},{4,5},{5,4},{6,7},{7,6},{8,9},{9,8},{10,11... | collective-permute-start | bytes 761864 | tf_op jit(solution)/shard_map/ppermute | solution.py:29
  29.5 2.5 %collective-permute-start.12 = (bf16[496,256]{1,0:T(8,128)(2,1)S(1)}, bf16[496,256]{1,0:T(8,128)(2,1)}, u32[]{:S(2)}, u32[]{:S(2)}) collective-permute-start(bf16[496,256]{1,0:T(8,128)(2,1)S(1)} %collective-permute-done.7.refs_3_), channel_id=1, source_target_pairs={{0,1},{1,0},{2,3},{3,2},{4,5},{5,4},{6,7},{7,6},{8,9},{9,8},{10,11... | collective-permute-start | bytes 761864 | tf_op jit(solution)/shard_map/ppermute | solution.py:29
  30.0 2.1 %collective-permute-start.14 = (bf16[304,256]{1,0:T(8,128)(2,1)}, bf16[304,256]{1,0:T(8,128)(2,1)}, u32[]{:S(2)}, u32[]{:S(2)}) collective-permute-start(bf16[304,256]{1,0:T(8,128)(2,1)} %collective-permute-done.9.refs_5_), channel_id=1, source_target_pairs={{0,1},{1,0},{2,3},{3,2},{4,5},{5,4},{6,7},{7,6},{8,9},{9,8},{10,11... | collective-permute-start | bytes 466952 | tf_op jit(solution)/shard_map/ppermute | solution.py:29
  37.4 5.1 %collective-permute-start.17 = (f32[64,128]{1,0:T(8,128)S(1)}, f32[64,128]{1,0:T(8,128)S(1)}, u32[]{:S(2)}, u32[]{:S(2)}) collective-permute-start(f32[64,128]{1,0:T(8,128)S(1)} %get-tuple-element.35.refs_0_), channel_id=1, source_target_pairs={{0,24},{8,16},{16,8},{24,0},{1,25},{9,17},{17,9},{25,1},{2,26},{10... | collective-permute-start | bytes 98312 | tf_op jit(solution)/shard_map/ppermute | solution.py:34
  38.4 4.2 %collective-permute-start.16 = (f32[64,128]{1,0:T(8,128)S(1)}, f32[64,128]{1,0:T(8,128)S(1)}, u32[]{:S(2)}, u32[]{:S(2)}) collective-permute-start(f32[64,128]{1,0:T(8,128)S(1)} %get-tuple-element.35.refs_0_), channel_id=1, source_target_pairs={{0,16},{8,24},{16,0},{24,8},{1,17},{9,25},{17,1},{25,9},{2,18},{10... | collective-permute-start | bytes 98312 | tf_op jit(solution)/shard_map/ppermute | solution.py:34
  39.4 3.9 %collective-permute-start.15 = (f32[64,128]{1,0:T(8,128)S(1)}, f32[64,128]{1,0:T(8,128)S(1)}, u32[]{:S(2)}, u32[]{:S(2)}) collective-permute-start(f32[64,128]{1,0:T(8,128)S(1)} %get-tuple-element.35.refs_0_), channel_id=1, source_target_pairs={{0,8},{8,0},{16,24},{24,16},{1,9},{9,1},{17,25},{25,17},{2,10},{10... | collective-permute-start | bytes 98312 | tf_op jit(solution)/shard_map/ppermute | solution.py:34
  46.0 1.9 %collective-permute-start.18 = (bf16[2,144,256]{2,1,0:T(8,128)(2,1)S(1)}, bf16[2,144,256]{2,1,0:T(8,128)(2,1)S(1)}, u32[]{:S(2)}, u32[]{:S(2)}) collective-permute-start(bf16[2,144,256]{2,1,0:T(8,128)(2,1)S(1)} %get-tuple-element.39), channel_id=1, source_target_pairs={{0,1},{1,0},{2,3},{3,2},{4,5},{5,4},{6,7},{7,6},{8,9},{9,8},{10,11... | collective-permute-start | bytes 442376 | tf_op jit(solution)/shard_map/ppermute | solution.py:29
  47.9 3.8 %collective-permute-start.19 = (bf16[2,144,256]{2,1,0:T(8,128)(2,1)S(1)}, bf16[2,144,256]{2,1,0:T(8,128)(2,1)S(1)}, u32[]{:S(2)}, u32[]{:S(2)}) collective-permute-start(bf16[2,144,256]{2,1,0:T(8,128)(2,1)S(1)} %get-tuple-element.45), channel_id=1, source_target_pairs={{0,1},{1,0},{2,3},{3,2},{4,5},{5,4},{6,7},{7,6},{8,9},{9,8},{10,11... | collective-permute-start | bytes 442376 | tf_op jit(solution)/shard_map/ppermute | solution.py:29
  48.5 6.6 %collective-permute-start.20 = (bf16[144,256]{1,0:T(8,128)(2,1)S(1)}, bf16[144,256]{1,0:T(8,128)(2,1)S(1)}, u32[]{:S(2)}, u32[]{:S(2)}) collective-permute-start(bf16[144,256]{1,0:T(8,128)(2,1)S(1)} %get-tuple-element.49), channel_id=1, source_target_pairs={{0,6},{1,7},{2,4},{3,5},{4,2},{5,3},{6,0},{7,1},{8,14},{9,15},{10,... | collective-permute-start | bytes 221192 | tf_op jit(solution)/shard_map/ppermute | solution.py:20
  50.8 7.7 %collective-permute-start.21 = (bf16[144,256]{1,0:T(8,128)(2,1)S(1)}, bf16[144,256]{1,0:T(8,128)(2,1)S(1)}, u32[]{:S(2)}, u32[]{:S(2)}) collective-permute-start(bf16[144,256]{1,0:T(8,128)(2,1)S(1)} %get-tuple-element.50), channel_id=1, source_target_pairs={{0,4},{1,5},{2,6},{3,7},{4,0},{5,1},{6,2},{7,3},{8,12},{9,13},{10,... | collective-permute-start | bytes 221192 | tf_op jit(solution)/shard_map/ppermute | solution.py:20
  51.7 6.9 %collective-permute-start.22 = (bf16[144,256]{1,0:T(8,128)(2,1)S(1)}, bf16[144,256]{1,0:T(8,128)(2,1)S(1)}, u32[]{:S(2)}, u32[]{:S(2)}) collective-permute-start(bf16[144,256]{1,0:T(8,128)(2,1)S(1)} %get-tuple-element.51), channel_id=1, source_target_pairs={{0,2},{1,3},{2,0},{3,1},{4,6},{5,7},{6,4},{7,5},{8,10},{9,11},{10,... | collective-permute-start | bytes 221192 | tf_op jit(solution)/shard_map/ppermute | solution.py:20
  58.6 6.1 %collective-permute-start.25 = (bf16[144,256]{1,0:T(8,128)(2,1)S(1)}, bf16[144,256]{1,0:T(8,128)(2,1)S(1)}, u32[]{:S(2)}, u32[]{:S(2)}) collective-permute-start(bf16[144,256]{1,0:T(8,128)(2,1)S(1)} %z_sum.1.refs_0_), channel_id=1, source_target_pairs={{0,24},{8,16},{16,8},{24,0},{1,25},{9,17},{17,9},{25,1},{2,26},{10... | collective-permute-start | bytes 221192 | tf_op jit(solution)/shard_map/ppermute | solution.py:34
  60.1 4.9 %collective-permute-start.24 = (bf16[144,256]{1,0:T(8,128)(2,1)S(1)}, bf16[144,256]{1,0:T(8,128)(2,1)S(1)}, u32[]{:S(2)}, u32[]{:S(2)}) collective-permute-start(bf16[144,256]{1,0:T(8,128)(2,1)S(1)} %z_sum.1.refs_0_), channel_id=1, source_target_pairs={{0,16},{8,24},{16,0},{24,8},{1,17},{9,25},{17,1},{25,9},{2,18},{10... | collective-permute-start | bytes 221192 | tf_op jit(solution)/shard_map/ppermute | solution.py:34
  61.6 4.4 %collective-permute-start.23 = (bf16[144,256]{1,0:T(8,128)(2,1)S(1)}, bf16[144,256]{1,0:T(8,128)(2,1)S(1)}, u32[]{:S(2)}, u32[]{:S(2)}) collective-permute-start(bf16[144,256]{1,0:T(8,128)(2,1)S(1)} %z_sum.1.refs_0_), channel_id=1, source_target_pairs={{0,8},{8,0},{16,24},{24,16},{1,9},{9,1},{17,25},{25,17},{2,10},{10... | collective-permute-start | bytes 221192 | tf_op jit(solution)/shard_map/ppermute | solution.py:34

commit v7 on v5

--- a/solution.py
+++ b/solution.py
@@ -207,31 +207,33 @@
     gained = gout[...]
     trips, numer = sums[0], sums[1]
     group = 8
-    for n in range(act.shape[1] // (blk * window)):
-        score = scores[0][n * blk : (n + 1) * blk, :]
-        for k in range(1, n_region):
-            at = (n ^ k) * blk if scores[k].shape[0] > blk else 0
-            score = score + scores[k][at : at + blk, :]
-        table = win[step + n]
-        valid = table > 0
-        flow = jnp.where(valid, table - 1.0, 0.0)
-        top = jnp.max(jnp.where(valid, score, -jnp.inf), axis=1, keepdims=True)
-        expo = jnp.where(valid, jnp.exp(score - top), 0.0)
-        mass = jnp.sum(expo, axis=1, keepdims=True)
-        probs = expo / mass
-        logp = score - top - jnp.log(mass)
-        anchor_total = jnp.sum(flow, axis=1, keepdims=True)
-        sgrad = jnp.where(valid, probs * anchor_total - flow, 0.0)
-        trips = trips + flow
-        numer = numer - jnp.where(valid, flow * logp, 0.0)
-        for c in range(0, blk, group):
-            wide = jnp.concatenate([sgrad[c + a : c + a + 1, :window] for a in range(group)], axis=1)
-            for q in range(0, group * window, 128):
-                line = wide[:, q : q + 128]
-                at = slice((n * blk + c) * window + q, (n * blk + c) * window + q + 128)
-                active = act[:, at].astype(F32)
-                gained = gained + active * line
-                pre_out[:, at] = jnp.where(active > 0, weight * line, 0.0).astype(BF)
+    regions = act.shape[1] // (blk * window)
+    score = scores[0][...]
+    for k in range(1, n_region):
+        order = [n ^ k if regions > 1 else 0 for n in range(regions)]
+        score = score + jnp.concatenate([scores[k][n * blk : (n + 1) * blk, :] for n in order], axis=0)
+    table = jnp.concatenate([win[step + n] for n in range(regions)], axis=0)
+    valid = table > 0
+    flow = jnp.where(valid, table - 1.0, 0.0)
+    top = jnp.max(jnp.where(valid, score, -jnp.inf), axis=1, keepdims=True)
+    expo = jnp.where(valid, jnp.exp(score - top), 0.0)
+    mass = jnp.sum(expo, axis=1, keepdims=True)
+    probs = expo / mass
+    logp = score - top - jnp.log(mass)
+    anchor_total = jnp.sum(flow, axis=1, keepdims=True)
+    sgrad = jnp.where(valid, probs * anchor_total - flow, 0.0)
+    lost = jnp.where(valid, flow * logp, 0.0)
+    for n in range(regions):
+        trips = trips + flow[n * blk : (n + 1) * blk, :]
+        numer = numer - lost[n * blk : (n + 1) * blk, :]
+    for c in range(0, regions * blk, group):
+        wide = jnp.concatenate([sgrad[c + a : c + a + 1, :window] for a in range(group)], axis=1)
+        for q in range(0, group * window, 128):
+            line = wide[:, q : q + 128]
+            at = slice(c * window + q, c * window + q + 128)
+            active = act[:, at].astype(F32)
+            gained = gained + active * line
+            pre_out[:, at] = jnp.where(active > 0, weight * line, 0.0).astype(BF)
     gout[...] = gained
     sums[0] = trips
     sums[1] = numer

time: 67.3 us -> 67.4 us (level)
  no operation moved by 1% of the time
where the time goes in v7:
time: 67.4 us; the launch traced here: 66.9 us
  starting transfers between devices  28 us (42%)
  waiting for transfers between devices  19.5 us (29%)
  Pallas kernels  10.8 us (16%)
  local copies, waits for them, and re-layouts  3.58 us (5%)
  other arithmetic  2.98 us (4%)
  matrix products  1.04 us (2%)
  between operations  0.93 us (1%)
    ppermute x9, starting transfers between devices, along_z(): lax.ppermute(array, 'shard', [(i, i ^ 2 * by) for i in range(devices)])  14.7 us
    ppermute x9, waiting for transfers between devices, along_z(): lax.ppermute(array, 'shard', [(i, i ^ 2 * by) for i in range(devices)])  12.2 us
    ppermute x9, starting transfers between devices, swap_region(): return lax.ppermute(array, 'region', [(i, i ^ by) for i in range(devices)])  11.4 us
    ppermute x9, waiting for transfers between devices, swap_region(): return lax.ppermute(array, 'region', [(i, i ^ by) for i in range(devices)])  6.25 us
    pallas_call x1, Pallas kernels, shards(): pl.pallas_call(functools.partial(score_kernel, n_region, n_z, blk), grid=...  5.34 us
    dynamic_slice x4, local copies, waits for them, and re-layouts, cut(): lax.dynamic_slice_in_dim(array, (region ^ i) * cols, cols, array.ndim - 1)  3.37 us
    pallas_call x1, Pallas kernels, shards(): pl.pallas_call(functools.partial(grad_kernel, n_region, early, window), g...  2.68 us
    ppermute x8, starting transfers between devices, swap_core(): return lax.ppermute(array, 'shard', [(i, i ^ 1) for i in range(devices)])  1.93 us
  transfers between devices with their start and end apart: 26, of which 12 were waited for; matrix products, arithmetic and copies ran while one was open for 10% of the time, Pallas kernels for 3%

profile of v7, /device:TPU:0, one launch (start us, length us, event | category | flops | bytes accessed | tf_op | source)
XLA Modules:
  0.0 66.9 jit_solution(15786591416563573390)
XLA Ops:
  0.7 0.9 %constant_dynamic-slice_fusion.9 = (bf16[64,256]{1,0:T(8,128)(2,1)S(1)}, bf16[64,256]{1,0:T(8,128)(2,1)S(1)}) fusion(bf16[64,1024]{1,0:T(8,128)(2,1)} %param.15, s32[]{:T(128)S(6)} %select_n.32, bf16[64,1024]{1,0:T(8,128)(2,1)} %param.14), kind=kLoop, calls=%fused_computation.52 | loop fusion | bytes 131076 | tf_op jit(solution)/shard_map/dynamic_slice | solution.py:313
  1.5 4.1 %collective-permute-start.1 = (bf16[128,256]{1,0:T(8,128)(2,1)S(1)}, bf16[128,256]{1,0:T(8,128)(2,1)S(1)}, u32[]{:S(2)}, u32[]{:S(2)}) collective-permute-start(bf16[128,256]{1,0:T(8,128)(2,1)S(1)} %pad_maximum_fusion.4), channel_id=1, source_target_pairs={{0,4},{1,5},{2,6},{3,7},{4,0},{5,1},{6,2},{7,3},{8,12},{9,13},{10,... | collective-permute-start | bytes 196616 | tf_op jit(solution)/shard_map/ppermute | solution.py:20
  5.6 1.0 %multiply_reduce_fusion = (f32[16]{0:T(128)S(1)}, f32[16,512]{1,0:T(8,128)S(1)}) fusion(bf16[1024,512]{1,0:T(8,128)(2,1)S(1)} %copy-done, s32[1024]{0:T(1024)} %param.10), kind=kOutput, calls=%fused_computation.34 | convolution fusion | flops 16809968 | bytes 1085504 | tf_op jit(solution)/shard_map/dot_general | solution.py:322
  6.8 1.4 %collective-permute-start.2 = (bf16[160,256]{1,0:T(8,128)(2,1)S(1)}, bf16[160,256]{1,0:T(8,128)(2,1)S(1)}, u32[]{:S(2)}, u32[]{:S(2)}) collective-permute-start(bf16[160,256]{1,0:T(8,128)(2,1)S(1)} %pad_maximum_fusion.3), channel_id=1, source_target_pairs={{0,6},{1,7},{2,4},{3,5},{4,2},{5,3},{6,0},{7,1},{8,14},{9,15},{10,... | collective-permute-start | bytes 245768 | tf_op jit(solution)/shard_map/ppermute | solution.py:20
  8.2 0.3 collective-permute-start
  8.5 0.7 %iota_compare_fusion.3 = pred[16,64]{1,0:T(8,128)(4,1)S(1)} fusion(s32[16]{0:T(128)} %param.12), kind=kLoop, calls=%fused_computation.41 | loop fusion | flops 1024 | bytes 1088 | tf_op jit(solution)/shard_map/lt | solution.py:332
  9.2 0.7 %fusion.4 = (s32[16,64]{1,0:T(8,128)S(1)}, s32[16,64]{1,0:T(8,128)S(1)}) fusion(s32[16,64]{1,0:T(8,128)} %param.11, s32[]{:T(128)S(6)} %mul.42, s32[16,64]{1,0:T(8,128)} %param.13), kind=kLoop, calls=%fused_computation.40 | loop fusion | flops 13312 | bytes 16388 | tf_op jit(solution)/shard_map/sub | solution.py:331
  10.0 0.6 select_reduce_fusion
  10.6 0.9 %constant_dynamic-slice_fusion = bf16[128,256]{1,0:T(8,128)(2,1)S(1)} fusion(bf16[128,1024]{1,0:T(8,128)(2,1)} %param.16, s32[]{:T(128)S(6)} %select_n.32), kind=kLoop, calls=%fused_computation.43 | loop fusion | bytes 131076 | tf_op jit(solution)/shard_map/dynamic_slice | solution.py:313
  11.4 0.8 %constant_dynamic-slice_fusion.8 = (bf16[64,256]{1,0:T(8,128)(2,1)S(1)}, bf16[64,256]{1,0:T(8,128)(2,1)S(1)}, bf16[64,256]{1,0:T(8,128)(2,1)S(1)}, bf16[64,256]{1,0:T(8,128)(2,1)S(1)}) fusion(bf16[64,1024]{1,0:T(8,128)(2,1)} %param.14, s32[]{:T(128)S(6)} %select_n.32, s32[]{:T(128)S(6)} %select_n.35, s32[]{:T(128)S(6)} %select_n.34, s32[]{:T(128)S(6)} %select_n.33), kind=kLoop, calls=%fused_computation.51 | loop fusion | bytes 262160 | tf_op jit(solution)/shard_map/dynamic_slice | solution.py:313
  12.2 0.8 %constant_dynamic-slice_fusion.7 = (bf16[64,256]{1,0:T(8,128)(2,1)S(1)}, bf16[64,256]{1,0:T(8,128)(2,1)S(1)}, bf16[64,256]{1,0:T(8,128)(2,1)S(1)}, bf16[64,256]{1,0:T(8,128)(2,1)S(1)}) fusion(bf16[64,1024]{1,0:T(8,128)(2,1)} %param.15, s32[]{:T(128)S(6)} %select_n.32, s32[]{:T(128)S(6)} %select_n.35, s32[]{:T(128)S(6)} %select_n.34, s32[]{:T(128)S(6)} %select_n.33), kind=kLoop, calls=%fused_computation.50 | loop fusion | bytes 262160 | tf_op jit(solution)/shard_map/dynamic_slice | solution.py:313
  13.1 0.7 %collective-permute-done = bf16[160,256]{1,0:T(8,128)(2,1)S(1)} collective-permute-done((bf16[160,256]{1,0:T(8,128)(2,1)S(1)}, bf16[160,256]{1,0:T(8,128)(2,1)S(1)}, u32[]{:S(2)}, u32[]{:S(2)}) %collective-permute-start) | collective-permute-done | bytes 81952 | tf_op jit(solution)/shard_map/ppermute | solution.py:20
  14.1 1.6 %collective-permute-start.8 = (bf16[496,256]{1,0:T(8,128)(2,1)S(1)}, bf16[496,256]{1,0:T(8,128)(2,1)S(1)}, u32[]{:S(2)}, u32[]{:S(2)}) collective-permute-start(bf16[496,256]{1,0:T(8,128)(2,1)S(1)} %constant_dynamic-update-slice_fusion.refs_2_), channel_id=1, source_target_pairs={{0,16},{8,24},{16,0},{24,8},{1,17},{9,25},{17,1},{25,9},{2,18},{10... | collective-permute-start | bytes 761864 | tf_op jit(solution)/shard_map/ppermute | solution.py:34
  15.7 1.5 %collective-permute-start.7 = (bf16[496,256]{1,0:T(8,128)(2,1)S(1)}, bf16[496,256]{1,0:T(8,128)(2,1)S(1)}, u32[]{:S(2)}, u32[]{:S(2)}) collective-permute-start(bf16[496,256]{1,0:T(8,128)(2,1)S(1)} %constant_dynamic-update-slice_fusion.refs_2_), channel_id=1, source_target_pairs={{0,8},{8,0},{16,24},{24,16},{1,9},{9,1},{17,25},{25,17},{2,10},{10... | collective-permute-start | bytes 761864 | tf_op jit(solution)/shard_map/ppermute | solution.py:34
  17.2 1.0 %collective-permute-start.6 = (bf16[192,256]{1,0:T(8,128)(2,1)S(1)}, bf16[192,256]{1,0:T(8,128)(2,1)S(1)}, u32[]{:S(2)}, u32[]{:S(2)}) collective-permute-start(bf16[192,256]{1,0:T(8,128)(2,1)S(1)} %pad_maximum_fusion.2), channel_id=1, source_target_pairs={{0,2},{1,3},{2,0},{3,1},{4,6},{5,7},{6,4},{7,5},{8,10},{9,11},{10,... | collective-permute-start | bytes 294920 | tf_op jit(solution)/shard_map/ppermute | solution.py:20
  18.2 2.1 %collective-permute-start.5 = (bf16[192,256]{1,0:T(8,128)(2,1)S(1)}, bf16[192,256]{1,0:T(8,128)(2,1)S(1)}, u32[]{:S(2)}, u32[]{:S(2)}) collective-permute-start(bf16[192,256]{1,0:T(8,128)(2,1)S(1)} %pad_maximum_fusion.2), channel_id=1, source_target_pairs={{0,4},{1,5},{2,6},{3,7},{4,0},{5,1},{6,2},{7,3},{8,12},{9,13},{10,... | collective-permute-start | bytes 294920 | tf_op jit(solution)/shard_map/ppermute | solution.py:20
  20.3 1.3 %collective-permute-start.4 = (bf16[192,256]{1,0:T(8,128)(2,1)S(1)}, bf16[192,256]{1,0:T(8,128)(2,1)S(1)}, u32[]{:S(2)}, u32[]{:S(2)}) collective-permute-start(bf16[192,256]{1,0:T(8,128)(2,1)S(1)} %pad_maximum_fusion.2), channel_id=1, source_target_pairs={{0,6},{1,7},{2,4},{3,5},{4,2},{5,3},{6,0},{7,1},{8,14},{9,15},{10,... | collective-permute-start | bytes 294920 | tf_op jit(solution)/shard_map/ppermute | solution.py:20
  21.6 1.4 %collective-permute-done.6 = bf16[192,256]{1,0:T(8,128)(2,1)S(1)} collective-permute-done((bf16[192,256]{1,0:T(8,128)(2,1)S(1)}, bf16[192,256]{1,0:T(8,128)(2,1)S(1)}, u32[]{:S(2)}, u32[]{:S(2)}) %collective-permute-start.6) | collective-permute-done | bytes 98336 | tf_op jit(solution)/shard_map/ppermute | solution.py:20
  22.9 1.2 %collective-permute-start.9 = (bf16[304,256]{1,0:T(8,128)(2,1)S(1)}, bf16[304,256]{1,0:T(8,128)(2,1)}, u32[]{:S(2)}, u32[]{:S(2)}) collective-permute-start(bf16[304,256]{1,0:T(8,128)(2,1)S(1)} %get-tuple-element.77), channel_id=1, source_target_pairs={{0,24},{8,16},{16,8},{24,0},{1,25},{9,17},{17,9},{25,1},{2,26},{10... | collective-permute-start | bytes 466952 | tf_op jit(solution)/shard_map/ppermute | solution.py:34
  24.1 4.6 %collective-permute-done.5 = bf16[192,256]{1,0:T(8,128)(2,1)S(1)} collective-permute-done((bf16[192,256]{1,0:T(8,128)(2,1)S(1)}, bf16[192,256]{1,0:T(8,128)(2,1)S(1)}, u32[]{:S(2)}, u32[]{:S(2)}) %collective-permute-start.5) | collective-permute-done | bytes 98336 | tf_op jit(solution)/shard_map/ppermute | solution.py:20
  28.9 0.6 collective-permute-start.10
  29.5 0.1 collective-permute-start.13
  29.5 0.4 collective-permute-start.12
  30.1 0.8 %dynamic-slice_convert_fusion = f32[256]{0:T(256)S(1)} fusion(bf16[1024]{0:T(1024)(128)(2,1)} %param.17, s32[]{:T(128)S(6)} %select_n.32), kind=kLoop, calls=%fused_computation.54 | loop fusion | flops 256 | bytes 1540 | tf_op jit(solution)/shard_map/reshape | solution.py:352
  30.8 0.1 copy.14.refs_12_.refs_7_
  31.0 1.1 %collective-permute-done.14.refs_11_ = bf16[304,256]{1,0:T(8,128)(2,1)} collective-permute-done((bf16[304,256]{1,0:T(8,128)(2,1)}, bf16[304,256]{1,0:T(8,128)(2,1)}, u32[]{:S(2)}, u32[]{:S(2)}) %collective-permute-start.14) | collective-permute-done | bytes 155680 | tf_op jit(solution)/shard_map/ppermute | solution.py:29
  32.1 5.3 %scores.1 = (bf16[5120,1024]{1,0:T(8,128)(2,1)S(1)}, bf16[256,5120]{1,0:T(8,128)(2,1)S(1)}, f32[64,128]{1,0:T(8,128)S(1)}, f32[4,16,128]{2,1,0:T(8,128)S(1)}) custom-call(bf16[4,128,256]{2,1,0:T(8,128)(2,1)S(1)} %pad_maximum_fusion.1.refs_0_, bf16[704,256]{1,0:T(8,128)(2,1)S(1)} %pad_maximum_fusion.refs_1_, ...), custom_call_target="tpu_custom_call" | custom-call | tf_op jit(solution)/shard_map/scores/pallas_call | solution.py:364
  37.4 1.0 %collective-permute-start.17 = (f32[64,128]{1,0:T(8,128)S(1)}, f32[64,128]{1,0:T(8,128)S(1)}, u32[]{:S(2)}, u32[]{:S(2)}) collective-permute-start(f32[64,128]{1,0:T(8,128)S(1)} %get-tuple-element.35.refs_0_), channel_id=1, source_target_pairs={{0,24},{8,16},{16,8},{24,0},{1,25},{9,17},{17,9},{25,1},{2,26},{10... | collective-permute-start | bytes 98312 | tf_op jit(solution)/shard_map/ppermute | solution.py:34
  38.4 1.0 %collective-permute-start.16 = (f32[64,128]{1,0:T(8,128)S(1)}, f32[64,128]{1,0:T(8,128)S(1)}, u32[]{:S(2)}, u32[]{:S(2)}) collective-permute-start(f32[64,128]{1,0:T(8,128)S(1)} %get-tuple-element.35.refs_0_), channel_id=1, source_target_pairs={{0,16},{8,24},{16,0},{24,8},{1,17},{9,25},{17,1},{25,9},{2,18},{10... | collective-permute-start | bytes 98312 | tf_op jit(solution)/shard_map/ppermute | solution.py:34
  39.4 1.5 %collective-permute-start.15 = (f32[64,128]{1,0:T(8,128)S(1)}, f32[64,128]{1,0:T(8,128)S(1)}, u32[]{:S(2)}, u32[]{:S(2)}) collective-permute-start(f32[64,128]{1,0:T(8,128)S(1)} %get-tuple-element.35.refs_0_), channel_id=1, source_target_pairs={{0,8},{8,0},{16,24},{24,16},{1,9},{9,1},{17,25},{25,17},{2,10},{10... | collective-permute-start | bytes 98312 | tf_op jit(solution)/shard_map/ppermute | solution.py:34
  40.9 1.5 %collective-permute-done.17.refs_3_ = f32[64,128]{1,0:T(8,128)S(1)} collective-permute-done((f32[64,128]{1,0:T(8,128)S(1)}, f32[64,128]{1,0:T(8,128)S(1)}, u32[]{:S(2)}, u32[]{:S(2)}) %collective-permute-start.17) | collective-permute-done | bytes 32800 | tf_op jit(solution)/shard_map/ppermute | solution.py:34
  42.5 0.1 collective-permute-done.16.refs_2_
  42.6 0.7 %collective-permute-done.15.refs_1_ = f32[64,128]{1,0:T(8,128)S(1)} collective-permute-done((f32[64,128]{1,0:T(8,128)S(1)}, f32[64,128]{1,0:T(8,128)S(1)}, u32[]{:S(2)}, u32[]{:S(2)}) %collective-permute-start.15) | collective-permute-done | bytes 32800 | tf_op jit(solution)/shard_map/ppermute | solution.py:34
  43.4 2.7 %gradient.1 = (bf16[256,5120]{1,0:T(8,128)(2,1)S(1)}, bf16[16,256]{1,0:T(8,128)(2,1)S(1)}, bf16[2,144,256]{2,1,0:T(8,128)(2,1)S(1)}, bf16[2,144,256]{2,1,0:T(8,128)(2,1)S(1)}) custom-call(f32[64,128]{1,0:T(8,128)S(1)} %get-tuple-element.35.refs_0_, f32[64,128]{1,0:T(8,128)S(1)} %collective-permute-done.15.refs_1_, ...), custom_call_target="tpu_custom_call" | custom-call | tf_op jit(solution)/shard_map/gradient/pallas_call | solution.py:422
  46.1 1.8 %gradient_rest.1 = (bf16[2,144,256]{2,1,0:T(8,128)(2,1)S(1)}, bf16[2,144,256]{2,1,0:T(8,128)(2,1)S(1)}) custom-call(bf16[5120,1024]{1,0:T(8,128)(2,1)S(1)} %get-tuple-element.37.refs_5_.refs_0_, bf16[256,5120]{1,0:T(8,128)(2,1)S(1)} %get-tuple-element.40.refs_1_, bf16[16,256]{1,0:T(8,128)(2,1)S(1)} %get-tuple-element.41.refs_2_), custom_call_target="tpu_custom_call" | custom-call | tf_op jit(solution)/shard_map/gradient_rest/pallas_call | solution.py:411
  47.9 0.6 collective-permute-start.19
  48.5 2.3 %collective-permute-start.20 = (bf16[144,256]{1,0:T(8,128)(2,1)S(1)}, bf16[144,256]{1,0:T(8,128)(2,1)S(1)}, u32[]{:S(2)}, u32[]{:S(2)}) collective-permute-start(bf16[144,256]{1,0:T(8,128)(2,1)S(1)} %get-tuple-element.49), channel_id=1, source_target_pairs={{0,6},{1,7},{2,4},{3,5},{4,2},{5,3},{6,0},{7,1},{8,14},{9,15},{10,... | collective-permute-start | bytes 221192 | tf_op jit(solution)/shard_map/ppermute | solution.py:20
  50.8 0.8 %collective-permute-start.21 = (bf16[144,256]{1,0:T(8,128)(2,1)S(1)}, bf16[144,256]{1,0:T(8,128)(2,1)S(1)}, u32[]{:S(2)}, u32[]{:S(2)}) collective-permute-start(bf16[144,256]{1,0:T(8,128)(2,1)S(1)} %get-tuple-element.50), channel_id=1, source_target_pairs={{0,4},{1,5},{2,6},{3,7},{4,0},{5,1},{6,2},{7,3},{8,12},{9,13},{10,... | collective-permute-start | bytes 221192 | tf_op jit(solution)/shard_map/ppermute | solution.py:20
  51.7 1.4 %collective-permute-start.22 = (bf16[144,256]{1,0:T(8,128)(2,1)S(1)}, bf16[144,256]{1,0:T(8,128)(2,1)S(1)}, u32[]{:S(2)}, u32[]{:S(2)}) collective-permute-start(bf16[144,256]{1,0:T(8,128)(2,1)S(1)} %get-tuple-element.51), channel_id=1, source_target_pairs={{0,2},{1,3},{2,0},{3,1},{4,6},{5,7},{6,4},{7,5},{8,10},{9,11},{10,... | collective-permute-start | bytes 221192 | tf_op jit(solution)/shard_map/ppermute | solution.py:20
  53.1 2.1 %collective-permute-done.20.refs_1_ = bf16[144,256]{1,0:T(8,128)(2,1)S(1)} collective-permute-done((bf16[144,256]{1,0:T(8,128)(2,1)S(1)}, bf16[144,256]{1,0:T(8,128)(2,1)S(1)}, u32[]{:S(2)}, u32[]{:S(2)}) %collective-permute-start.20) | collective-permute-done | bytes 73760 | tf_op jit(solution)/shard_map/ppermute | solution.py:20
  55.2 3.4 %collective-permute-done.21.refs_2_ = bf16[144,256]{1,0:T(8,128)(2,1)S(1)} collective-permute-done((bf16[144,256]{1,0:T(8,128)(2,1)S(1)}, bf16[144,256]{1,0:T(8,128)(2,1)S(1)}, u32[]{:S(2)}, u32[]{:S(2)}) %collective-permute-start.21) | collective-permute-done | bytes 73760 | tf_op jit(solution)/shard_map/ppermute | solution.py:20
  58.6 1.5 %collective-permute-start.25 = (bf16[144,256]{1,0:T(8,128)(2,1)S(1)}, bf16[144,256]{1,0:T(8,128)(2,1)S(1)}, u32[]{:S(2)}, u32[]{:S(2)}) collective-permute-start(bf16[144,256]{1,0:T(8,128)(2,1)S(1)} %z_sum.1.refs_0_), channel_id=1, source_target_pairs={{0,24},{8,16},{16,8},{24,0},{1,25},{9,17},{17,9},{25,1},{2,26},{10... | collective-permute-start | bytes 221192 | tf_op jit(solution)/shard_map/ppermute | solution.py:34
  60.1 1.5 %collective-permute-start.24 = (bf16[144,256]{1,0:T(8,128)(2,1)S(1)}, bf16[144,256]{1,0:T(8,128)(2,1)S(1)}, u32[]{:S(2)}, u32[]{:S(2)}) collective-permute-start(bf16[144,256]{1,0:T(8,128)(2,1)S(1)} %z_sum.1.refs_0_), channel_id=1, source_target_pairs={{0,16},{8,24},{16,0},{24,8},{1,17},{9,25},{17,1},{25,9},{2,18},{10... | collective-permute-start | bytes 221192 | tf_op jit(solution)/shard_map/ppermute | solution.py:34
  61.7 0.5 collective-permute-start.23
  62.2 2.6 %collective-permute-done.25.refs_3_ = bf16[144,256]{1,0:T(8,128)(2,1)S(1)} collective-permute-done((bf16[144,256]{1,0:T(8,128)(2,1)S(1)}, bf16[144,256]{1,0:T(8,128)(2,1)S(1)}, u32[]{:S(2)}, u32[]{:S(2)}) %collective-permute-start.25) | collective-permute-done | bytes 73760 | tf_op jit(solution)/shard_map/ppermute | solution.py:34
  64.8 0.2 collective-permute-done.24.refs_2_
  65.0 1.0 %collective-permute-done.23.refs_1_ = bf16[144,256]{1,0:T(8,128)(2,1)S(1)} collective-permute-done((bf16[144,256]{1,0:T(8,128)(2,1)S(1)}, bf16[144,256]{1,0:T(8,128)(2,1)S(1)}, u32[]{:S(2)}, u32[]{:S(2)}) %collective-permute-start.23) | collective-permute-done | bytes 73760 | tf_op jit(solution)/shard_map/ppermute | solution.py:34
  66.0 0.9 %finish.1 = (f32[128,1024]{1,0:T(8,128)}, f32[1,1024]{1,0:T(1,128)}, f32[1,1]{1,0:T(1,128)}) custom-call(bf16[144,256]{1,0:T(8,128)(2,1)S(1)} %z_sum.1.refs_0_, bf16[144,256]{1,0:T(8,128)(2,1)S(1)} %collective-permute-done.23.refs_1_, bf16[144,256]{1,0:T(8,128)(2,1)S(1)} %collective-permute-done.24.refs_2_, bf16[144,256]{1,0:T(8,128)(2,1)S(1)} %collective-permute-done.25.refs_3_), custom_call_target="tpu_custom_call" | custom-call | tf_op jit(solution)/shard_map/finish/pallas_call | solution.py:459
  (48 shorter events, 0.8 us)
Async XLA Ops:
  0.6 5.0 %copy-start = (bf16[1024,512]{1,0:T(8,128)(2,1)S(1)}, bf16[1024,512]{1,0:T(8,128)(2,1)}, u32[]{:S(2)}) copy-start(bf16[1024,512]{1,0:T(8,128)(2,1)} %param.9) | copy-start | bytes 3145732
  1.5 12.3 %collective-permute-start.1 = (bf16[128,256]{1,0:T(8,128)(2,1)S(1)}, bf16[128,256]{1,0:T(8,128)(2,1)S(1)}, u32[]{:S(2)}, u32[]{:S(2)}) collective-permute-start(bf16[128,256]{1,0:T(8,128)(2,1)S(1)} %pad_maximum_fusion.4), channel_id=1, source_target_pairs={{0,4},{1,5},{2,6},{3,7},{4,0},{5,1},{6,2},{7,3},{8,12},{9,13},{10,... | collective-permute-start | bytes 196616 | tf_op jit(solution)/shard_map/ppermute | solution.py:20
  6.8 7.1 %collective-permute-start.2 = (bf16[160,256]{1,0:T(8,128)(2,1)S(1)}, bf16[160,256]{1,0:T(8,128)(2,1)S(1)}, u32[]{:S(2)}, u32[]{:S(2)}) collective-permute-start(bf16[160,256]{1,0:T(8,128)(2,1)S(1)} %pad_maximum_fusion.3), channel_id=1, source_target_pairs={{0,6},{1,7},{2,4},{3,5},{4,2},{5,3},{6,0},{7,1},{8,14},{9,15},{10,... | collective-permute-start | bytes 245768 | tf_op jit(solution)/shard_map/ppermute | solution.py:20
  8.2 5.6 %collective-permute-start = (bf16[160,256]{1,0:T(8,128)(2,1)S(1)}, bf16[160,256]{1,0:T(8,128)(2,1)S(1)}, u32[]{:S(2)}, u32[]{:S(2)}) collective-permute-start(bf16[160,256]{1,0:T(8,128)(2,1)S(1)} %pad_maximum_fusion.3), channel_id=1, source_target_pairs={{0,2},{1,3},{2,0},{3,1},{4,6},{5,7},{6,4},{7,5},{8,10},{9,11},{10,... | collective-permute-start | bytes 245768 | tf_op jit(solution)/shard_map/ppermute | solution.py:20
  14.0 3.2 %collective-permute-start.3 = (bf16[496,256]{1,0:T(8,128)(2,1)S(1)}, bf16[496,256]{1,0:T(8,128)(2,1)S(1)}, u32[]{:S(2)}, u32[]{:S(2)}) collective-permute-start(bf16[496,256]{1,0:T(8,128)(2,1)S(1)} %constant_dynamic-update-slice_fusion.refs_2_), channel_id=1, source_target_pairs={{0,1},{1,0},{2,3},{3,2},{4,5},{5,4},{6,7},{7,6},{8,9},{9,8},{10,11... | collective-permute-start | bytes 761864 | tf_op jit(solution)/shard_map/ppermute | solution.py:29
  14.1 15.3 %collective-permute-start.8 = (bf16[496,256]{1,0:T(8,128)(2,1)S(1)}, bf16[496,256]{1,0:T(8,128)(2,1)S(1)}, u32[]{:S(2)}, u32[]{:S(2)}) collective-permute-start(bf16[496,256]{1,0:T(8,128)(2,1)S(1)} %constant_dynamic-update-slice_fusion.refs_2_), channel_id=1, source_target_pairs={{0,16},{8,24},{16,0},{24,8},{1,17},{9,25},{17,1},{25,9},{2,18},{10... | collective-permute-start | bytes 761864 | tf_op jit(solution)/shard_map/ppermute | solution.py:34
  15.7 13.8 %collective-permute-start.7 = (bf16[496,256]{1,0:T(8,128)(2,1)S(1)}, bf16[496,256]{1,0:T(8,128)(2,1)S(1)}, u32[]{:S(2)}, u32[]{:S(2)}) collective-permute-start(bf16[496,256]{1,0:T(8,128)(2,1)S(1)} %constant_dynamic-update-slice_fusion.refs_2_), channel_id=1, source_target_pairs={{0,8},{8,0},{16,24},{24,16},{1,9},{9,1},{17,25},{25,17},{2,10},{10... | collective-permute-start | bytes 761864 | tf_op jit(solution)/shard_map/ppermute | solution.py:34
  17.2 5.7 %collective-permute-start.6 = (bf16[192,256]{1,0:T(8,128)(2,1)S(1)}, bf16[192,256]{1,0:T(8,128)(2,1)S(1)}, u32[]{:S(2)}, u32[]{:S(2)}) collective-permute-start(bf16[192,256]{1,0:T(8,128)(2,1)S(1)} %pad_maximum_fusion.2), channel_id=1, source_target_pairs={{0,2},{1,3},{2,0},{3,1},{4,6},{5,7},{6,4},{7,5},{8,10},{9,11},{10,... | collective-permute-start | bytes 294920 | tf_op jit(solution)/shard_map/ppermute | solution.py:20
  18.2 10.5 %collective-permute-start.5 = (bf16[192,256]{1,0:T(8,128)(2,1)S(1)}, bf16[192,256]{1,0:T(8,128)(2,1)S(1)}, u32[]{:S(2)}, u32[]{:S(2)}) collective-permute-start(bf16[192,256]{1,0:T(8,128)(2,1)S(1)} %pad_maximum_fusion.2), channel_id=1, source_target_pairs={{0,4},{1,5},{2,6},{3,7},{4,0},{5,1},{6,2},{7,3},{8,12},{9,13},{10,... | collective-permute-start | bytes 294920 | tf_op jit(solution)/shard_map/ppermute | solution.py:20
  20.3 8.5 %collective-permute-start.4 = (bf16[192,256]{1,0:T(8,128)(2,1)S(1)}, bf16[192,256]{1,0:T(8,128)(2,1)S(1)}, u32[]{:S(2)}, u32[]{:S(2)}) collective-permute-start(bf16[192,256]{1,0:T(8,128)(2,1)S(1)} %pad_maximum_fusion.2), channel_id=1, source_target_pairs={{0,6},{1,7},{2,4},{3,5},{4,2},{5,3},{6,0},{7,1},{8,14},{9,15},{10,... | collective-permute-start | bytes 294920 | tf_op jit(solution)/shard_map/ppermute | solution.py:20
  22.9 7.0 %collective-permute-start.9 = (bf16[304,256]{1,0:T(8,128)(2,1)S(1)}, bf16[304,256]{1,0:T(8,128)(2,1)}, u32[]{:S(2)}, u32[]{:S(2)}) collective-permute-start(bf16[304,256]{1,0:T(8,128)(2,1)S(1)} %get-tuple-element.77), channel_id=1, source_target_pairs={{0,24},{8,16},{16,8},{24,0},{1,25},{9,17},{17,9},{25,1},{2,26},{10... | collective-permute-start | bytes 466952 | tf_op jit(solution)/shard_map/ppermute | solution.py:34
  28.8 3.3 %collective-permute-start.11 = (bf16[704,256]{1,0:T(8,128)(2,1)S(1)}, bf16[704,256]{1,0:T(8,128)(2,1)S(1)}, u32[]{:S(2)}, u32[]{:S(2)}) collective-permute-start(bf16[704,256]{1,0:T(8,128)(2,1)S(1)} %pad_maximum_fusion.refs_1_), channel_id=1, source_target_pairs={{0,1},{1,0},{2,3},{3,2},{4,5},{5,4},{6,7},{7,6},{8,9},{9,8},{10,11... | collective-permute-start | bytes 1081352 | tf_op jit(solution)/shard_map/ppermute | solution.py:29
  28.9 2.1 %collective-permute-start.10 = (bf16[4,128,256]{2,1,0:T(8,128)(2,1)S(1)}, bf16[4,128,256]{2,1,0:T(8,128)(2,1)S(1)}, u32[]{:S(2)}, u32[]{:S(2)}) collective-permute-start(bf16[4,128,256]{2,1,0:T(8,128)(2,1)S(1)} %pad_maximum_fusion.1.refs_0_), channel_id=1, source_target_pairs={{0,1},{1,0},{2,3},{3,2},{4,5},{5,4},{6,7},{7,6},{8,9},{9,8},{10,11... | collective-permute-start | bytes 786440 | tf_op jit(solution)/shard_map/ppermute | solution.py:29
  29.5 2.6 %collective-permute-start.13 = (bf16[496,256]{1,0:T(8,128)(2,1)S(1)}, bf16[496,256]{1,0:T(8,128)(2,1)}, u32[]{:S(2)}, u32[]{:S(2)}) collective-permute-start(bf16[496,256]{1,0:T(8,128)(2,1)S(1)} %collective-permute-done.8.refs_4_), channel_id=1, source_target_pairs={{0,1},{1,0},{2,3},{3,2},{4,5},{5,4},{6,7},{7,6},{8,9},{9,8},{10,11... | collective-permute-start | bytes 761864 | tf_op jit(solution)/shard_map/ppermute | solution.py:29
  29.5 2.5 %collective-permute-start.12 = (bf16[496,256]{1,0:T(8,128)(2,1)S(1)}, bf16[496,256]{1,0:T(8,128)(2,1)}, u32[]{:S(2)}, u32[]{:S(2)}) collective-permute-start(bf16[496,256]{1,0:T(8,128)(2,1)S(1)} %collective-permute-done.7.refs_3_), channel_id=1, source_target_pairs={{0,1},{1,0},{2,3},{3,2},{4,5},{5,4},{6,7},{7,6},{8,9},{9,8},{10,11... | collective-permute-start | bytes 761864 | tf_op jit(solution)/shard_map/ppermute | solution.py:29
  30.0 2.1 %collective-permute-start.14 = (bf16[304,256]{1,0:T(8,128)(2,1)}, bf16[304,256]{1,0:T(8,128)(2,1)}, u32[]{:S(2)}, u32[]{:S(2)}) collective-permute-start(bf16[304,256]{1,0:T(8,128)(2,1)} %collective-permute-done.9.refs_5_), channel_id=1, source_target_pairs={{0,1},{1,0},{2,3},{3,2},{4,5},{5,4},{6,7},{7,6},{8,9},{9,8},{10,11... | collective-permute-start | bytes 466952 | tf_op jit(solution)/shard_map/ppermute | solution.py:29
  37.4 5.1 %collective-permute-start.17 = (f32[64,128]{1,0:T(8,128)S(1)}, f32[64,128]{1,0:T(8,128)S(1)}, u32[]{:S(2)}, u32[]{:S(2)}) collective-permute-start(f32[64,128]{1,0:T(8,128)S(1)} %get-tuple-element.35.refs_0_), channel_id=1, source_target_pairs={{0,24},{8,16},{16,8},{24,0},{1,25},{9,17},{17,9},{25,1},{2,26},{10... | collective-permute-start | bytes 98312 | tf_op jit(solution)/shard_map/ppermute | solution.py:34
  38.4 4.2 %collective-permute-start.16 = (f32[64,128]{1,0:T(8,128)S(1)}, f32[64,128]{1,0:T(8,128)S(1)}, u32[]{:S(2)}, u32[]{:S(2)}) collective-permute-start(f32[64,128]{1,0:T(8,128)S(1)} %get-tuple-element.35.refs_0_), channel_id=1, source_target_pairs={{0,16},{8,24},{16,0},{24,8},{1,17},{9,25},{17,1},{25,9},{2,18},{10... | collective-permute-start | bytes 98312 | tf_op jit(solution)/shard_map/ppermute | solution.py:34
  39.4 3.9 %collective-permute-start.15 = (f32[64,128]{1,0:T(8,128)S(1)}, f32[64,128]{1,0:T(8,128)S(1)}, u32[]{:S(2)}, u32[]{:S(2)}) collective-permute-start(f32[64,128]{1,0:T(8,128)S(1)} %get-tuple-element.35.refs_0_), channel_id=1, source_target_pairs={{0,8},{8,0},{16,24},{24,16},{1,9},{9,1},{17,25},{25,17},{2,10},{10... | collective-permute-start | bytes 98312 | tf_op jit(solution)/shard_map/ppermute | solution.py:34
  46.1 1.9 %collective-permute-start.18 = (bf16[2,144,256]{2,1,0:T(8,128)(2,1)S(1)}, bf16[2,144,256]{2,1,0:T(8,128)(2,1)S(1)}, u32[]{:S(2)}, u32[]{:S(2)}) collective-permute-start(bf16[2,144,256]{2,1,0:T(8,128)(2,1)S(1)} %get-tuple-element.39), channel_id=1, source_target_pairs={{0,1},{1,0},{2,3},{3,2},{4,5},{5,4},{6,7},{7,6},{8,9},{9,8},{10,11... | collective-permute-start | bytes 442376 | tf_op jit(solution)/shard_map/ppermute | solution.py:29
  47.9 3.8 %collective-permute-start.19 = (bf16[2,144,256]{2,1,0:T(8,128)(2,1)S(1)}, bf16[2,144,256]{2,1,0:T(8,128)(2,1)S(1)}, u32[]{:S(2)}, u32[]{:S(2)}) collective-permute-start(bf16[2,144,256]{2,1,0:T(8,128)(2,1)S(1)} %get-tuple-element.45), channel_id=1, source_target_pairs={{0,1},{1,0},{2,3},{3,2},{4,5},{5,4},{6,7},{7,6},{8,9},{9,8},{10,11... | collective-permute-start | bytes 442376 | tf_op jit(solution)/shard_map/ppermute | solution.py:29
  48.5 6.6 %collective-permute-start.20 = (bf16[144,256]{1,0:T(8,128)(2,1)S(1)}, bf16[144,256]{1,0:T(8,128)(2,1)S(1)}, u32[]{:S(2)}, u32[]{:S(2)}) collective-permute-start(bf16[144,256]{1,0:T(8,128)(2,1)S(1)} %get-tuple-element.49), channel_id=1, source_target_pairs={{0,6},{1,7},{2,4},{3,5},{4,2},{5,3},{6,0},{7,1},{8,14},{9,15},{10,... | collective-permute-start | bytes 221192 | tf_op jit(solution)/shard_map/ppermute | solution.py:20
  50.8 7.7 %collective-permute-start.21 = (bf16[144,256]{1,0:T(8,128)(2,1)S(1)}, bf16[144,256]{1,0:T(8,128)(2,1)S(1)}, u32[]{:S(2)}, u32[]{:S(2)}) collective-permute-start(bf16[144,256]{1,0:T(8,128)(2,1)S(1)} %get-tuple-element.50), channel_id=1, source_target_pairs={{0,4},{1,5},{2,6},{3,7},{4,0},{5,1},{6,2},{7,3},{8,12},{9,13},{10,... | collective-permute-start | bytes 221192 | tf_op jit(solution)/shard_map/ppermute | solution.py:20
  51.7 6.9 %collective-permute-start.22 = (bf16[144,256]{1,0:T(8,128)(2,1)S(1)}, bf16[144,256]{1,0:T(8,128)(2,1)S(1)}, u32[]{:S(2)}, u32[]{:S(2)}) collective-permute-start(bf16[144,256]{1,0:T(8,128)(2,1)S(1)} %get-tuple-element.51), channel_id=1, source_target_pairs={{0,2},{1,3},{2,0},{3,1},{4,6},{5,7},{6,4},{7,5},{8,10},{9,11},{10,... | collective-permute-start | bytes 221192 | tf_op jit(solution)/shard_map/ppermute | solution.py:20
  58.6 6.1 %collective-permute-start.25 = (bf16[144,256]{1,0:T(8,128)(2,1)S(1)}, bf16[144,256]{1,0:T(8,128)(2,1)S(1)}, u32[]{:S(2)}, u32[]{:S(2)}) collective-permute-start(bf16[144,256]{1,0:T(8,128)(2,1)S(1)} %z_sum.1.refs_0_), channel_id=1, source_target_pairs={{0,24},{8,16},{16,8},{24,0},{1,25},{9,17},{17,9},{25,1},{2,26},{10... | collective-permute-start | bytes 221192 | tf_op jit(solution)/shard_map/ppermute | solution.py:34
  60.1 4.9 %collective-permute-start.24 = (bf16[144,256]{1,0:T(8,128)(2,1)S(1)}, bf16[144,256]{1,0:T(8,128)(2,1)S(1)}, u32[]{:S(2)}, u32[]{:S(2)}) collective-permute-start(bf16[144,256]{1,0:T(8,128)(2,1)S(1)} %z_sum.1.refs_0_), channel_id=1, source_target_pairs={{0,16},{8,24},{16,0},{24,8},{1,17},{9,25},{17,1},{25,9},{2,18},{10... | collective-permute-start | bytes 221192 | tf_op jit(solution)/shard_map/ppermute | solution.py:34
  61.7 4.4 %collective-permute-start.23 = (bf16[144,256]{1,0:T(8,128)(2,1)S(1)}, bf16[144,256]{1,0:T(8,128)(2,1)S(1)}, u32[]{:S(2)}, u32[]{:S(2)}) collective-permute-start(bf16[144,256]{1,0:T(8,128)(2,1)S(1)} %z_sum.1.refs_0_), channel_id=1, source_target_pairs={{0,8},{8,0},{16,24},{24,16},{1,9},{9,1},{17,25},{25,17},{2,10},{10... | collective-permute-start | bytes 221192 | tf_op jit(solution)/shard_map/ppermute | solution.py:34
